TPU v7x, 512 devices: a whole 4x8x8 slice. The times are simulated.
512 devices in a mesh: dp: 32 (over x, y), expert: 16 (over z, core).
Axes of the slice: x: 4, y: 8, z: 8, core: 2. Of those that a mesh axis runs over, the one named last changes fastest.
Arguments:
- tokens: bfloat16 [65536, 1792], P(('dp', 'expert')), may hold values from -6 to 6
- routes: int32 [65536, 2], P(('dp', 'expert')), may hold values from 0 to 15, all different within a row; in each aligned block of 128 rows (0 to 127, 128 to 255, ...) at most 32 rows name the same one
- gates: float32 [65536, 2], P(('dp', 'expert')), may hold values from 0.25 to 1
- grad_hidden: bfloat16 [65536, 2, 512], P(('dp', 'expert')), may hold values from -4 to 4
- w_in: bfloat16 [16, 1792, 512], P('expert', 'dp'), may hold values from -0.25 to 0.25
- error: bfloat16 [32, 16, 1792, 512], P('dp', 'expert'), may hold values from -6 to 6
- q_seed: float32 [16, 512, 32], P('expert'), may hold values from -6 to 6
Outputs:
- grad_tokens: bfloat16 [65536, 1792], P(('dp', 'expert'))
- error_next: bfloat16 [32, 16, 1792, 512], P('dp', 'expert')
- weight_grad: float32 [16, 1792, 512], P('expert', 'dp')
Inputs may be any that keep to these rules, and one draw needn't show every extreme that they name: `routes`: in the rows of one device no expert is named by more than 32 rows, a bound that some block reaches; the two experts of a row differ.
All inputs are finite; a program needn't handle non-finite values.
Results may differ from a plain program's by a relative error of at most 0.014.
Values may be sent and summed in bfloat16 or wider, within the bound.
No kernel may reach another device: no remote copies, remote signals or barrier semaphores. Data moves between devices by JAX's collectives and lax.ppermute only.
A program may use at most 64 MiB of HBM per device.

v0:
```python
import jax
import jax.numpy as jnp
from jax import lax
from jax.sharding import Mesh
from jax.sharding import PartitionSpec as P

DP = ("dp_0", "dp_1")
DP_EXPERT = ("dp_0", "dp_1", "expert")


highest = lax.Precision.HIGHEST


def sent_together(arrays, axis, split_dim, concat_dim, along):
    ends, at = ([], 0)
    for a in arrays[:-1]:
        at += a.shape[along]
        ends.append(at)
    both = jnp.concatenate(arrays, axis=along)
    return tuple(
        jnp.split(
            lax.all_to_all(both, axis, split_axis=split_dim, concat_axis=concat_dim, tiled=True),
            ends,
            axis=along,
        )
    )


def in_order(blocks, dim):
    dims = list(blocks.shape[1:])
    dims[dim] *= blocks.shape[0]
    return jnp.moveaxis(blocks, 0, dim).reshape(dims)


def all_blocks(x, axes, order):
    blocks = x
    for k in order:
        blocks = lax.all_gather(blocks, axes[k])
    done = order[::-1]
    back = [done.index(k) for k in range(len(axes))]
    blocks = blocks.transpose(*back, *range(len(axes), blocks.ndim))
    return blocks.reshape(-1, *x.shape)


def gather_axes(x, axes, order, dim):
    return in_order(all_blocks(x, axes, order), dim)


def split_up(x, dim, length):
    before, after = (x.shape[:dim], x.shape[dim + 1 :])
    return jnp.moveaxis(x.reshape(*before, length, -1, *after), dim, 0)


def sent_and_summed(x, axis, dim):
    length = lax.axis_size(axis)
    blocks = lax.all_to_all(split_up(x, dim, length), axis, 0, 0, tiled=True)
    return jnp.sum(blocks, axis=0)


def copy_for_each(x, axis):
    length = lax.axis_size(axis)
    return lax.all_to_all(jnp.broadcast_to(x[None], (length, *x.shape)), axis, 0, 0, tiled=True)


def over_copies(x, axis):
    everything = copy_for_each(x, axis)
    return jnp.sum(everything, axis=0)


def gather_directly(x, axis, dim):
    return in_order(copy_for_each(x, axis), dim)


def of_everyone(x, axis):
    return copy_for_each(x, axis).astype(jnp.float32).sum(axis=0)


def slopes(pre_act):
    squashed = jax.nn.sigmoid(pre_act)
    return squashed * (1.0 + pre_act * (1.0 - squashed))


def body(tokens, routes, gates, grad_hidden, w_in, error, q_seed):
    experts = lax.axis_size("expert")
    replicas = lax.axis_size(DP)
    row_count = tokens.shape[0]
    width = tokens.shape[1]
    hidden = grad_hidden.shape[2]
    capacity = 4 * row_count // experts
    chosen = routes.reshape(-1)
    matches = (chosen[:, None] == jnp.arange(experts, dtype=jnp.int32)[None, :]).astype(jnp.int32)
    earlier = jnp.cumsum(matches, axis=0) - matches
    position = chosen * capacity + jnp.sum(earlier * matches, axis=1)
    placer = (jnp.arange(experts * capacity, dtype=jnp.int32)[:, None] == position[None, :]).astype(
        jnp.bfloat16
    )
    gate_flat = gates.reshape(-1)
    scaled = (jnp.repeat(tokens, 2, axis=0).astype(jnp.float32) * gate_flat[:, None]).astype(
        jnp.bfloat16
    )
    sent_rows = jnp.dot(placer, scaled, preferred_element_type=jnp.float32).astype(jnp.bfloat16)
    sent_grad = jnp.dot(
        placer, grad_hidden.reshape(2 * row_count, hidden), preferred_element_type=jnp.float32
    ).astype(jnp.bfloat16)
    sent_rows = sent_rows.reshape(experts, capacity, width)
    sent_grad = sent_grad.reshape(experts, capacity, hidden)
    weight_part = w_in[0]
    arrived, arrived_grad = sent_together((sent_rows, sent_grad), "expert", 0, 0, 2)
    arrived = arrived.reshape(experts * capacity, width)
    arrived_grad = arrived_grad.reshape(experts * capacity, hidden)
    weight_full = gather_axes(weight_part, DP, (0, 1), 0)
    pre_act = jnp.dot(arrived, weight_full, preferred_element_type=jnp.float32)
    grad_pre = (arrived_grad.astype(jnp.float32) * slopes(pre_act)).astype(jnp.bfloat16)
    weight_term = lax.dot_general(
        arrived, grad_pre, (((0,), (0,)), ((), ())), preferred_element_type=jnp.float32
    )
    grad_rows = lax.dot_general(
        grad_pre, weight_full, (((1,), (1,)), ((), ())), preferred_element_type=jnp.float32
    )
    sending = grad_rows.astype(jnp.bfloat16).reshape(experts, capacity, width)
    returned = lax.all_to_all(sending, "expert", split_axis=0, concat_axis=0, tiled=True).reshape(
        experts * capacity, width
    )
    picked = jnp.take(returned, position, axis=0).astype(jnp.float32) * gate_flat[:, None]
    grad_tokens = jnp.sum(picked.reshape(row_count, 2, width), axis=1).astype(jnp.bfloat16)
    merged = weight_term + error[0, 0].astype(jnp.float32)
    q_start = q_seed[0]
    local_factor = lax.dot_general(q_start, merged, (((0,), (1,)), ((), ())), precision=highest)
    part_rows = sent_and_summed(local_factor, DP, 1) / replicas
    gram_matrix = over_copies(jnp.dot(part_rows, part_rows.T, precision=highest), DP)
    lower_factor = jnp.linalg.cholesky(gram_matrix)
    part_basis = jax.scipy.linalg.solve_triangular(lower_factor, part_rows, lower=True)
    basis = gather_directly(part_basis, DP, 1)
    q_factor = (
        of_everyone(jnp.dot(basis, merged, precision=highest).astype(jnp.bfloat16), DP).astype(
            jnp.float32
        )
        / replicas
    )
    low_rank = lax.dot_general(basis, q_factor, (((0,), (0,)), ((), ())), precision=highest)
    error_next = (merged - low_rank).astype(jnp.bfloat16)[None, None]
    shard_rows = width // replicas
    weight_grad = lax.dynamic_slice_in_dim(
        low_rank, lax.axis_index(DP) * shard_rows, shard_rows, 0
    )[None]
    return (grad_tokens, error_next, weight_grad)


def solution(mesh):
    torus = Mesh(mesh.devices.reshape(4, 8, mesh.shape["expert"]), ("dp_0", "dp_1", "expert"))
    in_specs = (
        P(DP_EXPERT, None),
        P(DP_EXPERT, None),
        P(DP_EXPERT, None),
        P(DP_EXPERT, None, None),
        P("expert", DP, None),
        P(DP, "expert", None, None),
        P("expert", None, None),
    )
    out_specs = (P(DP_EXPERT, None), P(DP, "expert", None, None), P("expert", DP, None))
    return jax.shard_map(body, mesh=torus, in_specs=in_specs, out_specs=out_specs, check_vma=False)
```

profile of v0, /device:TPU:1, one launch (start us, length us, event | category | flops | bytes accessed | tf_op | source)
XLA Modules:
  0.0 256.2 jit_solution(12965477628430742853)
XLA Ops:
  8.3 1.1 reshape.129
  10.3 2.7 %broadcast_in_dim.25 = f32[128,2,1792]{2,1,0:T(2,128)} broadcast(bf16[128,1792]{1,0:T(8,128)(2,1)} %param.7), dimensions={0,2} | broadcast | bytes 2293760 | tf_op jit(solution)/shard_map/broadcast_in_dim | solution.py:98
  13.0 2.6 convert_element_type.61
  16.9 1.6 pad_maximum_fusion
  18.5 12.0 %all-to-all-start = ((bf16[16,32,2304]{2,1,0:T(8,128)(2,1)}), bf16[16,32,2304]{2,1,0:T(8,128)(2,1)S(1)}, u32[]{:S(2)}, u32[]{:S(2)}) async-start(bf16[16,32,2304]{2,1,0:T(8,128)(2,1)} %pad_maximum_fusion), calls=%async_computation | async-start | bytes 4718592 | tf_op jit(solution)/shard_map/all_to_all | solution.py:22
  30.5 10.8 %all_gather.9 = bf16[4,56,512]{2,1,0:T(8,128)(2,1)} all-gather(bf16[1,56,512]{2,1,0:T(8,128)(2,1)S(1)} %copy-done.6), channel_id=1, replica_groups=mesh['dp_0'=4,'dp_1'=8,'expert'=16] {'dp_0'}, dimensions={0}, use_global_device_ids=true | all-gather | bytes 286720 | tf_op jit(solution)/shard_map/all_gather | solution.py:38
  41.3 41.8 %all-gather.3.cloned.1.call-done = bf16[32,56,512]{2,1,0:T(8,128)(2,1)} async-done(((bf16[4,56,512]{2,1,0:T(8,128)(2,1)}), bf16[32,56,512]{2,1,0:T(8,128)(2,1)}) %all-gather.3.cloned.1.call-update) | async-done | bytes 1835024 | tf_op jit(solution)/shard_map/all_gather | solution.py:38
  83.1 2.9 %copy.54 = bf16[4,8,56,512]{3,2,1,0:T(8,128)(2,1)} copy(bf16[4,8,56,512]{3,2,0,1:T(8,128)(2,1)} %bitcast.74) | data formatting | bytes 3670016 | tf_op jit(solution)/shard_map/transpose | solution.py:41
  86.2 1.4 copy-done.3
  87.5 1.1 fusion.31
  89.0 1.3 convert_add_fusion
  90.4 1.8 copy-done.1
  92.2 3.4 %convolution_bitcast_fusion = f32[32,1792]{1,0:T(8,128)S(1)} fusion(f32[1792,512]{1,0:T(8,128)S(1)} %convert_add_fusion, f32[1,512,32]{1,2,0:T(8,128)S(1)} %copy-done), kind=kOutput, calls=%fused_computation.6 | convolution fusion | flops 352321536 | bytes 3964928 | tf_op jit(solution)/shard_map/dot_general | solution.py:128
  96.9 17.8 %all_to_all.30 = f32[32,1,1792]{2,1,0:T(1,128)S(1)} all-to-all(f32[32,1,1792]{2,1,0:T(1,128)S(1)} %reshape.148), channel_id=1, replica_groups=mesh['dp_0'=4,'dp_1'=8,'expert'=16] {'dp_0','dp_1'}, dimensions={0} | all-to-all | bytes 458752 | tf_op jit(solution)/shard_map/all_to_all | solution.py:56
  115.2 1.2 reduce.8
  117.4 13.3 %all_to_all.31 = f32[32,1,1024]{2,1,0:T(1,128)S(1)} all-to-all(f32[32,1,1024]{2,1,0:T(1,128)S(1)} %reshape.150), channel_id=1, replica_groups=mesh['dp_0'=4,'dp_1'=8,'expert'=16] {'dp_0','dp_1'}, dimensions={0} | all-to-all | bytes 262144 | tf_op jit(solution)/shard_map/all_to_all | solution.py:62
  130.7 1.0 reduce.9
  132.0 2.9 %cholesky.16 = f32[32,32]{1,0:T(8,128)S(1)} custom-call(f32[32,32]{1,0:T(8,128)S(1)} %fusion.19), custom_call_target="Cholesky" | custom-call | tf_op jit(solution)/shard_map/jit(cholesky)/cholesky | solution.py:131
  136.2 2.4 custom-call.7
  139.5 13.0 %all_to_all.32 = f32[32,1,1792]{2,1,0:T(1,128)S(1)} all-to-all(f32[32,1,1792]{2,1,0:T(1,128)S(1)} %reshape.152), channel_id=1, replica_groups=mesh['dp_0'=4,'dp_1'=8,'expert'=16] {'dp_0','dp_1'}, dimensions={0} | all-to-all | bytes 458752 | tf_op jit(solution)/shard_map/all_to_all | solution.py:62
  152.5 1.2 reduce.10
  154.7 4.2 %convolution_convert_fusion.3 = bf16[32,512]{1,0:T(8,128)(2,1)S(1)} fusion(f32[32,1792]{1,0:T(8,128)S(1)} %reshape.135, f32[1792,512]{1,0:T(8,128)} %copy-done.1), kind=kOutput, calls=%fused_computation.13 | convolution fusion | flops 352337920 | bytes 3932160 | tf_op jit(solution)/shard_map/dot_general | solution.py:135
  159.0 1.1 broadcast_in_dim.47
  160.1 4.2 %all-to-all-start.5 = ((bf16[32,32,512]{2,1,0:T(8,128)(2,1)}), bf16[32,32,512]{2,1,0:T(8,128)(2,1)S(1)}, u32[]{:S(2)}, u32[]{:S(2)}) async-start(bf16[32,32,512]{2,1,0:T(8,128)(2,1)} %broadcast_in_dim.47), calls=%async_computation.5 | async-start | bytes 2097152 | tf_op jit(solution)/shard_map/all_to_all | solution.py:62
  164.3 4.0 %convolution_convert_fusion.1 = bf16[512,1792]{1,0:T(8,128)(2,1)} fusion(bf16[1792,512]{1,0:T(8,128)(2,1)S(1)} %bitcast.72, bf16[512,512]{1,0:T(8,128)(2,1)} %bitcast.78, f32[512,512]{1,0:T(8,128)} %copy-done.10), kind=kOutput, calls=%fused_computation.4 | convolution fusion | flops 943063040 | bytes 5242880 | tf_op jit(solution)/shard_map/dot_general | solution.py:117
  168.3 14.9 %all-to-all-done.5 = bf16[32,32,512]{2,1,0:T(8,128)(2,1)S(1)} async-done(((bf16[32,32,512]{2,1,0:T(8,128)(2,1)}), bf16[32,32,512]{2,1,0:T(8,128)(2,1)S(1)}, u32[]{:S(2)}, u32[]{:S(2)}) %all-to-all-start.5) | async-done | bytes 1048608 | tf_op jit(solution)/shard_map/all_to_all | solution.py:62
  183.2 16.3 %all-to-all-start.1 = ((bf16[16,32,1792]{2,1,0:T(8,128)(2,1)}), bf16[16,32,1792]{2,1,0:T(8,128)(2,1)S(1)}, u32[]{:S(2)}, u32[]{:S(2)}) async-start(bf16[16,32,1792]{2,1,0:T(8,128)(2,1)} %bitcast.73), calls=%async_computation.1 | async-start | bytes 3670016 | tf_op jit(solution)/shard_map/all_to_all | solution.py:121
  200.4 3.1 %fusion.10 = f32[1792,512]{1,0:T(8,128)S(1)} fusion(f32[32,1792]{1,0:T(8,128)S(1)} %reshape.135, f32[32,512]{1,0:T(8,128)S(1)} %convert_reduce_fusion), kind=kOutput, calls=%fused_computation.25 | convolution fusion | flops 352337920 | bytes 3964928 | tf_op jit(solution)/shard_map/dot_general | solution.py:140
  204.1 2.0 fusion
  206.1 37.1 %all-to-all-done.1 = bf16[16,32,1792]{2,1,0:T(8,128)(2,1)S(1)} async-done(((bf16[16,32,1792]{2,1,0:T(8,128)(2,1)}), bf16[16,32,1792]{2,1,0:T(8,128)(2,1)S(1)}, u32[]{:S(2)}, u32[]{:S(2)}) %all-to-all-start.1) | async-done | bytes 1835040 | tf_op jit(solution)/shard_map/all_to_all | solution.py:121
  243.2 1.3 gather_fusion
  244.9 4.5 %multiply_reduce_fusion = bf16[128,1792]{1,0:T(8,128)(2,1)} fusion(bf16[128,2,1792]{2,1,0:T(2,128)(2,1)S(1)} %gather.7, pred[128,2]{1,0:T(8,128)(4,1)S(1)} %copy.52, f32[128,2]{1,0:T(8,128)S(1)} %copy.53), kind=kLoop, calls=%fused_computation.9 | loop fusion | flops 1605632 | bytes 1377536 | tf_op jit(solution)/shard_map/reduce_sum | solution.py:125
  (73 shorter events, 11.9 us)
Async XLA Ops:
  7.2 85.0 %copy-start = (f32[1,512,32]{1,2,0:T(8,128)S(1)}, f32[1,512,32]{1,2,0:T(8,128)}, u32[]{:S(2)}) copy-start(f32[1,512,32]{1,2,0:T(8,128)} %param.13) | copy-start | bytes 196612
  13.0 2.6 %copy-start.8 = (f32[128,2]{0,1:T(2,128)S(1)}, f32[128,2]{0,1:T(2,128)}, u32[]{:S(2)}) copy-start(f32[128,2]{0,1:T(2,128)} %param.9) | copy-start | bytes 3076
  18.5 12.0 %copy-start.6 = (bf16[1,56,512]{2,1,0:T(8,128)(2,1)S(1)}, bf16[1,56,512]{2,1,0:T(8,128)(2,1)}, u32[]{:S(2)}) copy-start(bf16[1,56,512]{2,1,0:T(8,128)(2,1)} %param.11) | copy-start | bytes 172036
  18.5 67.6 %all-to-all-start = ((bf16[16,32,2304]{2,1,0:T(8,128)(2,1)}), bf16[16,32,2304]{2,1,0:T(8,128)(2,1)S(1)}, u32[]{:S(2)}, u32[]{:S(2)}) async-start(bf16[16,32,2304]{2,1,0:T(8,128)(2,1)} %pad_maximum_fusion), calls=%async_computation | async-start | bytes 4718592 | tf_op jit(solution)/shard_map/all_to_all | solution.py:22
  30.4 52.7 %all-gather.3.cloned.1.call-start = ((), (), s32[]{:S(2)}) async-start(), calls=%async_computation.6 | async-start | bytes 2064384 | tf_op jit(solution)/shard_map/all_gather | solution.py:38
  86.0 1.5 copy-start.3
  87.5 1.5 copy-start.9
  88.6 1.7 copy-start.10
  88.7 1.7 copy-start.5
  90.4 1.8 copy-start.1
  159.0 5.3 %copy-start.4 = (bf16[4,8,56,512]{3,2,1,0:T(8,128)(2,1)S(1)}, bf16[4,8,56,512]{3,2,1,0:T(8,128)(2,1)}, u32[]{:S(2)}) copy-start(bf16[4,8,56,512]{3,2,1,0:T(8,128)(2,1)} %copy.54) | copy-start | bytes 5505028
  160.1 23.1 %all-to-all-start.5 = ((bf16[32,32,512]{2,1,0:T(8,128)(2,1)}), bf16[32,32,512]{2,1,0:T(8,128)(2,1)S(1)}, u32[]{:S(2)}, u32[]{:S(2)}) async-start(bf16[32,32,512]{2,1,0:T(8,128)(2,1)} %broadcast_in_dim.47), calls=%async_computation.5 | async-start | bytes 2097152 | tf_op jit(solution)/shard_map/all_to_all | solution.py:62
  183.2 16.5 %copy-start.7 = (s32[128,2]{0,1:T(2,128)S(1)}, s32[128,2]{0,1:T(2,128)}, u32[]{:S(2)}) copy-start(s32[128,2]{0,1:T(2,128)} %param.8) | copy-start | bytes 3076
  183.2 60.0 %all-to-all-start.1 = ((bf16[16,32,1792]{2,1,0:T(8,128)(2,1)}), bf16[16,32,1792]{2,1,0:T(8,128)(2,1)S(1)}, u32[]{:S(2)}, u32[]{:S(2)}) async-start(bf16[16,32,1792]{2,1,0:T(8,128)(2,1)} %bitcast.73), calls=%async_computation.1 | async-start | bytes 3670016 | tf_op jit(solution)/shard_map/all_to_all | solution.py:121
  200.3 3.8 %copy-start.2 = (f32[1792,512]{1,0:T(8,128)S(1)}, f32[1792,512]{1,0:T(8,128)}, u32[]{:S(2)}) copy-start(f32[1792,512]{1,0:T(8,128)} %copy-done.1) | copy-start | bytes 11010052
Sparse Core Ops, SparseCore 0:
  41.4 41.6 all-gather.2
where the time goes:
time: 257 us; the launch traced here: 256 us
  waiting for transfers between devices  93.8 us (36%)
  blocking collectives  54.9 us (21%)
  starting transfers between devices  32.5 us (13%)
  local copies, waits for them, and re-layouts  22.9 us (9%)
  other arithmetic  19.1 us (7%)
  matrix products  18.6 us (7%)
  between operations  14.4 us (6%)
    all_gather x1, waiting for transfers between devices, all_blocks(): blocks = lax.all_gather(blocks, axes[k])  41.8 us
    all_to_all x1, waiting for transfers between devices, body(): lax.all_to_all(sending, 'expert', split_axis=0, concat_axis=0, tiled=True)  37.1 us
    all_to_all x2, blocking collectives, copy_for_each(): lax.all_to_all(jnp.broadcast_to(x[None], (length, *x.shape)), axis, 0, 0,...  26.3 us
    all_to_all x1, blocking collectives, sent_and_summed(): blocks = lax.all_to_all(split_up(x, dim, length), axis, 0, 0, tiled=True)  17.8 us
    all_to_all x1, starting transfers between devices, body(): lax.all_to_all(sending, 'expert', split_axis=0, concat_axis=0, tiled=True)  16.3 us
    all_to_all x1, waiting for transfers between devices, copy_for_each(): lax.all_to_all(jnp.broadcast_to(x[None], (length, *x.shape)), axis, 0, 0,...  14.9 us
    all_to_all x1, starting transfers between devices, sent_together(): lax.all_to_all(both, axis, split_axis=split_dim, concat_axis=concat_dim,...  12 us
    all_gather x1, blocking collectives, all_blocks(): blocks = lax.all_gather(blocks, axes[k])  10.8 us
  transfers between devices with their start and end apart: 4, of which 3 were waited for; matrix products, arithmetic and copies ran while one was open for 5% of the time, Pallas kernels for 0%

commit v1 on v0

v1 whole, which is shorter than its diff:
```python
import jax
import jax.numpy as jnp
from jax import lax
from jax.experimental import pallas as pl
from jax.experimental.pallas import tpu as pltpu
from jax.sharding import Mesh
from jax.sharding import PartitionSpec as P

DP = ("dp_0", "dp_1")
DP_EXPERT = ("dp_0", "dp_1", "expert")

f32, bf16 = jnp.float32, jnp.bfloat16
VMEM = pl.BlockSpec(memory_space=pltpu.VMEM)
LANES = 128


def nn(a, b):
    return lax.dot_general(a, b, (((1,), (0,)), ((), ())), preferred_element_type=f32)


def nt(a, b):
    return lax.dot_general(a, b, (((1,), (1,)), ((), ())), preferred_element_type=f32)


def tn(a, b):
    return lax.dot_general(a, b, (((0,), (0,)), ((), ())), preferred_element_type=f32)


def halves(x):
    high = x.astype(bf16)
    return high, (x - high.astype(f32)).astype(bf16)


def call(kernel, outs, args, flops=0, moved=0, megabytes=28, **more):
    return pl.pallas_call(
        kernel,
        out_shape=outs,
        compiler_params=pltpu.CompilerParams(vmem_limit_bytes=megabytes << 20),
        cost_estimate=pl.CostEstimate(flops=flops, bytes_accessed=moved, transcendentals=0),
        **more,
    )(*args)


def one_hots(routes, experts, capacity):
    rows = routes.shape[1]
    slots = experts * capacity
    before = (
        lax.broadcasted_iota(jnp.int32, (rows, rows), 0) < lax.broadcasted_iota(jnp.int32, (rows, rows), 1)
    ).astype(bf16)
    expert = lax.broadcasted_iota(jnp.int32, (experts, rows), 0)
    slot = lax.broadcasted_iota(jnp.int32, (slots, rows), 0)
    started = jnp.zeros((experts, 1), f32)
    out = []
    for k in range(2):
        chosen = routes[k : k + 1, :]
        match = (expert == chosen).astype(f32)
        earlier = nn(match.astype(bf16), before) + started
        place = jnp.sum(match * earlier, axis=0, keepdims=True).astype(jnp.int32) + chosen * capacity
        out.append((slot == place).astype(f32))
        started = started + jnp.sum(match, axis=1, keepdims=True)
    return out


def prepare_kernel(experts, capacity, routes_ref, gates_ref, tokens_ref, grad_ref, sent_ref):
    width = tokens_ref.shape[1]
    hidden = grad_ref.shape[1] // 2
    first, second = one_hots(routes_ref[...], experts, capacity)
    gates = gates_ref[...]
    gate = jnp.sum(first * gates[0:1, :] + second * gates[1:2, :], axis=1, keepdims=True)
    either = (first + second).astype(bf16)
    sent_ref[:, :width] = (nn(either, tokens_ref[...]) * gate).astype(bf16)
    grads = nn(first.astype(bf16), grad_ref[:, :hidden]) + nn(second.astype(bf16), grad_ref[:, hidden:])
    sent_ref[:, width:] = grads.astype(bf16)


def select_kernel(experts, capacity, routes_ref, select_ref):
    rows = routes_ref.shape[1]
    for k, places in enumerate(one_hots(routes_ref[...], experts, capacity)):
        select_ref[k * rows : (k + 1) * rows, :] = places.T.astype(bf16)


def merge_kernel(
    width, arrived_ref, weight_ref, error_ref, seed_ref, grad_pre_ref, merged_ref, factor_ref
):
    rank = seed_ref.shape[1]
    pre = nn(arrived_ref[:, :width], weight_ref[...])
    s = 1.0 / (1.0 + jnp.exp(-pre))
    grad_pre = (arrived_ref[:, width:].astype(f32) * (s * (1.0 + pre * (1.0 - s)))).astype(bf16)
    grad_pre_ref[...] = grad_pre
    high, low = halves(seed_ref[...])
    both = jnp.concatenate([high, low], axis=1)
    step = width // 7
    for i in range(7):
        rows = slice(i * step, (i + 1) * step)
        merged = tn(arrived_ref[:, rows], grad_pre) + error_ref[rows, :].astype(f32)
        merged_ref[rows, :] = merged
        upper, lower = halves(merged)
        part = nn(upper, both)
        part = part[:, :rank] + part[:, rank:] + nn(lower, high)
        part = part.T
        for j in range(step // LANES):
            factor_ref[:, i * (step // LANES) + j, :] = part[:, j * LANES : (j + 1) * LANES]


def rows_kernel(grad_pre_ref, weight_ref, grad_rows_ref):
    grad_rows_ref[...] = nt(grad_pre_ref[...], weight_ref[...]).astype(bf16)


def sum_and_copy_kernel(parts_ref, copies_ref):
    total = jnp.sum(parts_ref[...], axis=0)
    copies_ref[...] = jnp.broadcast_to(total[None], copies_ref.shape)


def right_kernel(factor_ref, merged_ref, right_ref):
    rank, blocks, _ = factor_ref.shape
    total = jnp.zeros(right_ref.shape, f32)
    for j in range(0, blocks, 2):
        pair = jnp.concatenate([factor_ref[:, j, :], factor_ref[:, j + 1, :]], axis=1)
        both = jnp.concatenate(halves(pair), axis=0)
        part = nn(both, merged_ref[j * LANES : (j + 2) * LANES, :].astype(bf16))
        total = total + part[:rank] + part[rank:]
    right_ref[...] = total


def left_kernel(factor_ref, left_ref, gathered_ref):
    rank, blocks, _ = factor_ref.shape
    for j in range(blocks):
        gathered_ref[:, j * LANES : (j + 1) * LANES] = factor_ref[:, j, :]
    factor = gathered_ref[...]
    high, low = halves(factor)
    gram = nt(high, high) + nt(high, low) + nt(low, high)
    line = lax.broadcasted_iota(jnp.int32, (rank, rank), 0)
    column = lax.broadcasted_iota(jnp.int32, (rank, rank), 1)
    eye = (line == column).astype(f32)

    def eliminate(i, both):
        gram, inverse = both
        own = line == i
        at_column = jnp.where(column == i, gram, 0.0)
        entries = jnp.sum(at_column, axis=1, keepdims=True)
        pivot = jnp.sum(jnp.where(own, at_column, 0.0), axis=(0, 1), keepdims=True)
        row = jnp.sum(jnp.where(own, gram, 0.0), axis=0, keepdims=True) / pivot
        inverse_row = jnp.sum(jnp.where(own, inverse, 0.0), axis=0, keepdims=True) / pivot
        return (
            jnp.where(own, row, gram - entries * row),
            jnp.where(own, inverse_row, inverse - entries * inverse_row),
        )

    _, inverse = lax.fori_loop(0, rank, eliminate, (gram, eye))
    upper, lower = halves(inverse)
    left_ref[...] = nn(upper, high) + nn(upper, low) + nn(lower, high)


def finish_kernel(count, total_ref, left_ref, mine_ref, merged_ref, error_ref, weight_ref, right_ref):
    @pl.when(pl.program_id(0) == 0)
    def _():
        total = total_ref[...] / count
        high, low = halves(total)
        right_ref[...] = jnp.concatenate([high, low, high], axis=0)
        upper, lower = halves(mine_ref[...])
        weight_ref[...] = tn(jnp.concatenate([upper, upper, lower], axis=0), right_ref[...])

    upper, lower = halves(left_ref[...])
    low_rank = tn(jnp.concatenate([upper, upper, lower], axis=0), right_ref[...])
    error_ref[...] = (merged_ref[...] - low_rank).astype(bf16)


def combine_kernel(select_ref, gates_ref, returned_ref, out_ref):
    rows = out_ref.shape[0]
    returned = returned_ref[...]
    picked = nn(select_ref[...], returned)
    gates = gates_ref[...]
    out_ref[...] = (picked[:rows] * gates[:, 0:1] + picked[rows:] * gates[:, 1:2]).astype(bf16)


def shape(dims, dtype):
    return jax.ShapeDtypeStruct(dims, dtype)


def summed(x, axis):
    size, step = lax.axis_size(axis), 1
    while step < size:
        x = x + lax.ppermute(x, axis, [(i, i ^ step) for i in range(size)])
        step *= 2
    return x


def body(tokens, routes, gates, grad_hidden, w_in, error, q_seed):
    experts = lax.axis_size("expert")
    replicas = lax.axis_size(DP)
    row_count, width = tokens.shape
    hidden = grad_hidden.shape[2]
    rank = q_seed.shape[2]
    capacity = 4 * row_count // experts
    slots = experts * capacity
    routes_t = routes.T

    sent = call(
        lambda *refs: prepare_kernel(experts, capacity, *refs),
        shape((slots, width + hidden), bf16),
        (routes_t, gates.T, tokens, grad_hidden.reshape(row_count, 2 * hidden)),
    )
    w_mine, sent = lax.optimization_barrier((w_in[0], sent))
    arrived = lax.all_to_all(
        sent.reshape(experts, capacity, width + hidden), "expert", 0, 0, tiled=True
    ).reshape(slots, width + hidden)
    weight = lax.all_gather(lax.all_gather(w_mine, DP[1], tiled=True), DP[0], tiled=True)
    select = call(
        lambda *refs: select_kernel(experts, capacity, *refs),
        shape((2 * row_count, slots), bf16),
        (routes_t,),
    )

    blocks = width // LANES
    grad_pre, merged, factor = call(
        lambda *refs: merge_kernel(width, *refs),
        (shape((slots, hidden), bf16), shape((width, hidden), f32), shape((rank, blocks, LANES), f32)),
        (arrived, weight, error[0, 0], q_seed[0]),
    )
    each = rank // replicas
    parts = lax.all_to_all(factor, DP, 0, 0, tiled=True)
    grad_rows = call(rows_kernel, shape((slots, width), bf16), (grad_pre, weight))
    copies = call(
        sum_and_copy_kernel,
        shape((replicas, each * blocks, LANES), f32),
        (parts.reshape(replicas, each * blocks, LANES),),
    )
    factor = lax.all_to_all(copies, DP, 0, 0, tiled=True).reshape(rank, blocks, LANES)
    factor, grad_rows = lax.optimization_barrier((factor, grad_rows))
    returned = lax.all_to_all(
        grad_rows.reshape(experts, capacity, width), "expert", 0, 0, tiled=True
    ).reshape(slots, width)

    right = call(right_kernel, shape((rank, hidden), f32), (factor, merged))
    right = summed(summed(right, DP[1]), DP[0])
    left = call(
        left_kernel,
        shape((rank, width), f32),
        (factor,),
        scratch_shapes=[pltpu.VMEM((rank, width), f32)],
    )
    shard = width // replicas
    mine = lax.dynamic_slice_in_dim(left, lax.axis_index(DP) * shard, shard, 1)

    step = width // 7
    error_next, weight_grad = call(
        lambda *refs: finish_kernel(replicas, *refs),
        (shape((width, hidden), bf16), shape((shard, hidden), f32)),
        (right, left, mine, merged),
        grid=(7,),
        in_specs=[
            pl.BlockSpec((rank, hidden), lambda i: (0, 0)),
            pl.BlockSpec((rank, step), lambda i: (0, i)),
            pl.BlockSpec((rank, shard), lambda i: (0, 0)),
            pl.BlockSpec((step, hidden), lambda i: (i, 0)),
        ],
        out_specs=[
            pl.BlockSpec((step, hidden), lambda i: (i, 0)),
            pl.BlockSpec((shard, hidden), lambda i: (0, 0)),
        ],
        scratch_shapes=[pltpu.VMEM((3 * rank, hidden), bf16)],
    )
    grad_tokens = call(combine_kernel, shape((row_count, width), bf16), (select, gates, returned))
    return grad_tokens, error_next[None, None], weight_grad[None]


def solution(mesh):
    torus = Mesh(mesh.devices.reshape(4, 8, mesh.shape["expert"]), DP_EXPERT)
    in_specs = (
        P(DP_EXPERT, None),
        P(DP_EXPERT, None),
        P(DP_EXPERT, None),
        P(DP_EXPERT, None, None),
        P("expert", DP, None),
        P(DP, "expert", None, None),
        P("expert", None, None),
    )
    out_specs = (P(DP_EXPERT, None), P(DP, "expert", None, None), P("expert", DP, None))
    return jax.shard_map(body, mesh=torus, in_specs=in_specs, out_specs=out_specs, check_vma=False)
```

time: 257 us -> 197 us (0.77)
  waiting for transfers between devices: 93.8 us -> 56.3 us
  other arithmetic: 19.1 us -> 0.05 us
  matrix products: 18.6 us -> 0 us
  Pallas kernels: 0 us -> 18.2 us
  starting transfers between devices: 32.5 us -> 46.7 us
  blocking collectives: 54.9 us -> 41.5 us
  local copies, waits for them, and re-layouts: 22.9 us -> 16.7 us
    all_to_all x3, waiting for transfers between devices: 51.9 us -> 5.74 us  [the longest x1 5.73 us: body(): lax.all_to_all(copies, DP, 0, 0, tiled=True).reshape(rank, blocks, LANES)]
    all_to_all x3 -> x1, blocking collectives: 44.1 us -> 17.4 us  [body(): parts = lax.all_to_all(factor, DP, 0, 0, tiled=True)]
    dot_general x9 -> x0, matrix products: 18.4 us -> none  [the longest x1 4.22 us: body(): jnp.dot(basis, merged, precision=highest).astype(jnp.bfloat16)]
    pallas_call x0 -> x9, Pallas kernels: none -> 18.2 us  [call(): pl.pallas_call(kernel, out_shape=outs, compiler_params=pltpu.CompilerPara...]
    ppermute x0 -> x5, starting transfers between devices: none -> 17.5 us  [summed(): x = x + lax.ppermute(x, axis, [(i, i ^ step) for i in range(size)])]
    all_gather x1, blocking collectives: 10.8 us -> 24.1 us  [body(): lax.all_gather(w_mine, DP[1], tiled=True)]
    ppermute x0 -> x5, waiting for transfers between devices: none -> 12.5 us  [summed(): x = x + lax.ppermute(x, axis, [(i, i ^ step) for i in range(size)])]
    unnamed x30 -> x33, local copies, waits for them, and re-layouts: 6.8 us -> 16.6 us
  transfers between devices with their start and end apart: 4 -> 9, of which waited for: 3 -> 6; matrix products, arithmetic and copies ran while one was open for 5% -> 0% of each run, Pallas kernels for 0% -> 6%
where the time goes in v1:
time: 197 us; the launch traced here: 194 us
  waiting for transfers between devices  56.3 us (29%)
  starting transfers between devices  46.7 us (24%)
  blocking collectives  41.5 us (21%)
  Pallas kernels  18.2 us (9%)
  local copies, waits for them, and re-layouts  16.7 us (8%)
  between operations  14.3 us (7%)
    all_gather x1, waiting for transfers between devices, body(): lax.all_gather(lax.all_gather(w_mine, DP[1], tiled=True), DP[0], tiled=True)  38 us
    all_gather x1, blocking collectives, body(): lax.all_gather(w_mine, DP[1], tiled=True)  24.1 us
    pallas_call x9, Pallas kernels, call(): pl.pallas_call(kernel, out_shape=outs, compiler_params=pltpu.CompilerPara...  18.2 us
    ppermute x5, starting transfers between devices, summed(): x = x + lax.ppermute(x, axis, [(i, i ^ step) for i in range(size)])  17.5 us
    all_to_all x1, blocking collectives, body(): parts = lax.all_to_all(factor, DP, 0, 0, tiled=True)  17.4 us
    unnamed x33, local copies, waits for them, and re-layouts  16.6 us
    ppermute x5, waiting for transfers between devices, summed(): x = x + lax.ppermute(x, axis, [(i, i ^ step) for i in range(size)])  12.5 us
    all_to_all x1, starting transfers between devices, body(): lax.all_to_all(sent.reshape(experts, capacity, width + hidden), 'expert',...  12 us
  transfers between devices with their start and end apart: 9, of which 6 were waited for; matrix products, arithmetic and copies ran while one was open for 0% of the time, Pallas kernels for 6%

profile of v1, /device:TPU:1, one launch (start us, length us, event | category | flops | bytes accessed | tf_op | source)
XLA Modules:
  0.0 193.7 jit_solution(11181729327100198419)
XLA Ops:
  7.2 1.0 copy.12
  8.2 1.0 copy-done.8
  10.5 1.1 shard_map.95
  11.6 1.4 copy-done.3
  13.0 12.0 %all-to-all-start = ((bf16[16,32,2304]{2,1,0:T(8,128)(2,1)}), bf16[16,32,2304]{2,1,0:T(8,128)(2,1)S(1)}, u32[]{:S(2)}, u32[]{:S(2)}) async-start(bf16[16,32,2304]{2,1,0:T(8,128)(2,1)} %bitcast.14), calls=%async_computation | async-start | bytes 4718592 | tf_op jit(solution)/shard_map/all_to_all | solution.py:204
  25.1 24.1 %all_gather.6 = bf16[448,512]{1,0:T(8,128)(2,1)} all-gather(bf16[56,512]{1,0:T(8,128)(2,1)S(1)} %bitcast.24), channel_id=1, replica_groups=mesh['dp_0'=4,'dp_1'=8,'expert'=16] {'dp_1'}, dimensions={0}, use_global_device_ids=true | all-gather | bytes 516096 | tf_op jit(solution)/shard_map/all_gather | solution.py:207
  49.3 38.0 %all-gather.2.cloned.1.call-done.refs_1_.weight_ref = bf16[1792,512]{1,0:T(8,128)(2,1)} async-done(((bf16[448,512]{1,0:T(8,128)(2,1)}), bf16[1792,512]{1,0:T(8,128)(2,1)}) %all-gather.2.cloned.1.call-update) | async-done | bytes 1835024 | tf_op jit(solution)/shard_map/all_gather | solution.py:207
  87.3 1.5 copy-done.5
  88.8 1.5 copy-done.7
  90.3 4.1 %shard_map.96 = (bf16[512,512]{1,0:T(8,128)(2,1)S(1)}, f32[1792,512]{1,0:T(8,128)S(1)}, f32[32,14,128]{2,1,0:T(8,128)S(1)}) custom-call(bf16[512,2304]{1,0:T(8,128)(2,1)S(1)} %bitcast.13, bf16[1792,512]{1,0:T(8,128)(2,1)S(1)} %copy-done.5, bf16[1792,512]{1,0:T(8,128)(2,1)S(1)} %bitcast.17, f32[512,32]{1,0:T(8,128)S(1)} %bitcast.18), custom_call_target="tpu_custom_call" | custom-call | tf_op jit(solution)/shard_map/pallas_call | solution.py:35
  94.5 1.8 copy-done
  96.2 17.4 %all_to_all.20.parts_ref = f32[32,14,128]{2,1,0:T(8,128)S(1)} all-to-all(f32[32,14,128]{2,1,0:T(8,128)S(1)} %get-tuple-element.14), channel_id=1, replica_groups=mesh['dp_0'=4,'dp_1'=8,'expert'=16] {'dp_0','dp_1'}, dimensions={0} | all-to-all | bytes 458752 | tf_op jit(solution)/shard_map/all_to_all | solution.py:221
  114.4 6.3 %all-to-all-start.2 = ((f32[32,14,128]{2,1,0:T(8,128)}), f32[32,14,128]{2,1,0:T(8,128)S(1)}, u32[]{:S(2)}, u32[]{:S(2)}) async-start(f32[32,14,128]{2,1,0:T(8,128)} %shard_map.97), calls=%async_computation.2 | async-start | bytes 524288 | tf_op jit(solution)/shard_map/all_to_all | solution.py:228
  120.7 1.5 copy-done.6
  122.2 1.2 shard_map.98
  123.4 1.3 copy-done.4
  124.6 5.7 %all-to-all-done.2.factor_ref = f32[32,14,128]{2,1,0:T(8,128)S(1)} async-done(((f32[32,14,128]{2,1,0:T(8,128)}), f32[32,14,128]{2,1,0:T(8,128)S(1)}, u32[]{:S(2)}, u32[]{:S(2)}) %all-to-all-start.2) | async-done | bytes 229408 | tf_op jit(solution)/shard_map/all_to_all | solution.py:228
  130.4 11.0 %all-to-all-start.3 = ((bf16[16,32,1792]{2,1,0:T(8,128)(2,1)}), bf16[16,32,1792]{2,1,0:T(8,128)(2,1)S(1)}, u32[]{:S(2)}, u32[]{:S(2)}) async-start(bf16[16,32,1792]{2,1,0:T(8,128)(2,1)} %bitcast.16), calls=%async_computation.3 | async-start | bytes 3670016 | tf_op jit(solution)/shard_map/all_to_all | solution.py:230
  141.4 2.0 %copy-done.1 = f32[1792,512]{1,0:T(8,128)S(1)} copy-done((f32[1792,512]{1,0:T(8,128)S(1)}, f32[1792,512]{1,0:T(8,128)}, u32[]{:S(2)}) %copy-start.1) | copy-done | bytes 3670040
  143.8 3.4 %collective-permute-start = (f32[32,512]{1,0:T(8,128)S(1)}, f32[32,512]{1,0:T(8,128)S(1)}, u32[]{:S(2)}, u32[]{:S(2)}) collective-permute-start(f32[32,512]{1,0:T(8,128)S(1)} %shard_map.100), channel_id=1, source_target_pairs={{0,16},{16,0},{32,48},{48,32},{64,80},{80,64},{96,112},{112,96},{1... | collective-permute-start | bytes 196616 | tf_op jit(solution)/shard_map/ppermute | solution.py:183
  147.3 2.2 %collective-permute-done = f32[32,512]{1,0:T(8,128)S(1)} collective-permute-done((f32[32,512]{1,0:T(8,128)S(1)}, f32[32,512]{1,0:T(8,128)S(1)}, u32[]{:S(2)}, u32[]{:S(2)}) %collective-permute-start) | collective-permute-done | bytes 65568 | tf_op jit(solution)/shard_map/ppermute | solution.py:183
  149.4 3.7 %collective-permute-start.1 = (f32[32,512]{1,0:T(8,128)S(1)}, f32[32,512]{1,0:T(8,128)S(1)}, u32[]{:S(2)}, u32[]{:S(2)}) collective-permute-start(f32[32,512]{1,0:T(8,128)S(1)} %add.21), channel_id=1, source_target_pairs={{0,32},{16,48},{32,0},{48,16},{64,96},{80,112},{96,64},{112,80},{1... | collective-permute-start | bytes 196616 | tf_op jit(solution)/shard_map/ppermute | solution.py:183
  153.1 2.5 %collective-permute-done.1 = f32[32,512]{1,0:T(8,128)S(1)} collective-permute-done((f32[32,512]{1,0:T(8,128)S(1)}, f32[32,512]{1,0:T(8,128)S(1)}, u32[]{:S(2)}, u32[]{:S(2)}) %collective-permute-start.1) | collective-permute-done | bytes 65568 | tf_op jit(solution)/shard_map/ppermute | solution.py:183
  155.7 4.3 %collective-permute-start.2 = (f32[32,512]{1,0:T(8,128)S(1)}, f32[32,512]{1,0:T(8,128)S(1)}, u32[]{:S(2)}, u32[]{:S(2)}) collective-permute-start(f32[32,512]{1,0:T(8,128)S(1)} %add.22), channel_id=1, source_target_pairs={{0,64},{16,80},{32,96},{48,112},{64,0},{80,16},{96,32},{112,48},{1... | collective-permute-start | bytes 196616 | tf_op jit(solution)/shard_map/ppermute | solution.py:183
  160.0 4.9 %collective-permute-done.2 = f32[32,512]{1,0:T(8,128)S(1)} collective-permute-done((f32[32,512]{1,0:T(8,128)S(1)}, f32[32,512]{1,0:T(8,128)S(1)}, u32[]{:S(2)}, u32[]{:S(2)}) %collective-permute-start.2) | collective-permute-done | bytes 65568 | tf_op jit(solution)/shard_map/ppermute | solution.py:183
  164.9 2.3 %collective-permute-start.3 = (f32[32,512]{1,0:T(8,128)S(1)}, f32[32,512]{1,0:T(8,128)S(1)}, u32[]{:S(2)}, u32[]{:S(2)}) collective-permute-start(f32[32,512]{1,0:T(8,128)S(1)} %add.23), channel_id=1, source_target_pairs={{0,128},{128,0},{256,384},{384,256},{1,129},{129,1},{257,385},{385... | collective-permute-start | bytes 196616 | tf_op jit(solution)/shard_map/ppermute | solution.py:183
  167.6 4.9 %shard_map.101.refs_1_ = f32[32,1792]{1,0:T(8,128)S(1)} custom-call(f32[32,14,128]{2,1,0:T(8,128)S(1)} %all-to-all-done.2.factor_ref), custom_call_target="tpu_custom_call" | custom-call | tf_op jit(solution)/shard_map/pallas_call | solution.py:35
  172.6 3.8 %collective-permute-start.4 = (f32[32,512]{1,0:T(8,128)S(1)}, f32[32,512]{1,0:T(8,128)S(1)}, u32[]{:S(2)}, u32[]{:S(2)}) collective-permute-start(f32[32,512]{1,0:T(8,128)S(1)} %add.24), channel_id=1, source_target_pairs={{0,256},{128,384},{256,0},{384,128},{1,257},{129,385},{257,1},{385... | collective-permute-start | bytes 196616 | tf_op jit(solution)/shard_map/ppermute | solution.py:183
  176.4 2.9 %collective-permute-done.4 = f32[32,512]{1,0:T(8,128)S(1)} collective-permute-done((f32[32,512]{1,0:T(8,128)S(1)}, f32[32,512]{1,0:T(8,128)S(1)}, u32[]{:S(2)}, u32[]{:S(2)}) %collective-permute-start.4) | collective-permute-done | bytes 65568 | tf_op jit(solution)/shard_map/ppermute | solution.py:183
  179.4 2.0 %copy-done.2 = f32[1792,512]{1,0:T(8,128)S(1)} copy-done((f32[1792,512]{1,0:T(8,128)S(1)}, f32[1792,512]{1,0:T(8,128)}, u32[]{:S(2)}) %copy-start.2) | copy-done | bytes 3670040
  181.4 4.0 %shard_map.102 = (bf16[1792,512]{1,0:T(8,128)(2,1)}, f32[56,512]{1,0:T(8,128)}) custom-call(f32[32,512]{1,0:T(8,128)S(1)} %add.25.refs_0_, f32[32,1792]{1,0:T(8,128)S(1)} %shard_map.101.refs_1_, f32[32,56]{1,0:T(8,128)S(1)} %constant_dynamic-slice_fusion.refs_2_, f32[1792,512]{1,0:T(8,128)S(1)} %copy-done.2), custom_call_target="tpu_custom_call" | custom-call | tf_op jit(solution)/shard_map/pallas_call | solution.py:35
  185.4 1.4 shard_map.99
  (37 shorter events, 3.3 us)
Async XLA Ops:
  8.1 1.0 copy-start.8
  9.2 0.7 copy-start.9
  9.9 0.7 copy-start.11
  11.6 1.4 copy-start.3
  13.0 12.0 %copy-start.14 = (bf16[1,56,512]{2,1,0:T(8,128)(2,1)S(1)}, bf16[1,56,512]{2,1,0:T(8,128)(2,1)}, u32[]{:S(2)}) copy-start(bf16[1,56,512]{2,1,0:T(8,128)(2,1)} %param.11) | copy-start | bytes 172036
  13.0 36.1 %copy-start.13 = (f32[1,512,32]{1,2,0:T(8,128)S(1)}, f32[1,512,32]{1,2,0:T(8,128)}, u32[]{:S(2)}) copy-start(f32[1,512,32]{1,2,0:T(8,128)} %param.13) | copy-start | bytes 196612
  13.0 74.3 %all-to-all-start = ((bf16[16,32,2304]{2,1,0:T(8,128)(2,1)}), bf16[16,32,2304]{2,1,0:T(8,128)(2,1)S(1)}, u32[]{:S(2)}, u32[]{:S(2)}) async-start(bf16[16,32,2304]{2,1,0:T(8,128)(2,1)} %bitcast.14), calls=%async_computation | async-start | bytes 4718592 | tf_op jit(solution)/shard_map/all_to_all | solution.py:204
  25.0 62.3 %all-gather.2.cloned.1.call-start = ((), (), s32[]{:S(2)}) async-start(), calls=%async_computation.4 | async-start | bytes 2293760 | tf_op jit(solution)/shard_map/all_gather | solution.py:207
  87.3 1.5 copy-start.5
  88.8 1.5 copy-start.7
  94.4 1.8 copy-start
  114.4 16.0 %all-to-all-start.2 = ((f32[32,14,128]{2,1,0:T(8,128)}), f32[32,14,128]{2,1,0:T(8,128)S(1)}, u32[]{:S(2)}, u32[]{:S(2)}) async-start(f32[32,14,128]{2,1,0:T(8,128)} %shard_map.97), calls=%async_computation.2 | async-start | bytes 524288 | tf_op jit(solution)/shard_map/all_to_all | solution.py:228
  120.7 1.5 copy-start.6
  123.4 1.3 copy-start.4
  130.4 55.1 %all-to-all-start.3 = ((bf16[16,32,1792]{2,1,0:T(8,128)(2,1)}), bf16[16,32,1792]{2,1,0:T(8,128)(2,1)S(1)}, u32[]{:S(2)}, u32[]{:S(2)}) async-start(bf16[16,32,1792]{2,1,0:T(8,128)(2,1)} %bitcast.16), calls=%async_computation.3 | async-start | bytes 3670016 | tf_op jit(solution)/shard_map/all_to_all | solution.py:230
  141.4 2.0 %copy-start.1 = (f32[1792,512]{1,0:T(8,128)S(1)}, f32[1792,512]{1,0:T(8,128)}, u32[]{:S(2)}) copy-start(f32[1792,512]{1,0:T(8,128)} %copy-done) | copy-start | bytes 11010052
  143.4 23.7 %copy-start.10 = (s32[128,2]{0,1:T(2,128)S(1)}, s32[128,2]{0,1:T(2,128)}, u32[]{:S(2)}) copy-start(s32[128,2]{0,1:T(2,128)} %param.8) | copy-start | bytes 3076
  143.4 24.0 %copy-start.12 = (f32[128,2]{0,1:T(2,128)S(1)}, f32[128,2]{0,1:T(2,128)}, u32[]{:S(2)}) copy-start(f32[128,2]{0,1:T(2,128)} %param.9) | copy-start | bytes 3076
  143.8 5.6 %collective-permute-start = (f32[32,512]{1,0:T(8,128)S(1)}, f32[32,512]{1,0:T(8,128)S(1)}, u32[]{:S(2)}, u32[]{:S(2)}) collective-permute-start(f32[32,512]{1,0:T(8,128)S(1)} %shard_map.100), channel_id=1, source_target_pairs={{0,16},{16,0},{32,48},{48,32},{64,80},{80,64},{96,112},{112,96},{1... | collective-permute-start | bytes 196616 | tf_op jit(solution)/shard_map/ppermute | solution.py:183
  149.4 6.2 %collective-permute-start.1 = (f32[32,512]{1,0:T(8,128)S(1)}, f32[32,512]{1,0:T(8,128)S(1)}, u32[]{:S(2)}, u32[]{:S(2)}) collective-permute-start(f32[32,512]{1,0:T(8,128)S(1)} %add.21), channel_id=1, source_target_pairs={{0,32},{16,48},{32,0},{48,16},{64,96},{80,112},{96,64},{112,80},{1... | collective-permute-start | bytes 196616 | tf_op jit(solution)/shard_map/ppermute | solution.py:183
  155.7 9.2 %collective-permute-start.2 = (f32[32,512]{1,0:T(8,128)S(1)}, f32[32,512]{1,0:T(8,128)S(1)}, u32[]{:S(2)}, u32[]{:S(2)}) collective-permute-start(f32[32,512]{1,0:T(8,128)S(1)} %add.22), channel_id=1, source_target_pairs={{0,64},{16,80},{32,96},{48,112},{64,0},{80,16},{96,32},{112,48},{1... | collective-permute-start | bytes 196616 | tf_op jit(solution)/shard_map/ppermute | solution.py:183
  164.9 7.7 %collective-permute-start.3 = (f32[32,512]{1,0:T(8,128)S(1)}, f32[32,512]{1,0:T(8,128)S(1)}, u32[]{:S(2)}, u32[]{:S(2)}) collective-permute-start(f32[32,512]{1,0:T(8,128)S(1)} %add.23), channel_id=1, source_target_pairs={{0,128},{128,0},{256,384},{384,256},{1,129},{129,1},{257,385},{385... | collective-permute-start | bytes 196616 | tf_op jit(solution)/shard_map/ppermute | solution.py:183
  172.6 6.8 %collective-permute-start.4 = (f32[32,512]{1,0:T(8,128)S(1)}, f32[32,512]{1,0:T(8,128)S(1)}, u32[]{:S(2)}, u32[]{:S(2)}) collective-permute-start(f32[32,512]{1,0:T(8,128)S(1)} %add.24), channel_id=1, source_target_pairs={{0,256},{128,384},{256,0},{384,128},{1,257},{129,385},{257,1},{385... | collective-permute-start | bytes 196616 | tf_op jit(solution)/shard_map/ppermute | solution.py:183
  179.4 2.0 %copy-start.2 = (f32[1792,512]{1,0:T(8,128)S(1)}, f32[1792,512]{1,0:T(8,128)}, u32[]{:S(2)}) copy-start(f32[1792,512]{1,0:T(8,128)} %copy-done) | copy-start | bytes 11010052
Sparse Core Ops, SparseCore 0:
  49.3 37.9 all-gather.1

commit v2 on v1

v2 whole, which is shorter than its diff:
```python
import jax
import jax.numpy as jnp
from jax import lax
from jax.experimental import pallas as pl
from jax.experimental.pallas import tpu as pltpu
from jax.sharding import Mesh
from jax.sharding import PartitionSpec as P

DP = ("dp_0", "dp_1")
DP_EXPERT = ("dp_0", "dp_1", "expert")

f32, bf16 = jnp.float32, jnp.bfloat16
HBM = pl.BlockSpec(memory_space=pltpu.HBM)
VMEM = pl.BlockSpec(memory_space=pltpu.VMEM)
TILES = 7
ROOM = 50_000_000
LANES = 128


def nn(a, b):
    return lax.dot_general(a, b, (((1,), (0,)), ((), ())), preferred_element_type=f32)


def nt(a, b):
    return lax.dot_general(a, b, (((1,), (1,)), ((), ())), preferred_element_type=f32)


def tn(a, b):
    return lax.dot_general(a, b, (((0,), (0,)), ((), ())), preferred_element_type=f32)


def halves(x):
    high = x.astype(bf16)
    return high, (x - high.astype(f32)).astype(bf16)


def call(kernel, outs, args, room=63_400_000, **more):
    return pl.pallas_call(
        kernel,
        out_shape=outs,
        compiler_params=pltpu.CompilerParams(vmem_limit_bytes=room),
        cost_estimate=pl.CostEstimate(flops=0, bytes_accessed=0, transcendentals=0),
        **more,
    )(*args)


def one_hots(routes, experts, capacity):
    rows = routes.shape[1]
    slots = experts * capacity
    before = (
        lax.broadcasted_iota(jnp.int32, (rows, rows), 0) < lax.broadcasted_iota(jnp.int32, (rows, rows), 1)
    ).astype(bf16)
    expert = lax.broadcasted_iota(jnp.int32, (experts, rows), 0)
    slot = lax.broadcasted_iota(jnp.int32, (slots, rows), 0)
    started = jnp.zeros((experts, 1), f32)
    out = []
    for k in range(2):
        chosen = routes[k : k + 1, :]
        match = (expert == chosen).astype(f32)
        earlier = nn(match.astype(bf16), before) + started
        place = jnp.sum(match * earlier, axis=0, keepdims=True).astype(jnp.int32) + chosen * capacity
        out.append((slot == place).astype(f32))
        started = started + jnp.sum(match, axis=1, keepdims=True)
    return out


def prepare_kernel(
    experts, capacity, routes_hbm, gates_hbm, tokens_hbm, grad_hbm, sent_hbm, routes, gates, tokens, grad, sent, sem
):
    width = tokens.shape[1]
    hidden = grad.shape[1] // 2
    copies = [
        pltpu.make_async_copy(routes_hbm, routes, sem.at[0]),
        pltpu.make_async_copy(gates_hbm, gates, sem.at[1]),
        pltpu.make_async_copy(tokens_hbm, tokens, sem.at[2]),
        pltpu.make_async_copy(grad_hbm, grad, sem.at[3]),
    ]
    for copy in copies:
        copy.start()
    copies[0].wait()
    first, second = one_hots(routes[...], experts, capacity)
    copies[1].wait()
    gate = jnp.sum(first * gates[0:1, :] + second * gates[1:2, :], axis=1, keepdims=True)
    either, first, second = (first + second).astype(bf16), first.astype(bf16), second.astype(bf16)
    copies[2].wait()
    copies[3].wait()
    parts = 4
    step = first.shape[0] // parts
    done = []
    for i in range(parts):
        rows = slice(i * step, (i + 1) * step)
        sent[rows, :width] = (nn(either[rows], tokens[...]) * gate[rows]).astype(bf16)
        grads = nn(first[rows], grad[:, :hidden]) + nn(second[rows], grad[:, hidden:])
        sent[rows, width:] = grads.astype(bf16)
        copy = pltpu.make_async_copy(sent.at[rows], sent_hbm.at[rows], sem.at[4 + i])
        copy.start()
        done.append(copy)
    for copy in done:
        copy.wait()


def select_kernel(experts, capacity, routes_ref, select_ref):
    rows = routes_ref.shape[1]
    for k, places in enumerate(one_hots(routes_ref[...], experts, capacity)):
        select_ref[k * rows : (k + 1) * rows, :] = places.T.astype(bf16)


def merge_kernel(
    width,
    arrived_hbm,
    weight_0_hbm,
    weight_1_hbm,
    error_hbm,
    seed_ref,
    grad_pre_ref,
    merged_hbm,
    rounded_hbm,
    factor_ref,
    arrived_ref,
    weight_0,
    weight_1,
    error,
    merged,
    rounded,
    arrived_sem,
    weight_sem,
    error_sem,
    merged_sem,
    rounded_sem,
):
    rank = seed_ref.shape[1]
    step = width // TILES
    tiles = [slice(i * step, (i + 1) * step) for i in range(TILES)]
    needs = []
    for i, rows in enumerate(tiles):
        needs.append(
            [
                pltpu.make_async_copy(arrived_hbm.at[:, rows], arrived_ref.at[:, rows], arrived_sem.at[i]),
                pltpu.make_async_copy(weight_0_hbm.at[rows], weight_0.at[rows], weight_sem.at[2 * i]),
                pltpu.make_async_copy(weight_1_hbm.at[rows], weight_1.at[rows], weight_sem.at[2 * i + 1]),
            ]
        )
        for load in needs[i]:
            load.start()
    rest = slice(width, arrived_ref.shape[1])
    grads = pltpu.make_async_copy(arrived_hbm.at[:, rest], arrived_ref.at[:, rest], arrived_sem.at[TILES])
    grads.start()
    loads = [
        pltpu.make_async_copy(error_hbm.at[rows], error.at[rows], error_sem.at[i])
        for i, rows in enumerate(tiles)
    ]
    for load in loads:
        load.start()
    pre = jnp.zeros(grad_pre_ref.shape, f32)
    for i, rows in enumerate(tiles):
        for load in needs[i]:
            load.wait()
        weight = jnp.concatenate([weight_0[rows, :], weight_1[rows, :]], axis=1)
        pre = pre + nn(arrived_ref[:, rows], weight)
    grads.wait()
    s = 1.0 / (1.0 + jnp.exp(-pre))
    grad_pre = (arrived_ref[:, width:].astype(f32) * (s * (1.0 + pre * (1.0 - s)))).astype(bf16)
    grad_pre_ref[...] = grad_pre
    high, low = halves(seed_ref[...])
    both = jnp.concatenate([high, low], axis=1)
    stores = []
    for i, rows in enumerate(tiles):
        loads[i].wait()
        total = tn(arrived_ref[:, rows], grad_pre) + error[rows, :].astype(f32)
        upper, lower = halves(total)
        merged[rows, :] = total
        rounded[rows, :] = upper
        stores.append(pltpu.make_async_copy(merged.at[rows], merged_hbm.at[rows], merged_sem.at[i]))
        stores.append(pltpu.make_async_copy(rounded.at[rows], rounded_hbm.at[rows], rounded_sem.at[i]))
        for store in stores[-2:]:
            store.start()
        part = nn(upper, both)
        part = part[:, :rank] + part[:, rank:] + nn(lower, high)
        part = part.T
        for j in range(step // LANES):
            factor_ref[:, i * (step // LANES) + j, :] = part[:, j * LANES : (j + 1) * LANES]
    for store in stores:
        store.wait()


def rows_kernel(grad_pre_ref, weight_0, weight_1, grad_rows_ref):
    half = weight_0.shape[1]
    rows = nt(grad_pre_ref[:, :half], weight_0[...]) + nt(grad_pre_ref[:, half:], weight_1[...])
    grad_rows_ref[...] = rows.astype(bf16)


def sum_and_copy_kernel(parts_ref, copies_ref):
    total = jnp.sum(parts_ref[...], axis=0)
    copies_ref[...] = jnp.broadcast_to(total[None], copies_ref.shape)


def right_kernel(factor_ref, rounded_hbm, right_ref, rounded, sem):
    rank, blocks, _ = factor_ref.shape
    step = 2 * LANES
    loads = []
    for i in range(blocks // 2):
        rows = slice(i * step, (i + 1) * step)
        loads.append(pltpu.make_async_copy(rounded_hbm.at[rows], rounded.at[rows], sem.at[i]))
        loads[i].start()
    total = jnp.zeros(right_ref.shape, f32)
    for i in range(blocks // 2):
        pair = jnp.concatenate([factor_ref[:, 2 * i, :], factor_ref[:, 2 * i + 1, :]], axis=1)
        both = jnp.concatenate(halves(pair), axis=0)
        loads[i].wait()
        part = nn(both, rounded[i * step : (i + 1) * step, :])
        total = total + part[:rank] + part[rank:]
    right_ref[...] = total


def left_kernel(factor_ref, left_ref, gathered_ref):
    rank, blocks, _ = factor_ref.shape
    for j in range(blocks):
        gathered_ref[:, j * LANES : (j + 1) * LANES] = factor_ref[:, j, :]
    high, low = halves(gathered_ref[...])
    gram = nt(high, high) + nt(high, low) + nt(low, high)
    line = lax.broadcasted_iota(jnp.int32, (rank, rank), 0)
    column = lax.broadcasted_iota(jnp.int32, (rank, rank), 1)
    both = jnp.concatenate([gram, (line == column).astype(f32)], axis=1)
    own = lax.broadcasted_iota(jnp.int32, both.shape, 0)
    for i in range(rank):
        row = both[i : i + 1, :] / both[i : i + 1, i : i + 1]
        both = jnp.where(own == i, row, both - both[:, i : i + 1] * row)
    upper, lower = halves(both[:, rank:])
    left_ref[...] = nn(upper, high) + nn(upper, low) + nn(lower, high)


def finish_kernel(
    count, total_ref, left_ref, mine_ref, merged_hbm, error_hbm, weight_ref, merged, error, load_sem, store_sem
):
    step = merged.shape[0] // TILES
    tiles = [slice(i * step, (i + 1) * step) for i in range(TILES)]
    loads = [
        pltpu.make_async_copy(merged_hbm.at[rows], merged.at[rows], load_sem.at[i])
        for i, rows in enumerate(tiles)
    ]
    for load in loads:
        load.start()
    high, low = halves(total_ref[...] / count)
    right = jnp.concatenate([high, low, high], axis=0)
    upper, lower = halves(mine_ref[...])
    weight_ref[...] = tn(jnp.concatenate([upper, upper, lower], axis=0), right)
    stores = []
    for i, rows in enumerate(tiles):
        upper, lower = halves(left_ref[:, rows])
        low_rank = tn(jnp.concatenate([upper, upper, lower], axis=0), right)
        loads[i].wait()
        error[rows, :] = (merged[rows, :] - low_rank).astype(bf16)
        stores.append(pltpu.make_async_copy(error.at[rows], error_hbm.at[rows], store_sem.at[i]))
        stores[i].start()
    for store in stores:
        store.wait()


def combine_kernel(select_ref, gates_ref, returned_ref, out_hbm, out, store_sem):
    rows, width = out.shape
    step = width // TILES
    tiles = [slice(i * step, (i + 1) * step) for i in range(TILES)]
    gates = gates_ref[...]
    stores = []
    for i, c in enumerate(tiles):
        picked = nn(select_ref[...], returned_ref[:, c])
        out[:, c] = (picked[:rows] * gates[:, 0:1] + picked[rows:] * gates[:, 1:2]).astype(bf16)
        stores.append(pltpu.make_async_copy(out.at[:, c], out_hbm.at[:, c], store_sem.at[i]))
        stores[i].start()
    for store in stores:
        store.wait()


def shape(dims, dtype):
    return jax.ShapeDtypeStruct(dims, dtype)


def summed(x, axis):
    size = lax.axis_size(axis)
    partners = [1 << k for k in range(size.bit_length() - 1)]
    if len(partners) > 1:
        partners[-1] = size - 1
    for partner in partners:
        x = x + lax.ppermute(x, axis, [(i, i ^ partner) for i in range(size)])
    return x


def body(tokens, routes, gates, grad_hidden, w_in, error, q_seed):
    experts = lax.axis_size("expert")
    replicas = lax.axis_size(DP)
    row_count, width = tokens.shape
    hidden = grad_hidden.shape[2]
    rank = q_seed.shape[2]
    capacity = 4 * row_count // experts
    slots = experts * capacity
    routes_t = routes.T
    dma = pltpu.SemaphoreType.DMA

    sent = call(
        lambda *refs: prepare_kernel(experts, capacity, *refs),
        shape((slots, width + hidden), bf16),
        (routes_t, gates.T, tokens, grad_hidden.reshape(row_count, 2 * hidden)),
        in_specs=[HBM, HBM, HBM, HBM],
        out_specs=HBM,
        scratch_shapes=[
            pltpu.VMEM((2, row_count), jnp.int32),
            pltpu.VMEM((2, row_count), f32),
            pltpu.VMEM((row_count, width), bf16),
            pltpu.VMEM((row_count, 2 * hidden), bf16),
            pltpu.VMEM((slots, width + hidden), bf16),
            dma((8,)),
        ],
    )
    w_mine, sent = lax.optimization_barrier((w_in[0], sent))
    arrived = lax.all_to_all(
        sent.reshape(experts, capacity, width + hidden), "expert", 0, 0, tiled=True
    ).reshape(slots, width + hidden)
    weight = lax.all_gather(w_mine, DP[1], tiled=True)
    half = hidden // 2
    weight_0 = lax.all_gather(weight[:, :half], DP[0], tiled=True)
    weight_1 = lax.all_gather(weight[:, half:], DP[0], tiled=True)
    select = call(
        lambda *refs: select_kernel(experts, capacity, *refs),
        shape((2 * row_count, slots), bf16),
        (routes_t,),
    )

    blocks = width // LANES
    grad_pre, merged, rounded, factor = call(
        lambda *refs: merge_kernel(width, *refs),
        (
            shape((slots, hidden), bf16),
            shape((width, hidden), f32),
            shape((width, hidden), bf16),
            shape((rank, blocks, LANES), f32),
        ),
        (arrived, weight_0, weight_1, error[0, 0], q_seed[0]),
        in_specs=[HBM, HBM, HBM, HBM, VMEM],
        out_specs=[VMEM, HBM, HBM, VMEM],
        scratch_shapes=[
            pltpu.VMEM((slots, width + hidden), bf16),
            pltpu.VMEM((width, half), bf16),
            pltpu.VMEM((width, half), bf16),
            pltpu.VMEM((width, hidden), bf16),
            pltpu.VMEM((width, hidden), f32),
            pltpu.VMEM((width, hidden), bf16),
            dma((TILES + 1,)),
            dma((2 * TILES,)),
            dma((TILES,)),
            dma((TILES,)),
            dma((TILES,)),
        ],
    )
    each = rank // replicas
    parts = lax.all_to_all(factor, DP, 0, 0, tiled=True)
    grad_rows = call(rows_kernel, shape((slots, width), bf16), (grad_pre, weight_0, weight_1))
    copies = call(
        sum_and_copy_kernel,
        shape((replicas, each * blocks, LANES), f32),
        (parts.reshape(replicas, each * blocks, LANES),),
    )
    factor = lax.all_to_all(copies, DP, 0, 0, tiled=True).reshape(rank, blocks, LANES)
    right = call(
        right_kernel,
        shape((rank, hidden), f32),
        (factor, rounded),
        in_specs=[VMEM, HBM],
        scratch_shapes=[pltpu.VMEM((width, hidden), bf16), dma((blocks // 2,))],
    )
    right, grad_rows = lax.optimization_barrier((right, grad_rows))
    returned = lax.all_to_all(
        grad_rows.reshape(experts, capacity, width), "expert", 0, 0, tiled=True
    ).reshape(slots, width)

    right = summed(summed(right, DP[1]), DP[0])
    left = call(
        left_kernel,
        shape((rank, width), f32),
        (factor,),
        scratch_shapes=[pltpu.VMEM((rank, width), f32)],
    )
    shard = width // replicas
    mine = lax.dynamic_slice_in_dim(left, lax.axis_index(DP) * shard, shard, 1)
    error_next, weight_grad = call(
        lambda *refs: finish_kernel(replicas, *refs),
        (shape((width, hidden), bf16), shape((shard, hidden), f32)),
        (right, left, mine, merged),
        in_specs=[VMEM, VMEM, VMEM, HBM],
        out_specs=[HBM, VMEM],
        scratch_shapes=[
            pltpu.VMEM((width, hidden), f32),
            pltpu.VMEM((width, hidden), bf16),
            dma((TILES,)),
            dma((TILES,)),
        ],
    )
    grad_tokens = call(
        combine_kernel,
        shape((row_count, width), bf16),
        (select, gates, returned),
        room=ROOM,
        in_specs=[VMEM, VMEM, VMEM],
        out_specs=HBM,
        scratch_shapes=[pltpu.VMEM((row_count, width), bf16), dma((TILES,))],
    )
    return grad_tokens, error_next[None, None], weight_grad[None]


def solution(mesh):
    torus = Mesh(mesh.devices.reshape(4, 8, mesh.shape["expert"]), DP_EXPERT)
    in_specs = (
        P(DP_EXPERT, None),
        P(DP_EXPERT, None),
        P(DP_EXPERT, None),
        P(DP_EXPERT, None, None),
        P("expert", DP, None),
        P(DP, "expert", None, None),
        P("expert", None, None),
    )
    out_specs = (P(DP_EXPERT, None), P(DP, "expert", None, None), P("expert", DP, None))
    return jax.shard_map(body, mesh=torus, in_specs=in_specs, out_specs=out_specs, check_vma=False)
```

time: 197 us -> 181 us (0.919); the launches traced: 194 us -> 180 us
  waiting for transfers between devices: 56.3 us -> 25.9 us
  blocking collectives: 41.5 us -> 67.9 us
  Pallas kernels: 18.2 us -> 35.9 us
  between operations: 14.3 us -> 0.78 us
  local copies, waits for them, and re-layouts: 16.7 us -> 6.24 us
  starting transfers between devices: 46.7 us -> 42.4 us
    all_gather x1 -> x0, waiting for transfers between devices: 38 us -> none  [body(): lax.all_gather(lax.all_gather(w_mine, DP[1], tiled=True), DP[0], tiled=True)]
    all_gather x1 -> x3, blocking collectives: 24.1 us -> 48.4 us  [the longest x1 22.6 us: body(): weight = lax.all_gather(w_mine, DP[1], tiled=True)]
    pallas_call x9, Pallas kernels: 18.2 us -> 35.9 us  [call(): pl.pallas_call(kernel, out_shape=outs, compiler_params=pltpu.CompilerPara...]
    unnamed x33 -> x17, local copies, waits for them, and re-layouts: 16.6 us -> 4.77 us
    all_to_all x1, waiting for transfers between devices: 0.01 us -> 5.06 us  [body(): lax.all_to_all(sent.reshape(experts, capacity, width + hidden), 'expert',...]
    all_to_all x1, waiting for transfers between devices: 0.01 us -> 3.59 us  [body(): lax.all_to_all(grad_rows.reshape(experts, capacity, width), 'expert', 0,...]
    ppermute x5, starting transfers between devices: 17.5 us -> 14.3 us  [summed(): x = x + lax.ppermute(x, axis, [(i, i ^ partner) for i in range(size)])]
    all_to_all x1, blocking collectives: 17.4 us -> 19.4 us  [body(): parts = lax.all_to_all(factor, DP, 0, 0, tiled=True)]
  transfers between devices with their start and end apart: 9 -> 8, of which waited for: 6 -> 7; matrix products, arithmetic and copies ran while one was open for 0% -> 2% of each run, Pallas kernels for 6% -> 9%
where the time goes in v2:
time: 181 us; the launch traced here: 180 us
  blocking collectives  67.9 us (38%)
  starting transfers between devices  42.4 us (23%)
  Pallas kernels  35.9 us (20%)
  waiting for transfers between devices  25.9 us (14%)
  local copies, waits for them, and re-layouts  6.24 us (3%)
    pallas_call x9, Pallas kernels, call(): pl.pallas_call(kernel, out_shape=outs, compiler_params=pltpu.CompilerPara...  35.9 us
    all_gather x1, blocking collectives, body(): weight = lax.all_gather(w_mine, DP[1], tiled=True)  22.6 us
    all_to_all x1, blocking collectives, body(): parts = lax.all_to_all(factor, DP, 0, 0, tiled=True)  19.4 us
    ppermute x5, starting transfers between devices, summed(): x = x + lax.ppermute(x, axis, [(i, i ^ partner) for i in range(size)])  14.3 us
    all_gather x1, blocking collectives, body(): weight_1 = lax.all_gather(weight[:, half:], DP[0], tiled=True)  13.3 us
    all_gather x1, blocking collectives, body(): weight_0 = lax.all_gather(weight[:, :half], DP[0], tiled=True)  12.5 us
    all_to_all x1, starting transfers between devices, body(): lax.all_to_all(sent.reshape(experts, capacity, width + hidden), 'expert',...  12 us
    ppermute x5, waiting for transfers between devices, summed(): x = x + lax.ppermute(x, axis, [(i, i ^ partner) for i in range(size)])  11.7 us
  transfers between devices with their start and end apart: 8, of which 7 were waited for; matrix products, arithmetic and copies ran while one was open for 2% of the time, Pallas kernels for 9%

profile of v2, /device:TPU:1, one launch (start us, length us, event | category | flops | bytes accessed | tf_op | source)
XLA Modules:
  0.0 179.9 jit_solution(11857706122618922132)
XLA Ops:
  0.6 1.7 copy.12
  2.3 3.0 %shard_map.95 = bf16[512,2304]{1,0:T(8,128)(2,1)} custom-call(s32[2,128]{1,0:T(2,128)} %bitcast.22, f32[2,128]{1,0:T(2,128)} %bitcast.24, bf16[128,1792]{1,0:T(8,128)(2,1)} %refs_2_.1, bf16[128,1024]{1,0:T(8,128)(2,1)} %bitcast.19), custom_call_target="tpu_custom_call" | custom-call | tf_op jit(solution)/shard_map/pallas_call | solution.py:38
  5.3 12.0 %all-to-all-start = ((bf16[16,32,2304]{2,1,0:T(8,128)(2,1)}), bf16[16,32,2304]{2,1,0:T(8,128)(2,1)S(1)}, u32[]{:S(2)}, u32[]{:S(2)}) async-start(bf16[16,32,2304]{2,1,0:T(8,128)(2,1)} %bitcast.15), calls=%async_computation | async-start | bytes 4718592 | tf_op jit(solution)/shard_map/all_to_all | solution.py:315
  17.3 0.8 copy.10
  18.1 22.6 %all_gather.9 = bf16[448,512]{1,0:T(8,128)(2,1)S(1)} all-gather(bf16[56,512]{1,0:T(8,128)(2,1)S(1)} %bitcast.21), channel_id=1, replica_groups=mesh['dp_0'=4,'dp_1'=8,'expert'=16] {'dp_1'}, dimensions={0}, use_global_device_ids=true | all-gather | bytes 516096 | tf_op jit(solution)/shard_map/all_gather | solution.py:318
  40.8 12.5 %all_gather.10.refs_1_.weight_0 = bf16[1792,256]{1,0:T(8,128)(2,1)} all-gather(bf16[448,256]{1,0:T(8,128)(2,1)S(1)} %get-tuple-element.24), channel_id=1, replica_groups=mesh['dp_0'=4,'dp_1'=8,'expert'=16] {'dp_0'}, dimensions={0}, use_global_device_ids=true | all-gather | bytes 1146880 | tf_op jit(solution)/shard_map/all_gather | solution.py:320
  53.3 13.3 %all_gather.11.refs_2_.weight_1 = bf16[1792,256]{1,0:T(8,128)(2,1)} all-gather(bf16[448,256]{1,0:T(8,128)(2,1)S(1)} %get-tuple-element.23), channel_id=1, replica_groups=mesh['dp_0'=4,'dp_1'=8,'expert'=16] {'dp_0'}, dimensions={0}, use_global_device_ids=true | all-gather | bytes 1146880 | tf_op jit(solution)/shard_map/all_gather | solution.py:321
  66.6 5.1 %all-to-all-done = bf16[16,32,2304]{2,1,0:T(8,128)(2,1)S(1)} async-done(((bf16[16,32,2304]{2,1,0:T(8,128)(2,1)}), bf16[16,32,2304]{2,1,0:T(8,128)(2,1)S(1)}, u32[]{:S(2)}, u32[]{:S(2)}) %all-to-all-start) | async-done | bytes 2359328 | tf_op jit(solution)/shard_map/all_to_all | solution.py:315
  71.6 1.4 copy-done.1
  73.0 10.8 %shard_map.96 = (bf16[512,512]{1,0:T(8,128)(2,1)}, f32[1792,512]{1,0:T(8,128)}, bf16[1792,512]{1,0:T(8,128)(2,1)}, f32[32,14,128]{2,1,0:T(8,128)}) custom-call(bf16[512,2304]{1,0:T(8,128)(2,1)} %bitcast.14, bf16[1792,256]{1,0:T(8,128)(2,1)} %all_gather.10.refs_1_.weight_0, bf16[1792,256]{1,0:T(8,128)(2,1)} %all_gather.11.refs_2_.weight_1, ...), custom_call_target="tpu_custom_call" | custom-call | tf_op jit(solution)/shard_map/pallas_call | solution.py:38
  83.9 19.4 %all_to_all.20.parts_ref = f32[32,14,128]{2,1,0:T(8,128)} all-to-all(f32[32,14,128]{2,1,0:T(8,128)} %get-tuple-element.15), channel_id=1, replica_groups=mesh['dp_0'=4,'dp_1'=8,'expert'=16] {'dp_0','dp_1'}, dimensions={0} | all-to-all | bytes 458752 | tf_op jit(solution)/shard_map/all_to_all | solution.py:355
  103.3 1.7 shard_map.97
  105.0 5.2 %all-to-all-start.2 = ((f32[32,14,128]{2,1,0:T(8,128)}), f32[32,14,128]{2,1,0:T(8,128)S(1)}, u32[]{:S(2)}, u32[]{:S(2)}) async-start(f32[32,14,128]{2,1,0:T(8,128)} %shard_map.97), calls=%async_computation.2 | async-start | bytes 524288 | tf_op jit(solution)/shard_map/all_to_all | solution.py:362
  110.2 4.0 %shard_map.99 = bf16[512,1792]{1,0:T(8,128)(2,1)} custom-call(bf16[512,512]{1,0:T(8,128)(2,1)} %get-tuple-element.17.grad_pre_ref, bf16[1792,256]{1,0:T(8,128)(2,1)} %all_gather.10.refs_1_.weight_0, bf16[1792,256]{1,0:T(8,128)(2,1)} %all_gather.11.refs_2_.weight_1), custom_call_target="tpu_custom_call" | custom-call | tf_op jit(solution)/shard_map/pallas_call | solution.py:38
  114.3 5.6 %all-to-all-done.2.factor_ref = f32[32,14,128]{2,1,0:T(8,128)S(1)} async-done(((f32[32,14,128]{2,1,0:T(8,128)}), f32[32,14,128]{2,1,0:T(8,128)S(1)}, u32[]{:S(2)}, u32[]{:S(2)}) %all-to-all-start.2) | async-done | bytes 229408 | tf_op jit(solution)/shard_map/all_to_all | solution.py:362
  120.6 3.2 %shard_map.98 = f32[32,512]{1,0:T(8,128)} custom-call(f32[32,14,128]{2,1,0:T(8,128)} %copy-done.2, bf16[1792,512]{1,0:T(8,128)(2,1)} %get-tuple-element.16.rounded_hbm), custom_call_target="tpu_custom_call" | custom-call | tf_op jit(solution)/shard_map/pallas_call | solution.py:38
  123.9 11.0 %all-to-all-start.3 = ((bf16[16,32,1792]{2,1,0:T(8,128)(2,1)}), bf16[16,32,1792]{2,1,0:T(8,128)(2,1)S(1)}, u32[]{:S(2)}, u32[]{:S(2)}) async-start(bf16[16,32,1792]{2,1,0:T(8,128)(2,1)} %bitcast.16), calls=%async_computation.3 | async-start | bytes 3670016 | tf_op jit(solution)/shard_map/all_to_all | solution.py:371
  134.8 3.6 %collective-permute-start = (f32[32,512]{1,0:T(8,128)S(1)}, f32[32,512]{1,0:T(8,128)S(1)}, u32[]{:S(2)}, u32[]{:S(2)}) collective-permute-start(f32[32,512]{1,0:T(8,128)S(1)} %copy-done.3), channel_id=1, source_target_pairs={{0,16},{16,0},{32,48},{48,32},{64,80},{80,64},{96,112},{112,96},{1... | collective-permute-start | bytes 196616 | tf_op jit(solution)/shard_map/ppermute | solution.py:284
  138.5 2.3 %collective-permute-done = f32[32,512]{1,0:T(8,128)S(1)} collective-permute-done((f32[32,512]{1,0:T(8,128)S(1)}, f32[32,512]{1,0:T(8,128)S(1)}, u32[]{:S(2)}, u32[]{:S(2)}) %collective-permute-start) | collective-permute-done | bytes 65568 | tf_op jit(solution)/shard_map/ppermute | solution.py:284
  140.8 3.2 %collective-permute-start.1 = (f32[32,512]{1,0:T(8,128)S(1)}, f32[32,512]{1,0:T(8,128)S(1)}, u32[]{:S(2)}, u32[]{:S(2)}) collective-permute-start(f32[32,512]{1,0:T(8,128)S(1)} %add.21), channel_id=1, source_target_pairs={{0,32},{16,48},{32,0},{48,16},{64,96},{80,112},{96,64},{112,80},{1... | collective-permute-start | bytes 196616 | tf_op jit(solution)/shard_map/ppermute | solution.py:284
  144.0 3.0 %collective-permute-done.1 = f32[32,512]{1,0:T(8,128)S(1)} collective-permute-done((f32[32,512]{1,0:T(8,128)S(1)}, f32[32,512]{1,0:T(8,128)S(1)}, u32[]{:S(2)}, u32[]{:S(2)}) %collective-permute-start.1) | collective-permute-done | bytes 65568 | tf_op jit(solution)/shard_map/ppermute | solution.py:284
  147.0 2.3 %collective-permute-start.2 = (f32[32,512]{1,0:T(8,128)S(1)}, f32[32,512]{1,0:T(8,128)S(1)}, u32[]{:S(2)}, u32[]{:S(2)}) collective-permute-start(f32[32,512]{1,0:T(8,128)S(1)} %add.22), channel_id=1, source_target_pairs={{0,112},{16,96},{32,80},{48,64},{64,48},{80,32},{96,16},{112,0},{1... | collective-permute-start | bytes 196616 | tf_op jit(solution)/shard_map/ppermute | solution.py:284
  149.3 4.2 %collective-permute-done.2 = f32[32,512]{1,0:T(8,128)S(1)} collective-permute-done((f32[32,512]{1,0:T(8,128)S(1)}, f32[32,512]{1,0:T(8,128)S(1)}, u32[]{:S(2)}, u32[]{:S(2)}) %collective-permute-start.2) | collective-permute-done | bytes 65568 | tf_op jit(solution)/shard_map/ppermute | solution.py:284
  153.5 2.3 %collective-permute-start.3 = (f32[32,512]{1,0:T(8,128)S(1)}, f32[32,512]{1,0:T(8,128)S(1)}, u32[]{:S(2)}, u32[]{:S(2)}) collective-permute-start(f32[32,512]{1,0:T(8,128)S(1)} %add.23), channel_id=1, source_target_pairs={{0,128},{128,0},{256,384},{384,256},{1,129},{129,1},{257,385},{385... | collective-permute-start | bytes 196616 | tf_op jit(solution)/shard_map/ppermute | solution.py:284
  155.8 1.7 shard_map.94.select_ref
  157.6 5.0 %shard_map.101.refs_1_ = f32[32,1792]{1,0:T(8,128)} custom-call(f32[32,14,128]{2,1,0:T(8,128)} %copy-done.2), custom_call_target="tpu_custom_call" | custom-call | tf_op jit(solution)/shard_map/pallas_call | solution.py:38
  162.7 2.8 %collective-permute-start.4 = (f32[32,512]{1,0:T(8,128)S(1)}, f32[32,512]{1,0:T(8,128)S(1)}, u32[]{:S(2)}, u32[]{:S(2)}) collective-permute-start(f32[32,512]{1,0:T(8,128)S(1)} %add.24), channel_id=1, source_target_pairs={{0,384},{128,256},{256,128},{384,0},{1,385},{129,257},{257,129},{3... | collective-permute-start | bytes 196616 | tf_op jit(solution)/shard_map/ppermute | solution.py:284
  165.5 1.4 constant_dynamic-slice_fusion.refs_2_
  166.9 2.2 %collective-permute-done.4 = f32[32,512]{1,0:T(8,128)S(1)} collective-permute-done((f32[32,512]{1,0:T(8,128)S(1)}, f32[32,512]{1,0:T(8,128)S(1)}, u32[]{:S(2)}, u32[]{:S(2)}) %collective-permute-start.4) | collective-permute-done | bytes 65568 | tf_op jit(solution)/shard_map/ppermute | solution.py:284
  169.8 5.1 %shard_map.102 = (bf16[1792,512]{1,0:T(8,128)(2,1)}, f32[56,512]{1,0:T(8,128)}) custom-call(f32[32,512]{1,0:T(8,128)} %add.25.refs_0_, f32[32,1792]{1,0:T(8,128)} %shard_map.101.refs_1_, f32[32,56]{1,0:T(8,128)} %constant_dynamic-slice_fusion.refs_2_, f32[1792,512]{1,0:T(8,128)} %get-tuple-element.20.refs_3_), custom_call_target="tpu_custom_call" | custom-call | tf_op jit(solution)/shard_map/pallas_call | solution.py:38
  174.9 3.6 %all-to-all-done.3 = bf16[16,32,1792]{2,1,0:T(8,128)(2,1)S(1)} async-done(((bf16[16,32,1792]{2,1,0:T(8,128)(2,1)}), bf16[16,32,1792]{2,1,0:T(8,128)(2,1)S(1)}, u32[]{:S(2)}, u32[]{:S(2)}) %all-to-all-start.3) | async-done | bytes 1835040 | tf_op jit(solution)/shard_map/all_to_all | solution.py:371
  178.5 1.4 shard_map.100
  (21 shorter events, 1.6 us)
Async XLA Ops:
  5.3 12.0 %copy-start.4 = (f32[1,512,32]{1,2,0:T(8,128)S(1)}, f32[1,512,32]{1,2,0:T(8,128)}, u32[]{:S(2)}) copy-start(f32[1,512,32]{1,2,0:T(8,128)} %param.13) | copy-start | bytes 196612
  5.3 12.8 %copy-start.5 = (bf16[1,56,512]{2,1,0:T(8,128)(2,1)S(1)}, bf16[1,56,512]{2,1,0:T(8,128)(2,1)}, u32[]{:S(2)}) copy-start(bf16[1,56,512]{2,1,0:T(8,128)(2,1)} %param.11) | copy-start | bytes 172036
  5.3 66.3 %all-to-all-start = ((bf16[16,32,2304]{2,1,0:T(8,128)(2,1)}), bf16[16,32,2304]{2,1,0:T(8,128)(2,1)S(1)}, u32[]{:S(2)}, u32[]{:S(2)}) async-start(bf16[16,32,2304]{2,1,0:T(8,128)(2,1)} %bitcast.15), calls=%async_computation | async-start | bytes 4718592 | tf_op jit(solution)/shard_map/all_to_all | solution.py:315
  71.6 1.4 copy-start.1
  105.0 14.9 %all-to-all-start.2 = ((f32[32,14,128]{2,1,0:T(8,128)}), f32[32,14,128]{2,1,0:T(8,128)S(1)}, u32[]{:S(2)}, u32[]{:S(2)}) async-start(f32[32,14,128]{2,1,0:T(8,128)} %shard_map.97), calls=%async_computation.2 | async-start | bytes 524288 | tf_op jit(solution)/shard_map/all_to_all | solution.py:362
  119.9 0.7 copy-start.2
  123.8 11.0 %copy-start.3 = (f32[32,512]{1,0:T(8,128)S(1)}, f32[32,512]{1,0:T(8,128)}, u32[]{:S(2)}) copy-start(f32[32,512]{1,0:T(8,128)} %shard_map.98) | copy-start | bytes 196612
  123.8 33.7 %copy-start.6 = (f32[128,2]{0,1:T(2,128)S(1)}, f32[128,2]{0,1:T(2,128)}, u32[]{:S(2)}) copy-start(f32[128,2]{0,1:T(2,128)} %param.9) | copy-start | bytes 3076
  123.9 54.6 %all-to-all-start.3 = ((bf16[16,32,1792]{2,1,0:T(8,128)(2,1)}), bf16[16,32,1792]{2,1,0:T(8,128)(2,1)S(1)}, u32[]{:S(2)}, u32[]{:S(2)}) async-start(bf16[16,32,1792]{2,1,0:T(8,128)(2,1)} %bitcast.16), calls=%async_computation.3 | async-start | bytes 3670016 | tf_op jit(solution)/shard_map/all_to_all | solution.py:371
  134.8 5.9 %collective-permute-start = (f32[32,512]{1,0:T(8,128)S(1)}, f32[32,512]{1,0:T(8,128)S(1)}, u32[]{:S(2)}, u32[]{:S(2)}) collective-permute-start(f32[32,512]{1,0:T(8,128)S(1)} %copy-done.3), channel_id=1, source_target_pairs={{0,16},{16,0},{32,48},{48,32},{64,80},{80,64},{96,112},{112,96},{1... | collective-permute-start | bytes 196616 | tf_op jit(solution)/shard_map/ppermute | solution.py:284
  140.8 6.2 %collective-permute-start.1 = (f32[32,512]{1,0:T(8,128)S(1)}, f32[32,512]{1,0:T(8,128)S(1)}, u32[]{:S(2)}, u32[]{:S(2)}) collective-permute-start(f32[32,512]{1,0:T(8,128)S(1)} %add.21), channel_id=1, source_target_pairs={{0,32},{16,48},{32,0},{48,16},{64,96},{80,112},{96,64},{112,80},{1... | collective-permute-start | bytes 196616 | tf_op jit(solution)/shard_map/ppermute | solution.py:284
  147.0 6.5 %collective-permute-start.2 = (f32[32,512]{1,0:T(8,128)S(1)}, f32[32,512]{1,0:T(8,128)S(1)}, u32[]{:S(2)}, u32[]{:S(2)}) collective-permute-start(f32[32,512]{1,0:T(8,128)S(1)} %add.22), channel_id=1, source_target_pairs={{0,112},{16,96},{32,80},{48,64},{64,48},{80,32},{96,16},{112,0},{1... | collective-permute-start | bytes 196616 | tf_op jit(solution)/shard_map/ppermute | solution.py:284
  153.5 9.1 %collective-permute-start.3 = (f32[32,512]{1,0:T(8,128)S(1)}, f32[32,512]{1,0:T(8,128)S(1)}, u32[]{:S(2)}, u32[]{:S(2)}) collective-permute-start(f32[32,512]{1,0:T(8,128)S(1)} %add.23), channel_id=1, source_target_pairs={{0,128},{128,0},{256,384},{384,256},{1,129},{129,1},{257,385},{385... | collective-permute-start | bytes 196616 | tf_op jit(solution)/shard_map/ppermute | solution.py:284
  162.7 6.5 %collective-permute-start.4 = (f32[32,512]{1,0:T(8,128)S(1)}, f32[32,512]{1,0:T(8,128)S(1)}, u32[]{:S(2)}, u32[]{:S(2)}) collective-permute-start(f32[32,512]{1,0:T(8,128)S(1)} %add.24), channel_id=1, source_target_pairs={{0,384},{128,256},{256,128},{384,0},{1,385},{129,257},{257,129},{3... | collective-permute-start | bytes 196616 | tf_op jit(solution)/shard_map/ppermute | solution.py:284
  169.8 8.7 %copy-start = (bf16[256,512]{1,0:T(8,128)(2,1)S(1)}, bf16[256,512]{1,0:T(8,128)(2,1)}, u32[]{:S(2)}) copy-start(bf16[256,512]{1,0:T(8,128)(2,1)} %shard_map.94.select_ref) | copy-start | bytes 786436

commit v3 on v2

--- a/solution.py
+++ b/solution.py
@@ -13,7 +13,8 @@
 HBM = pl.BlockSpec(memory_space=pltpu.HBM)
 VMEM = pl.BlockSpec(memory_space=pltpu.VMEM)
 TILES = 7
-ROOM = 50_000_000
+ROOM = 16_000_000
+FULL = 63_400_000
 LANES = 128
 
 
@@ -34,7 +35,7 @@
     return high, (x - high.astype(f32)).astype(bf16)
 
 
-def call(kernel, outs, args, room=63_400_000, **more):
+def call(kernel, outs, args, room=ROOM, **more):
     return pl.pallas_call(
         kernel,
         out_shape=outs,
@@ -106,81 +107,42 @@
 
 
 def merge_kernel(
-    width,
-    arrived_hbm,
-    weight_0_hbm,
-    weight_1_hbm,
-    error_hbm,
-    seed_ref,
-    grad_pre_ref,
-    merged_hbm,
-    rounded_hbm,
-    factor_ref,
-    arrived_ref,
-    weight_0,
-    weight_1,
-    error,
-    merged,
-    rounded,
-    arrived_sem,
-    weight_sem,
-    error_sem,
-    merged_sem,
-    rounded_sem,
+    width, arrived_ref, weight_0, weight_hbm, error_hbm, seed_ref, grad_pre_ref, merged_ref, factor_ref, weight_1, error, sem
 ):
     rank = seed_ref.shape[1]
     step = width // TILES
     tiles = [slice(i * step, (i + 1) * step) for i in range(TILES)]
-    needs = []
-    for i, rows in enumerate(tiles):
-        needs.append(
-            [
-                pltpu.make_async_copy(arrived_hbm.at[:, rows], arrived_ref.at[:, rows], arrived_sem.at[i]),
-                pltpu.make_async_copy(weight_0_hbm.at[rows], weight_0.at[rows], weight_sem.at[2 * i]),
-                pltpu.make_async_copy(weight_1_hbm.at[rows], weight_1.at[rows], weight_sem.at[2 * i + 1]),
-            ]
-        )
-        for load in needs[i]:
-            load.start()
-    rest = slice(width, arrived_ref.shape[1])
-    grads = pltpu.make_async_copy(arrived_hbm.at[:, rest], arrived_ref.at[:, rest], arrived_sem.at[TILES])
-    grads.start()
+    fetch = pltpu.make_async_copy(weight_hbm, weight_1, sem.at[TILES])
+    fetch.start()
     loads = [
-        pltpu.make_async_copy(error_hbm.at[rows], error.at[rows], error_sem.at[i])
-        for i, rows in enumerate(tiles)
+        pltpu.make_async_copy(error_hbm.at[rows], error.at[rows], sem.at[i]) for i, rows in enumerate(tiles)
     ]
     for load in loads:
         load.start()
-    pre = jnp.zeros(grad_pre_ref.shape, f32)
-    for i, rows in enumerate(tiles):
-        for load in needs[i]:
-            load.wait()
-        weight = jnp.concatenate([weight_0[rows, :], weight_1[rows, :]], axis=1)
-        pre = pre + nn(arrived_ref[:, rows], weight)
-    grads.wait()
-    s = 1.0 / (1.0 + jnp.exp(-pre))
-    grad_pre = (arrived_ref[:, width:].astype(f32) * (s * (1.0 + pre * (1.0 - s)))).astype(bf16)
-    grad_pre_ref[...] = grad_pre
+    x = arrived_ref[:, :width]
+    half = weight_1.shape[1]
+
+    def columns(weight, lanes):
+        pre = nn(x, weight[...])
+        s = 1.0 / (1.0 + jnp.exp(-pre))
+        grad = arrived_ref[:, width + lanes.start : width + lanes.stop].astype(f32)
+        grad_pre_ref[:, lanes] = (grad * (s * (1.0 + pre * (1.0 - s)))).astype(bf16)
+
+    columns(weight_0, slice(0, half))
+    fetch.wait()
+    columns(weight_1, slice(half, 2 * half))
+    grad_pre = grad_pre_ref[...]
     high, low = halves(seed_ref[...])
     both = jnp.concatenate([high, low], axis=1)
-    stores = []
     for i, rows in enumerate(tiles):
         loads[i].wait()
-        total = tn(arrived_ref[:, rows], grad_pre) + error[rows, :].astype(f32)
-        upper, lower = halves(total)
-        merged[rows, :] = total
-        rounded[rows, :] = upper
-        stores.append(pltpu.make_async_copy(merged.at[rows], merged_hbm.at[rows], merged_sem.at[i]))
-        stores.append(pltpu.make_async_copy(rounded.at[rows], rounded_hbm.at[rows], rounded_sem.at[i]))
-        for store in stores[-2:]:
-            store.start()
+        upper, lower = halves(tn(arrived_ref[:, rows], grad_pre) + error[rows, :].astype(f32))
+        merged_ref[rows, :] = upper
         part = nn(upper, both)
         part = part[:, :rank] + part[:, rank:] + nn(lower, high)
         part = part.T
         for j in range(step // LANES):
             factor_ref[:, i * (step // LANES) + j, :] = part[:, j * LANES : (j + 1) * LANES]
-    for store in stores:
-        store.wait()
 
 
 def rows_kernel(grad_pre_ref, weight_0, weight_1, grad_rows_ref):
@@ -194,20 +156,14 @@
     copies_ref[...] = jnp.broadcast_to(total[None], copies_ref.shape)
 
 
-def right_kernel(factor_ref, rounded_hbm, right_ref, rounded, sem):
+def right_kernel(factor_ref, merged_ref, right_ref):
     rank, blocks, _ = factor_ref.shape
     step = 2 * LANES
-    loads = []
-    for i in range(blocks // 2):
-        rows = slice(i * step, (i + 1) * step)
-        loads.append(pltpu.make_async_copy(rounded_hbm.at[rows], rounded.at[rows], sem.at[i]))
-        loads[i].start()
     total = jnp.zeros(right_ref.shape, f32)
     for i in range(blocks // 2):
         pair = jnp.concatenate([factor_ref[:, 2 * i, :], factor_ref[:, 2 * i + 1, :]], axis=1)
         both = jnp.concatenate(halves(pair), axis=0)
-        loads[i].wait()
-        part = nn(both, rounded[i * step : (i + 1) * step, :])
+        part = nn(both, merged_ref[i * step : (i + 1) * step, :])
         total = total + part[:rank] + part[rank:]
     right_ref[...] = total
 
@@ -249,7 +205,7 @@
         upper, lower = halves(left_ref[:, rows])
         low_rank = tn(jnp.concatenate([upper, upper, lower], axis=0), right)
         loads[i].wait()
-        error[rows, :] = (merged[rows, :] - low_rank).astype(bf16)
+        error[rows, :] = (merged[rows, :].astype(f32) - low_rank).astype(bf16)
         stores.append(pltpu.make_async_copy(error.at[rows], error_hbm.at[rows], store_sem.at[i]))
         stores[i].start()
     for store in stores:
@@ -275,14 +231,15 @@
     return jax.ShapeDtypeStruct(dims, dtype)
 
 
-def summed(x, axis):
-    size = lax.axis_size(axis)
-    partners = [1 << k for k in range(size.bit_length() - 1)]
-    if len(partners) > 1:
-        partners[-1] = size - 1
-    for partner in partners:
-        x = x + lax.ppermute(x, axis, [(i, i ^ partner) for i in range(size)])
-    return x
+def partners(size):
+    steps = [1 << k for k in range(size.bit_length() - 1)]
+    if len(steps) > 1:
+        steps[-1] = size - 1
+    return steps
+
+
+def from_partner(x, axis, step):
+    return lax.ppermute(x, axis, [(i, i ^ step) for i in range(lax.axis_size(axis))])
 
 
 def body(tokens, routes, gates, grad_hidden, w_in, error, q_seed):
@@ -300,6 +257,7 @@
         lambda *refs: prepare_kernel(experts, capacity, *refs),
         shape((slots, width + hidden), bf16),
         (routes_t, gates.T, tokens, grad_hidden.reshape(row_count, 2 * hidden)),
+        room=FULL,
         in_specs=[HBM, HBM, HBM, HBM],
         out_specs=HBM,
         scratch_shapes=[
@@ -316,40 +274,29 @@
         sent.reshape(experts, capacity, width + hidden), "expert", 0, 0, tiled=True
     ).reshape(slots, width + hidden)
     weight = lax.all_gather(w_mine, DP[1], tiled=True)
-    half = hidden // 2
-    weight_0 = lax.all_gather(weight[:, :half], DP[0], tiled=True)
-    weight_1 = lax.all_gather(weight[:, half:], DP[0], tiled=True)
     select = call(
         lambda *refs: select_kernel(experts, capacity, *refs),
         shape((2 * row_count, slots), bf16),
         (routes_t,),
     )
+    weight, select = lax.optimization_barrier((weight, select))
+    half = hidden // 2
+    weight_0 = lax.all_gather(weight[:, :half], DP[0], tiled=True)
+    weight_1 = lax.all_gather(weight[:, half:], DP[0], tiled=True)
 
     blocks = width // LANES
-    grad_pre, merged, rounded, factor = call(
+    grad_pre, merged, factor = call(
         lambda *refs: merge_kernel(width, *refs),
         (
             shape((slots, hidden), bf16),
-            shape((width, hidden), f32),
             shape((width, hidden), bf16),
             shape((rank, blocks, LANES), f32),
         ),
         (arrived, weight_0, weight_1, error[0, 0], q_seed[0]),
-        in_specs=[HBM, HBM, HBM, HBM, VMEM],
-        out_specs=[VMEM, HBM, HBM, VMEM],
-        scratch_shapes=[
-            pltpu.VMEM((slots, width + hidden), bf16),
-            pltpu.VMEM((width, half), bf16),
-            pltpu.VMEM((width, half), bf16),
-            pltpu.VMEM((width, hidden), bf16),
-            pltpu.VMEM((width, hidden), f32),
-            pltpu.VMEM((width, hidden), bf16),
-            dma((TILES + 1,)),
-            dma((2 * TILES,)),
-            dma((TILES,)),
-            dma((TILES,)),
-            dma((TILES,)),
-        ],
+        room=ROOM,
+        in_specs=[VMEM, VMEM, HBM, HBM, VMEM],
+        out_specs=[VMEM, VMEM, VMEM],
+        scratch_shapes=[pltpu.VMEM((width, half), bf16), pltpu.VMEM((width, hidden), bf16), dma((TILES + 1,))],
     )
     each = rank // replicas
     parts = lax.all_to_all(factor, DP, 0, 0, tiled=True)
@@ -360,19 +307,12 @@
         (parts.reshape(replicas, each * blocks, LANES),),
     )
     factor = lax.all_to_all(copies, DP, 0, 0, tiled=True).reshape(rank, blocks, LANES)
-    right = call(
-        right_kernel,
-        shape((rank, hidden), f32),
-        (factor, rounded),
-        in_specs=[VMEM, HBM],
-        scratch_shapes=[pltpu.VMEM((width, hidden), bf16), dma((blocks // 2,))],
-    )
+    right = call(right_kernel, shape((rank, hidden), f32), (factor, merged))
     right, grad_rows = lax.optimization_barrier((right, grad_rows))
     returned = lax.all_to_all(
         grad_rows.reshape(experts, capacity, width), "expert", 0, 0, tiled=True
     ).reshape(slots, width)
 
-    right = summed(summed(right, DP[1]), DP[0])
     left = call(
         left_kernel,
         shape((rank, width), f32),
@@ -381,14 +321,23 @@
     )
     shard = width // replicas
     mine = lax.dynamic_slice_in_dim(left, lax.axis_index(DP) * shard, shard, 1)
+    steps = [(axis, step) for axis in DP[::-1] for step in partners(lax.axis_size(axis))]
+    for i, (axis, step) in enumerate(steps):
+        other = from_partner(right, axis, step)
+        if i == len(steps) - 3:
+            other, left = lax.optimization_barrier((other, left))
+        if i == len(steps) - 2:
+            other, mine = lax.optimization_barrier((other, mine))
+        right = right + other
     error_next, weight_grad = call(
         lambda *refs: finish_kernel(replicas, *refs),
         (shape((width, hidden), bf16), shape((shard, hidden), f32)),
         (right, left, mine, merged),
+        room=FULL,
         in_specs=[VMEM, VMEM, VMEM, HBM],
         out_specs=[HBM, VMEM],
         scratch_shapes=[
-            pltpu.VMEM((width, hidden), f32),
+            pltpu.VMEM((width, hidden), bf16),
             pltpu.VMEM((width, hidden), bf16),
             dma((TILES,)),
             dma((TILES,)),
@@ -398,7 +347,6 @@
         combine_kernel,
         shape((row_count, width), bf16),
         (select, gates, returned),
-        room=ROOM,
         in_specs=[VMEM, VMEM, VMEM],
         out_specs=HBM,
         scratch_shapes=[pltpu.VMEM((row_count, width), bf16), dma((TILES,))],

time: 181 us -> 176 us (0.972)
  Pallas kernels: 35.9 us -> 22.3 us
  waiting for transfers between devices: 25.9 us -> 31.5 us
  local copies, waits for them, and re-layouts: 6.24 us -> 10.8 us
    pallas_call x9, Pallas kernels: 35.9 us -> 22.3 us  [call(): pl.pallas_call(kernel, out_shape=outs, compiler_params=pltpu.CompilerPara...]
    unnamed x17 -> x33, local copies, waits for them, and re-layouts: 4.77 us -> 10.1 us
    all_to_all x1, waiting for transfers between devices: 3.59 us -> 7.23 us  [body(): lax.all_to_all(grad_rows.reshape(experts, capacity, width), 'expert', 0,...]
  transfers between devices with their start and end apart: 8 -> 8, of which waited for: 7 -> 8; matrix products, arithmetic and copies ran while one was open for 2% -> 1% of each run, Pallas kernels for 9% -> 6%
where the time goes in v3:
time: 176 us; the launch traced here: 175 us
  blocking collectives  67.8 us (39%)
  starting transfers between devices  41.5 us (24%)
  waiting for transfers between devices  31.5 us (18%)
  Pallas kernels  22.3 us (13%)
  local copies, waits for them, and re-layouts  10.8 us (6%)
    all_gather x1, blocking collectives, body(): weight = lax.all_gather(w_mine, DP[1], tiled=True)  22.6 us
    pallas_call x9, Pallas kernels, call(): pl.pallas_call(kernel, out_shape=outs, compiler_params=pltpu.CompilerPara...  22.3 us
    all_to_all x1, blocking collectives, body(): parts = lax.all_to_all(factor, DP, 0, 0, tiled=True)  19.2 us
    ppermute x5, starting transfers between devices, from_partner(): lax.ppermute(x, axis, [(i, i ^ step) for i in range(lax.axis_size(axis))])  14 us
    all_gather x1, blocking collectives, body(): weight_1 = lax.all_gather(weight[:, half:], DP[0], tiled=True)  13.6 us
    ppermute x5, waiting for transfers between devices, from_partner(): lax.ppermute(x, axis, [(i, i ^ step) for i in range(lax.axis_size(axis))])  12.4 us
    all_gather x1, blocking collectives, body(): weight_0 = lax.all_gather(weight[:, :half], DP[0], tiled=True)  12.3 us
    all_to_all x1, starting transfers between devices, body(): lax.all_to_all(sent.reshape(experts, capacity, width + hidden), 'expert',...  12 us
  transfers between devices with their start and end apart: 8, of which 8 were waited for; matrix products, arithmetic and copies ran while one was open for 1% of the time, Pallas kernels for 6%

profile of v3, /device:TPU:1, one launch (start us, length us, event | category | flops | bytes accessed | tf_op | source)
XLA Modules:
  0.0 175.4 jit_solution(6370562878947044727)
XLA Ops:
  0.6 1.7 copy.12
  2.3 2.9 %shard_map.94 = bf16[512,2304]{1,0:T(8,128)(2,1)} custom-call(s32[2,128]{1,0:T(2,128)} %bitcast.18, f32[2,128]{1,0:T(2,128)} %bitcast.24, bf16[128,1792]{1,0:T(8,128)(2,1)} %refs_2_.1, bf16[128,1024]{1,0:T(8,128)(2,1)} %bitcast.21), custom_call_target="tpu_custom_call" | custom-call | tf_op jit(solution)/shard_map/pallas_call | solution.py:39
  5.3 12.0 %all-to-all-start = ((bf16[16,32,2304]{2,1,0:T(8,128)(2,1)}), bf16[16,32,2304]{2,1,0:T(8,128)(2,1)S(1)}, u32[]{:S(2)}, u32[]{:S(2)}) async-start(bf16[16,32,2304]{2,1,0:T(8,128)(2,1)} %bitcast.20), calls=%async_computation | async-start | bytes 4718592 | tf_op jit(solution)/shard_map/all_to_all | solution.py:273
  18.3 22.6 %all_gather.9 = bf16[448,512]{1,0:T(8,128)(2,1)S(1)} all-gather(bf16[56,512]{1,0:T(8,128)(2,1)S(1)} %bitcast.23), channel_id=1, replica_groups=mesh['dp_0'=4,'dp_1'=8,'expert'=16] {'dp_1'}, dimensions={0}, use_global_device_ids=true | all-gather | bytes 516096 | tf_op jit(solution)/shard_map/all_gather | solution.py:276
  41.1 12.3 %all_gather.10.refs_1_.weight_0 = bf16[1792,256]{1,0:T(8,128)(2,1)S(1)} all-gather(bf16[448,256]{1,0:T(8,128)(2,1)S(1)} %get-tuple-element.34), channel_id=1, replica_groups=mesh['dp_0'=4,'dp_1'=8,'expert'=16] {'dp_0'}, dimensions={0}, use_global_device_ids=true | all-gather | bytes 1146880 | tf_op jit(solution)/shard_map/all_gather | solution.py:284
  53.4 13.6 %all_gather.11.refs_2_.weight_1 = bf16[1792,256]{1,0:T(8,128)(2,1)} all-gather(bf16[448,256]{1,0:T(8,128)(2,1)S(1)} %get-tuple-element.33), channel_id=1, replica_groups=mesh['dp_0'=4,'dp_1'=8,'expert'=16] {'dp_0'}, dimensions={0}, use_global_device_ids=true | all-gather | bytes 1146880 | tf_op jit(solution)/shard_map/all_gather | solution.py:285
  67.0 4.7 %all-to-all-done = bf16[16,32,2304]{2,1,0:T(8,128)(2,1)S(1)} async-done(((bf16[16,32,2304]{2,1,0:T(8,128)(2,1)}), bf16[16,32,2304]{2,1,0:T(8,128)(2,1)S(1)}, u32[]{:S(2)}, u32[]{:S(2)}) %all-to-all-start) | async-done | bytes 2359328 | tf_op jit(solution)/shard_map/all_to_all | solution.py:273
  71.6 1.2 copy-done
  72.8 1.5 copy-done.5
  74.3 7.0 %shard_map.96 = (bf16[512,512]{1,0:T(8,128)(2,1)S(1)}, bf16[1792,512]{1,0:T(8,128)(2,1)S(1)}, f32[32,14,128]{2,1,0:T(8,128)S(1)}) custom-call(bf16[512,2304]{1,0:T(8,128)(2,1)S(1)} %bitcast.13, bf16[1792,256]{1,0:T(8,128)(2,1)S(1)} %all_gather.10.refs_1_.weight_0, bf16[1792,256]{1,0:T(8,128)(2,1)S(1)} %copy-done, bf16[1792,512]{1,0:T(8,128)(2,1)S(1)} %bitcast.16, ...), custom_call_target="tpu_custom_call" | custom-call | tf_op jit(solution)/shard_map/pallas_call | solution.py:39
  81.3 1.2 copy-done.3
  83.3 19.2 %all_to_all.20.parts_ref = f32[32,14,128]{2,1,0:T(8,128)S(1)} all-to-all(f32[32,14,128]{2,1,0:T(8,128)S(1)} %get-tuple-element.22), channel_id=1, replica_groups=mesh['dp_0'=4,'dp_1'=8,'expert'=16] {'dp_0','dp_1'}, dimensions={0} | all-to-all | bytes 458752 | tf_op jit(solution)/shard_map/all_to_all | solution.py:302
  103.3 5.3 %all-to-all-start.2 = ((f32[32,14,128]{2,1,0:T(8,128)}), f32[32,14,128]{2,1,0:T(8,128)S(1)}, u32[]{:S(2)}, u32[]{:S(2)}) async-start(f32[32,14,128]{2,1,0:T(8,128)} %shard_map.97), calls=%async_computation.2 | async-start | bytes 524288 | tf_op jit(solution)/shard_map/all_to_all | solution.py:309
  108.6 1.2 shard_map.99
  109.7 1.2 copy-done.2
  111.0 7.2 %all-to-all-done.2.factor_ref = f32[32,14,128]{2,1,0:T(8,128)S(1)} async-done(((f32[32,14,128]{2,1,0:T(8,128)}), f32[32,14,128]{2,1,0:T(8,128)S(1)}, u32[]{:S(2)}, u32[]{:S(2)}) %all-to-all-start.2) | async-done | bytes 229408 | tf_op jit(solution)/shard_map/all_to_all | solution.py:309
  118.2 1.5 copy-done.4
  120.1 10.3 %all-to-all-start.3 = ((bf16[16,32,1792]{2,1,0:T(8,128)(2,1)}), bf16[16,32,1792]{2,1,0:T(8,128)(2,1)S(1)}, u32[]{:S(2)}, u32[]{:S(2)}) async-start(bf16[16,32,1792]{2,1,0:T(8,128)(2,1)} %bitcast.15), calls=%async_computation.3 | async-start | bytes 3670016 | tf_op jit(solution)/shard_map/all_to_all | solution.py:312
  130.4 3.8 %collective-permute-start = (f32[32,512]{1,0:T(8,128)S(1)}, f32[32,512]{1,0:T(8,128)S(1)}, u32[]{:S(2)}, u32[]{:S(2)}) collective-permute-start(f32[32,512]{1,0:T(8,128)S(1)} %shard_map.98), channel_id=1, source_target_pairs={{0,16},{16,0},{32,48},{48,32},{64,80},{80,64},{96,112},{112,96},{1... | collective-permute-start | bytes 196616 | tf_op jit(solution)/shard_map/ppermute | solution.py:242
  134.2 2.3 %collective-permute-done = f32[32,512]{1,0:T(8,128)S(1)} collective-permute-done((f32[32,512]{1,0:T(8,128)S(1)}, f32[32,512]{1,0:T(8,128)S(1)}, u32[]{:S(2)}, u32[]{:S(2)}) %collective-permute-start) | collective-permute-done | bytes 65568 | tf_op jit(solution)/shard_map/ppermute | solution.py:242
  136.6 3.0 %collective-permute-start.1 = (f32[32,512]{1,0:T(8,128)S(1)}, f32[32,512]{1,0:T(8,128)S(1)}, u32[]{:S(2)}, u32[]{:S(2)}) collective-permute-start(f32[32,512]{1,0:T(8,128)S(1)} %add.21), channel_id=1, source_target_pairs={{0,32},{16,48},{32,0},{48,16},{64,96},{80,112},{96,64},{112,80},{1... | collective-permute-start | bytes 196616 | tf_op jit(solution)/shard_map/ppermute | solution.py:242
  139.6 3.2 %collective-permute-done.1 = f32[32,512]{1,0:T(8,128)S(1)} collective-permute-done((f32[32,512]{1,0:T(8,128)S(1)}, f32[32,512]{1,0:T(8,128)S(1)}, u32[]{:S(2)}, u32[]{:S(2)}) %collective-permute-start.1) | collective-permute-done | bytes 65568 | tf_op jit(solution)/shard_map/ppermute | solution.py:242
  142.8 2.2 %collective-permute-start.2 = (f32[32,512]{1,0:T(8,128)S(1)}, f32[32,512]{1,0:T(8,128)S(1)}, u32[]{:S(2)}, u32[]{:S(2)}) collective-permute-start(f32[32,512]{1,0:T(8,128)S(1)} %add.22), channel_id=1, source_target_pairs={{0,112},{16,96},{32,80},{48,64},{64,48},{80,32},{96,16},{112,0},{1... | collective-permute-start | bytes 196616 | tf_op jit(solution)/shard_map/ppermute | solution.py:242
  145.0 3.4 %shard_map.101.refs_1_ = f32[32,1792]{1,0:T(8,128)S(1)} custom-call(f32[32,14,128]{2,1,0:T(8,128)S(1)} %all-to-all-done.2.factor_ref), custom_call_target="tpu_custom_call" | custom-call | tf_op jit(solution)/shard_map/pallas_call | solution.py:39
  148.4 0.9 collective-permute-done.2
  149.3 2.2 %collective-permute-start.3 = (f32[32,512]{1,0:T(8,128)S(1)}, f32[32,512]{1,0:T(8,128)S(1)}, u32[]{:S(2)}, u32[]{:S(2)}) collective-permute-start(f32[32,512]{1,0:T(8,128)S(1)} %add.23), channel_id=1, source_target_pairs={{0,128},{128,0},{256,384},{384,256},{1,129},{129,1},{257,385},{385... | collective-permute-start | bytes 196616 | tf_op jit(solution)/shard_map/ppermute | solution.py:242
  152.2 2.4 %collective-permute-done.3 = f32[32,512]{1,0:T(8,128)S(1)} collective-permute-done((f32[32,512]{1,0:T(8,128)S(1)}, f32[32,512]{1,0:T(8,128)S(1)}, u32[]{:S(2)}, u32[]{:S(2)}) %collective-permute-start.3) | collective-permute-done | bytes 65568 | tf_op jit(solution)/shard_map/ppermute | solution.py:242
  154.6 2.7 %collective-permute-start.4 = (f32[32,512]{1,0:T(8,128)S(1)}, f32[32,512]{1,0:T(8,128)S(1)}, u32[]{:S(2)}, u32[]{:S(2)}) collective-permute-start(f32[32,512]{1,0:T(8,128)S(1)} %add.26), channel_id=1, source_target_pairs={{0,384},{128,256},{256,128},{384,0},{1,385},{129,257},{257,129},{3... | collective-permute-start | bytes 196616 | tf_op jit(solution)/shard_map/ppermute | solution.py:242
  157.5 3.7 %collective-permute-done.4 = f32[32,512]{1,0:T(8,128)S(1)} collective-permute-done((f32[32,512]{1,0:T(8,128)S(1)}, f32[32,512]{1,0:T(8,128)S(1)}, u32[]{:S(2)}, u32[]{:S(2)}) %collective-permute-start.4) | collective-permute-done | bytes 65568 | tf_op jit(solution)/shard_map/ppermute | solution.py:242
  161.8 5.0 %shard_map.102 = (bf16[1792,512]{1,0:T(8,128)(2,1)}, f32[56,512]{1,0:T(8,128)}) custom-call(f32[32,512]{1,0:T(8,128)} %add.27.refs_0_, f32[32,1792]{1,0:T(8,128)} %copy-done.8, f32[32,56]{1,0:T(8,128)} %constant_dynamic-slice_fusion.refs_2_, bf16[1792,512]{1,0:T(8,128)(2,1)} %copy-done.3), custom_call_target="tpu_custom_call" | custom-call | tf_op jit(solution)/shard_map/pallas_call | solution.py:39
  166.8 7.2 %all-to-all-done.3 = bf16[16,32,1792]{2,1,0:T(8,128)(2,1)S(1)} async-done(((bf16[16,32,1792]{2,1,0:T(8,128)(2,1)}), bf16[16,32,1792]{2,1,0:T(8,128)(2,1)S(1)}, u32[]{:S(2)}, u32[]{:S(2)}) %all-to-all-start.3) | async-done | bytes 1835040 | tf_op jit(solution)/shard_map/all_to_all | solution.py:312
  174.0 1.4 shard_map.100
  (37 shorter events, 4.6 us)
Async XLA Ops:
  5.3 12.0 %copy-start.11 = (s32[128,2]{0,1:T(2,128)S(1)}, s32[128,2]{0,1:T(2,128)}, u32[]{:S(2)}) copy-start(s32[128,2]{0,1:T(2,128)} %param.8) | copy-start | bytes 3076
  5.3 13.0 %copy-start.13 = (bf16[1,56,512]{2,1,0:T(8,128)(2,1)S(1)}, bf16[1,56,512]{2,1,0:T(8,128)(2,1)}, u32[]{:S(2)}) copy-start(bf16[1,56,512]{2,1,0:T(8,128)(2,1)} %param.11) | copy-start | bytes 172036
  5.3 35.6 %copy-start.12 = (f32[1,512,32]{1,2,0:T(8,128)S(1)}, f32[1,512,32]{1,2,0:T(8,128)}, u32[]{:S(2)}) copy-start(f32[1,512,32]{1,2,0:T(8,128)} %param.13) | copy-start | bytes 196612
  5.3 66.3 %all-to-all-start = ((bf16[16,32,2304]{2,1,0:T(8,128)(2,1)}), bf16[16,32,2304]{2,1,0:T(8,128)(2,1)S(1)}, u32[]{:S(2)}, u32[]{:S(2)}) async-start(bf16[16,32,2304]{2,1,0:T(8,128)(2,1)} %bitcast.20), calls=%async_computation | async-start | bytes 4718592 | tf_op jit(solution)/shard_map/all_to_all | solution.py:273
  17.6 0.7 copy-start.6
  71.6 1.2 copy-start
  72.8 1.5 copy-start.5
  81.3 1.2 copy-start.3
  82.5 0.8 copy-start.9
  83.3 25.3 %copy-start.1 = (bf16[1792,256]{1,0:T(8,128)(2,1)S(1)}, bf16[1792,256]{1,0:T(8,128)(2,1)}, u32[]{:S(2)}) copy-start(bf16[1792,256]{1,0:T(8,128)(2,1)} %all_gather.11.refs_2_.weight_1) | copy-start | bytes 2752516
  83.3 25.3 %copy-start.10 = (bf16[512,512]{1,0:T(8,128)(2,1)S(1)}, bf16[512,512]{1,0:T(8,128)(2,1)}, u32[]{:S(2)}) copy-start(bf16[512,512]{1,0:T(8,128)(2,1)} %copy-done.9) | copy-start | bytes 1572868
  103.3 14.9 %all-to-all-start.2 = ((f32[32,14,128]{2,1,0:T(8,128)}), f32[32,14,128]{2,1,0:T(8,128)S(1)}, u32[]{:S(2)}, u32[]{:S(2)}) async-start(f32[32,14,128]{2,1,0:T(8,128)} %shard_map.97), calls=%async_computation.2 | async-start | bytes 524288 | tf_op jit(solution)/shard_map/all_to_all | solution.py:309
  109.7 1.3 copy-start.2
  118.2 1.5 copy-start.4
  120.1 37.2 %copy-start.14 = (f32[128,2]{0,1:T(2,128)S(1)}, f32[128,2]{0,1:T(2,128)}, u32[]{:S(2)}) copy-start(f32[128,2]{0,1:T(2,128)} %param.9) | copy-start | bytes 3076
  120.1 53.9 %all-to-all-start.3 = ((bf16[16,32,1792]{2,1,0:T(8,128)(2,1)}), bf16[16,32,1792]{2,1,0:T(8,128)(2,1)S(1)}, u32[]{:S(2)}, u32[]{:S(2)}) async-start(bf16[16,32,1792]{2,1,0:T(8,128)(2,1)} %bitcast.15), calls=%async_computation.3 | async-start | bytes 3670016 | tf_op jit(solution)/shard_map/all_to_all | solution.py:312
  130.4 43.7 %copy-start.7 = (bf16[256,512]{1,0:T(8,128)(2,1)S(1)}, bf16[256,512]{1,0:T(8,128)(2,1)}, u32[]{:S(2)}) copy-start(bf16[256,512]{1,0:T(8,128)(2,1)} %copy-done.6) | copy-start | bytes 786436
  130.4 6.2 %collective-permute-start = (f32[32,512]{1,0:T(8,128)S(1)}, f32[32,512]{1,0:T(8,128)S(1)}, u32[]{:S(2)}, u32[]{:S(2)}) collective-permute-start(f32[32,512]{1,0:T(8,128)S(1)} %shard_map.98), channel_id=1, source_target_pairs={{0,16},{16,0},{32,48},{48,32},{64,80},{80,64},{96,112},{112,96},{1... | collective-permute-start | bytes 196616 | tf_op jit(solution)/shard_map/ppermute | solution.py:242
  136.6 6.2 %collective-permute-start.1 = (f32[32,512]{1,0:T(8,128)S(1)}, f32[32,512]{1,0:T(8,128)S(1)}, u32[]{:S(2)}, u32[]{:S(2)}) collective-permute-start(f32[32,512]{1,0:T(8,128)S(1)} %add.21), channel_id=1, source_target_pairs={{0,32},{16,48},{32,0},{48,16},{64,96},{80,112},{96,64},{112,80},{1... | collective-permute-start | bytes 196616 | tf_op jit(solution)/shard_map/ppermute | solution.py:242
  142.8 6.5 %collective-permute-start.2 = (f32[32,512]{1,0:T(8,128)S(1)}, f32[32,512]{1,0:T(8,128)S(1)}, u32[]{:S(2)}, u32[]{:S(2)}) collective-permute-start(f32[32,512]{1,0:T(8,128)S(1)} %add.22), channel_id=1, source_target_pairs={{0,112},{16,96},{32,80},{48,64},{64,48},{80,32},{96,16},{112,0},{1... | collective-permute-start | bytes 196616 | tf_op jit(solution)/shard_map/ppermute | solution.py:242
  148.4 13.4 %copy-start.8 = (f32[32,1792]{1,0:T(8,128)}, f32[32,1792]{1,0:T(8,128)S(1)}, u32[]{:S(2)}) copy-start(f32[32,1792]{1,0:T(8,128)S(1)} %shard_map.101.refs_1_) | copy-start | bytes 688132
  149.3 5.3 %collective-permute-start.3 = (f32[32,512]{1,0:T(8,128)S(1)}, f32[32,512]{1,0:T(8,128)S(1)}, u32[]{:S(2)}, u32[]{:S(2)}) collective-permute-start(f32[32,512]{1,0:T(8,128)S(1)} %add.23), channel_id=1, source_target_pairs={{0,128},{128,0},{256,384},{384,256},{1,129},{129,1},{257,385},{385... | collective-permute-start | bytes 196616 | tf_op jit(solution)/shard_map/ppermute | solution.py:242
  154.6 6.5 %collective-permute-start.4 = (f32[32,512]{1,0:T(8,128)S(1)}, f32[32,512]{1,0:T(8,128)S(1)}, u32[]{:S(2)}, u32[]{:S(2)}) collective-permute-start(f32[32,512]{1,0:T(8,128)S(1)} %add.26), channel_id=1, source_target_pairs={{0,384},{128,256},{256,128},{384,0},{1,385},{129,257},{257,129},{3... | collective-permute-start | bytes 196616 | tf_op jit(solution)/shard_map/ppermute | solution.py:242

commit v4 on v3

--- a/solution.py
+++ b/solution.py
@@ -107,18 +107,11 @@
 
 
 def merge_kernel(
-    width, arrived_ref, weight_0, weight_hbm, error_hbm, seed_ref, grad_pre_ref, merged_ref, factor_ref, weight_1, error, sem
+    width, arrived_ref, weight_0, weight_1, error_ref, seed_ref, grad_pre_ref, merged_ref, factor_ref
 ):
     rank = seed_ref.shape[1]
     step = width // TILES
     tiles = [slice(i * step, (i + 1) * step) for i in range(TILES)]
-    fetch = pltpu.make_async_copy(weight_hbm, weight_1, sem.at[TILES])
-    fetch.start()
-    loads = [
-        pltpu.make_async_copy(error_hbm.at[rows], error.at[rows], sem.at[i]) for i, rows in enumerate(tiles)
-    ]
-    for load in loads:
-        load.start()
     x = arrived_ref[:, :width]
     half = weight_1.shape[1]
 
@@ -129,14 +122,12 @@
         grad_pre_ref[:, lanes] = (grad * (s * (1.0 + pre * (1.0 - s)))).astype(bf16)
 
     columns(weight_0, slice(0, half))
-    fetch.wait()
     columns(weight_1, slice(half, 2 * half))
     grad_pre = grad_pre_ref[...]
     high, low = halves(seed_ref[...])
     both = jnp.concatenate([high, low], axis=1)
     for i, rows in enumerate(tiles):
-        loads[i].wait()
-        upper, lower = halves(tn(arrived_ref[:, rows], grad_pre) + error[rows, :].astype(f32))
+        upper, lower = halves(tn(arrived_ref[:, rows], grad_pre) + error_ref[rows, :].astype(f32))
         merged_ref[rows, :] = upper
         part = nn(upper, both)
         part = part[:, :rank] + part[:, rank:] + nn(lower, high)
@@ -182,7 +173,9 @@
         row = both[i : i + 1, :] / both[i : i + 1, i : i + 1]
         both = jnp.where(own == i, row, both - both[:, i : i + 1] * row)
     upper, lower = halves(both[:, rank:])
-    left_ref[...] = nn(upper, high) + nn(upper, low) + nn(lower, high)
+    left = (nn(upper, high) + nn(upper, low) + nn(lower, high)).T
+    upper, lower = halves(left)
+    left_ref[...] = jnp.concatenate([upper, upper, lower], axis=1)
 
 
 def finish_kernel(
@@ -198,12 +191,10 @@
         load.start()
     high, low = halves(total_ref[...] / count)
     right = jnp.concatenate([high, low, high], axis=0)
-    upper, lower = halves(mine_ref[...])
-    weight_ref[...] = tn(jnp.concatenate([upper, upper, lower], axis=0), right)
+    weight_ref[...] = nn(mine_ref[...], right)
     stores = []
     for i, rows in enumerate(tiles):
-        upper, lower = halves(left_ref[:, rows])
-        low_rank = tn(jnp.concatenate([upper, upper, lower], axis=0), right)
+        low_rank = nn(left_ref[rows, :], right)
         loads[i].wait()
         error[rows, :] = (merged[rows, :].astype(f32) - low_rank).astype(bf16)
         stores.append(pltpu.make_async_copy(error.at[rows], error_hbm.at[rows], store_sem.at[i]))
@@ -274,12 +265,6 @@
         sent.reshape(experts, capacity, width + hidden), "expert", 0, 0, tiled=True
     ).reshape(slots, width + hidden)
     weight = lax.all_gather(w_mine, DP[1], tiled=True)
-    select = call(
-        lambda *refs: select_kernel(experts, capacity, *refs),
-        shape((2 * row_count, slots), bf16),
-        (routes_t,),
-    )
-    weight, select = lax.optimization_barrier((weight, select))
     half = hidden // 2
     weight_0 = lax.all_gather(weight[:, :half], DP[0], tiled=True)
     weight_1 = lax.all_gather(weight[:, half:], DP[0], tiled=True)
@@ -293,10 +278,6 @@
             shape((rank, blocks, LANES), f32),
         ),
         (arrived, weight_0, weight_1, error[0, 0], q_seed[0]),
-        room=ROOM,
-        in_specs=[VMEM, VMEM, HBM, HBM, VMEM],
-        out_specs=[VMEM, VMEM, VMEM],
-        scratch_shapes=[pltpu.VMEM((width, half), bf16), pltpu.VMEM((width, hidden), bf16), dma((TILES + 1,))],
     )
     each = rank // replicas
     parts = lax.all_to_all(factor, DP, 0, 0, tiled=True)
@@ -307,23 +288,30 @@
         (parts.reshape(replicas, each * blocks, LANES),),
     )
     factor = lax.all_to_all(copies, DP, 0, 0, tiled=True).reshape(rank, blocks, LANES)
-    right = call(right_kernel, shape((rank, hidden), f32), (factor, merged))
-    right, grad_rows = lax.optimization_barrier((right, grad_rows))
+    factor, grad_rows = lax.optimization_barrier((factor, grad_rows))
     returned = lax.all_to_all(
         grad_rows.reshape(experts, capacity, width), "expert", 0, 0, tiled=True
     ).reshape(slots, width)
 
+    right = call(right_kernel, shape((rank, hidden), f32), (factor, merged))
     left = call(
         left_kernel,
-        shape((rank, width), f32),
+        shape((width, 3 * rank), bf16),
         (factor,),
         scratch_shapes=[pltpu.VMEM((rank, width), f32)],
     )
     shard = width // replicas
-    mine = lax.dynamic_slice_in_dim(left, lax.axis_index(DP) * shard, shard, 1)
+    mine = lax.dynamic_slice_in_dim(left, lax.axis_index(DP) * shard, shard, 0)
+    select = call(
+        lambda *refs: select_kernel(experts, capacity, *refs),
+        shape((2 * row_count, slots), bf16),
+        (routes_t,),
+    )
     steps = [(axis, step) for axis in DP[::-1] for step in partners(lax.axis_size(axis))]
     for i, (axis, step) in enumerate(steps):
         other = from_partner(right, axis, step)
+        if i == len(steps) - 4:
+            other, select = lax.optimization_barrier((other, select))
         if i == len(steps) - 3:
             other, left = lax.optimization_barrier((other, left))
         if i == len(steps) - 2:

time: 176 us -> 171 us (0.972)
  Pallas kernels: 22.3 us -> 20 us
  waiting for transfers between devices: 31.5 us -> 29.7 us
    pallas_call x9, Pallas kernels: 22.3 us -> 20 us  [call(): pl.pallas_call(kernel, out_shape=outs, compiler_params=pltpu.CompilerPara...]
    all_to_all x1, starting transfers between devices: 10.3 us -> 8.28 us  [body(): lax.all_to_all(grad_rows.reshape(experts, capacity, width), 'expert', 0,...]
    unnamed x33 -> x29, local copies, waits for them, and re-layouts: 10.1 us -> 9.39 us
where the time goes in v4:
time: 171 us; the launch traced here: 170 us
  blocking collectives  67.8 us (40%)
  starting transfers between devices  40.8 us (24%)
  waiting for transfers between devices  29.7 us (17%)
  Pallas kernels  20 us (12%)
  local copies, waits for them, and re-layouts  10 us (6%)
    all_gather x1, blocking collectives, body(): weight = lax.all_gather(w_mine, DP[1], tiled=True)  22.6 us
    pallas_call x9, Pallas kernels, call(): pl.pallas_call(kernel, out_shape=outs, compiler_params=pltpu.CompilerPara...  20 us
    all_to_all x1, blocking collectives, body(): parts = lax.all_to_all(factor, DP, 0, 0, tiled=True)  19.3 us
    ppermute x5, starting transfers between devices, from_partner(): lax.ppermute(x, axis, [(i, i ^ step) for i in range(lax.axis_size(axis))])  14.3 us
    all_gather x1, blocking collectives, body(): weight_1 = lax.all_gather(weight[:, half:], DP[0], tiled=True)  13.6 us
    all_gather x1, blocking collectives, body(): weight_0 = lax.all_gather(weight[:, :half], DP[0], tiled=True)  12.3 us
    all_to_all x1, starting transfers between devices, body(): lax.all_to_all(sent.reshape(experts, capacity, width + hidden), 'expert',...  12 us
    ppermute x5, waiting for transfers between devices, from_partner(): lax.ppermute(x, axis, [(i, i ^ step) for i in range(lax.axis_size(axis))])  11 us
  transfers between devices with their start and end apart: 8, of which 8 were waited for; matrix products, arithmetic and copies ran while one was open for 1% of the time, Pallas kernels for 6%

profile of v4, /device:TPU:1, one launch (start us, length us, event | category | flops | bytes accessed | tf_op | source)
XLA Modules:
  0.0 169.9 jit_solution(7393490739824878304)
XLA Ops:
  0.6 1.7 copy.12
  2.3 3.0 %shard_map.94 = bf16[512,2304]{1,0:T(8,128)(2,1)} custom-call(s32[2,128]{1,0:T(2,128)} %bitcast.18, f32[2,128]{1,0:T(2,128)} %bitcast.24, bf16[128,1792]{1,0:T(8,128)(2,1)} %refs_2_.1, bf16[128,1024]{1,0:T(8,128)(2,1)} %bitcast.21), custom_call_target="tpu_custom_call" | custom-call | tf_op jit(solution)/shard_map/pallas_call | solution.py:39
  5.3 12.0 %all-to-all-start = ((bf16[16,32,2304]{2,1,0:T(8,128)(2,1)}), bf16[16,32,2304]{2,1,0:T(8,128)(2,1)S(1)}, u32[]{:S(2)}, u32[]{:S(2)}) async-start(bf16[16,32,2304]{2,1,0:T(8,128)(2,1)} %bitcast.20), calls=%async_computation | async-start | bytes 4718592 | tf_op jit(solution)/shard_map/all_to_all | solution.py:264
  17.4 22.6 %all_gather.9 = bf16[448,512]{1,0:T(8,128)(2,1)S(1)} all-gather(bf16[56,512]{1,0:T(8,128)(2,1)S(1)} %bitcast.23), channel_id=1, replica_groups=mesh['dp_0'=4,'dp_1'=8,'expert'=16] {'dp_1'}, dimensions={0}, use_global_device_ids=true | all-gather | bytes 516096 | tf_op jit(solution)/shard_map/all_gather | solution.py:267
  40.1 12.3 %all_gather.10.refs_1_.weight_0 = bf16[1792,256]{1,0:T(8,128)(2,1)S(1)} all-gather(bf16[448,256]{1,0:T(8,128)(2,1)S(1)} %get-tuple-element.34), channel_id=1, replica_groups=mesh['dp_0'=4,'dp_1'=8,'expert'=16] {'dp_0'}, dimensions={0}, use_global_device_ids=true | all-gather | bytes 1146880 | tf_op jit(solution)/shard_map/all_gather | solution.py:269
  52.4 13.6 %all_gather.11.refs_2_.weight_1 = bf16[1792,256]{1,0:T(8,128)(2,1)} all-gather(bf16[448,256]{1,0:T(8,128)(2,1)S(1)} %get-tuple-element.33), channel_id=1, replica_groups=mesh['dp_0'=4,'dp_1'=8,'expert'=16] {'dp_0'}, dimensions={0}, use_global_device_ids=true | all-gather | bytes 1146880 | tf_op jit(solution)/shard_map/all_gather | solution.py:270
  66.0 5.6 %all-to-all-done = bf16[16,32,2304]{2,1,0:T(8,128)(2,1)S(1)} async-done(((bf16[16,32,2304]{2,1,0:T(8,128)(2,1)}), bf16[16,32,2304]{2,1,0:T(8,128)(2,1)S(1)}, u32[]{:S(2)}, u32[]{:S(2)}) %all-to-all-start) | async-done | bytes 2359328 | tf_op jit(solution)/shard_map/all_to_all | solution.py:264
  71.6 1.2 copy-done
  72.8 1.5 copy-done.6
  74.3 4.2 %shard_map.95 = (bf16[512,512]{1,0:T(8,128)(2,1)S(1)}, bf16[1792,512]{1,0:T(8,128)(2,1)S(1)}, f32[32,14,128]{2,1,0:T(8,128)S(1)}) custom-call(bf16[512,2304]{1,0:T(8,128)(2,1)S(1)} %bitcast.13, bf16[1792,256]{1,0:T(8,128)(2,1)S(1)} %all_gather.10.refs_1_.weight_0, bf16[1792,256]{1,0:T(8,128)(2,1)S(1)} %copy-done, bf16[1792,512]{1,0:T(8,128)(2,1)S(1)} %bitcast.16, ...), custom_call_target="tpu_custom_call" | custom-call | tf_op jit(solution)/shard_map/pallas_call | solution.py:39
  78.6 1.2 copy-done.3
  79.8 0.8 copy-done.7
  80.6 19.3 %all_to_all.20.parts_ref = f32[32,14,128]{2,1,0:T(8,128)S(1)} all-to-all(f32[32,14,128]{2,1,0:T(8,128)S(1)} %get-tuple-element.20), channel_id=1, replica_groups=mesh['dp_0'=4,'dp_1'=8,'expert'=16] {'dp_0','dp_1'}, dimensions={0} | all-to-all | bytes 458752 | tf_op jit(solution)/shard_map/all_to_all | solution.py:283
  100.6 6.3 %all-to-all-start.2 = ((f32[32,14,128]{2,1,0:T(8,128)}), f32[32,14,128]{2,1,0:T(8,128)S(1)}, u32[]{:S(2)}, u32[]{:S(2)}) async-start(f32[32,14,128]{2,1,0:T(8,128)} %shard_map.96), calls=%async_computation.2 | async-start | bytes 524288 | tf_op jit(solution)/shard_map/all_to_all | solution.py:290
  106.9 1.1 shard_map.97
  108.1 1.2 copy-done.2
  109.3 7.2 %all-to-all-done.2.factor_ref = f32[32,14,128]{2,1,0:T(8,128)S(1)} async-done(((f32[32,14,128]{2,1,0:T(8,128)}), f32[32,14,128]{2,1,0:T(8,128)S(1)}, u32[]{:S(2)}, u32[]{:S(2)}) %all-to-all-start.2) | async-done | bytes 229408 | tf_op jit(solution)/shard_map/all_to_all | solution.py:290
  116.6 8.3 %all-to-all-start.3 = ((bf16[16,32,1792]{2,1,0:T(8,128)(2,1)}), bf16[16,32,1792]{2,1,0:T(8,128)(2,1)S(1)}, u32[]{:S(2)}, u32[]{:S(2)}) async-start(bf16[16,32,1792]{2,1,0:T(8,128)(2,1)} %bitcast.15), calls=%async_computation.3 | async-start | bytes 3670016 | tf_op jit(solution)/shard_map/all_to_all | solution.py:292
  124.9 1.5 copy-done.4
  126.8 3.5 %collective-permute-start = (f32[32,512]{1,0:T(8,128)S(1)}, f32[32,512]{1,0:T(8,128)S(1)}, u32[]{:S(2)}, u32[]{:S(2)}) collective-permute-start(f32[32,512]{1,0:T(8,128)S(1)} %shard_map.98), channel_id=1, source_target_pairs={{0,16},{16,0},{32,48},{48,32},{64,80},{80,64},{96,112},{112,96},{1... | collective-permute-start | bytes 196616 | tf_op jit(solution)/shard_map/ppermute | solution.py:233
  130.3 2.3 %collective-permute-done = f32[32,512]{1,0:T(8,128)S(1)} collective-permute-done((f32[32,512]{1,0:T(8,128)S(1)}, f32[32,512]{1,0:T(8,128)S(1)}, u32[]{:S(2)}, u32[]{:S(2)}) %collective-permute-start) | collective-permute-done | bytes 65568 | tf_op jit(solution)/shard_map/ppermute | solution.py:233
  132.6 3.3 %collective-permute-start.1 = (f32[32,512]{1,0:T(8,128)S(1)}, f32[32,512]{1,0:T(8,128)S(1)}, u32[]{:S(2)}, u32[]{:S(2)}) collective-permute-start(f32[32,512]{1,0:T(8,128)S(1)} %add.21), channel_id=1, source_target_pairs={{0,32},{16,48},{32,0},{48,16},{64,96},{80,112},{96,64},{112,80},{1... | collective-permute-start | bytes 196616 | tf_op jit(solution)/shard_map/ppermute | solution.py:233
  136.2 2.6 %collective-permute-done.1 = f32[32,512]{1,0:T(8,128)S(1)} collective-permute-done((f32[32,512]{1,0:T(8,128)S(1)}, f32[32,512]{1,0:T(8,128)S(1)}, u32[]{:S(2)}, u32[]{:S(2)}) %collective-permute-start.1) | collective-permute-done | bytes 65568 | tf_op jit(solution)/shard_map/ppermute | solution.py:233
  138.8 2.3 %collective-permute-start.2 = (f32[32,512]{1,0:T(8,128)S(1)}, f32[32,512]{1,0:T(8,128)S(1)}, u32[]{:S(2)}, u32[]{:S(2)}) collective-permute-start(f32[32,512]{1,0:T(8,128)S(1)} %add.22), channel_id=1, source_target_pairs={{0,112},{16,96},{32,80},{48,64},{64,48},{80,32},{96,16},{112,0},{1... | collective-permute-start | bytes 196616 | tf_op jit(solution)/shard_map/ppermute | solution.py:233
  141.1 4.0 %shard_map.101.refs_1_ = bf16[1792,96]{1,0:T(8,128)(2,1)S(1)} custom-call(f32[32,14,128]{2,1,0:T(8,128)S(1)} %all-to-all-done.2.factor_ref), custom_call_target="tpu_custom_call" | custom-call | tf_op jit(solution)/shard_map/pallas_call | solution.py:39
  145.3 2.3 %collective-permute-start.3 = (f32[32,512]{1,0:T(8,128)S(1)}, f32[32,512]{1,0:T(8,128)S(1)}, u32[]{:S(2)}, u32[]{:S(2)}) collective-permute-start(f32[32,512]{1,0:T(8,128)S(1)} %add.23), channel_id=1, source_target_pairs={{0,128},{128,0},{256,384},{384,256},{1,129},{129,1},{257,385},{385... | collective-permute-start | bytes 196616 | tf_op jit(solution)/shard_map/ppermute | solution.py:233
  148.3 2.4 %collective-permute-done.3 = f32[32,512]{1,0:T(8,128)S(1)} collective-permute-done((f32[32,512]{1,0:T(8,128)S(1)}, f32[32,512]{1,0:T(8,128)S(1)}, u32[]{:S(2)}, u32[]{:S(2)}) %collective-permute-start.3) | collective-permute-done | bytes 65568 | tf_op jit(solution)/shard_map/ppermute | solution.py:233
  150.7 2.9 %collective-permute-start.4 = (f32[32,512]{1,0:T(8,128)S(1)}, f32[32,512]{1,0:T(8,128)S(1)}, u32[]{:S(2)}, u32[]{:S(2)}) collective-permute-start(f32[32,512]{1,0:T(8,128)S(1)} %add.26), channel_id=1, source_target_pairs={{0,384},{128,256},{256,128},{384,0},{1,385},{129,257},{257,129},{3... | collective-permute-start | bytes 196616 | tf_op jit(solution)/shard_map/ppermute | solution.py:233
  153.6 3.5 %collective-permute-done.4 = f32[32,512]{1,0:T(8,128)S(1)} collective-permute-done((f32[32,512]{1,0:T(8,128)S(1)}, f32[32,512]{1,0:T(8,128)S(1)}, u32[]{:S(2)}, u32[]{:S(2)}) %collective-permute-start.4) | collective-permute-done | bytes 65568 | tf_op jit(solution)/shard_map/ppermute | solution.py:233
  157.8 4.8 %shard_map.102 = (bf16[1792,512]{1,0:T(8,128)(2,1)}, f32[56,512]{1,0:T(8,128)}) custom-call(f32[32,512]{1,0:T(8,128)} %add.27.refs_0_, bf16[1792,96]{1,0:T(8,128)(2,1)} %copy-done.5, bf16[56,96]{1,0:T(8,128)(2,1)} %constant_dynamic-slice_fusion.refs_2_, bf16[1792,512]{1,0:T(8,128)(2,1)} %copy-done.3), custom_call_target="tpu_custom_call" | custom-call | tf_op jit(solution)/shard_map/pallas_call | solution.py:39
  162.6 5.9 %all-to-all-done.3 = bf16[16,32,1792]{2,1,0:T(8,128)(2,1)S(1)} async-done(((bf16[16,32,1792]{2,1,0:T(8,128)(2,1)}), bf16[16,32,1792]{2,1,0:T(8,128)(2,1)S(1)}, u32[]{:S(2)}, u32[]{:S(2)}) %all-to-all-start.3) | async-done | bytes 1835040 | tf_op jit(solution)/shard_map/all_to_all | solution.py:292
  168.5 1.4 shard_map.100
  (33 shorter events, 3.2 us)
Async XLA Ops:
  5.3 12.0 %copy-start.10 = (f32[1,512,32]{1,2,0:T(8,128)S(1)}, f32[1,512,32]{1,2,0:T(8,128)}, u32[]{:S(2)}) copy-start(f32[1,512,32]{1,2,0:T(8,128)} %param.13) | copy-start | bytes 196612
  5.3 12.1 %copy-start.11 = (bf16[1,56,512]{2,1,0:T(8,128)(2,1)S(1)}, bf16[1,56,512]{2,1,0:T(8,128)(2,1)}, u32[]{:S(2)}) copy-start(bf16[1,56,512]{2,1,0:T(8,128)(2,1)} %param.11) | copy-start | bytes 172036
  5.3 66.3 %all-to-all-start = ((bf16[16,32,2304]{2,1,0:T(8,128)(2,1)}), bf16[16,32,2304]{2,1,0:T(8,128)(2,1)S(1)}, u32[]{:S(2)}, u32[]{:S(2)}) async-start(bf16[16,32,2304]{2,1,0:T(8,128)(2,1)} %bitcast.20), calls=%async_computation | async-start | bytes 4718592 | tf_op jit(solution)/shard_map/all_to_all | solution.py:264
  71.6 1.2 copy-start
  72.8 1.5 copy-start.6
  78.6 1.2 copy-start.3
  79.8 0.8 copy-start.7
  80.6 26.3 %copy-start.1 = (bf16[1792,256]{1,0:T(8,128)(2,1)S(1)}, bf16[1792,256]{1,0:T(8,128)(2,1)}, u32[]{:S(2)}) copy-start(bf16[1792,256]{1,0:T(8,128)(2,1)} %all_gather.11.refs_2_.weight_1) | copy-start | bytes 2752516
  80.6 26.3 %copy-start.8 = (bf16[512,512]{1,0:T(8,128)(2,1)S(1)}, bf16[512,512]{1,0:T(8,128)(2,1)}, u32[]{:S(2)}) copy-start(bf16[512,512]{1,0:T(8,128)(2,1)} %copy-done.7) | copy-start | bytes 1572868
  100.6 16.0 %all-to-all-start.2 = ((f32[32,14,128]{2,1,0:T(8,128)}), f32[32,14,128]{2,1,0:T(8,128)S(1)}, u32[]{:S(2)}, u32[]{:S(2)}) async-start(f32[32,14,128]{2,1,0:T(8,128)} %shard_map.96), calls=%async_computation.2 | async-start | bytes 524288 | tf_op jit(solution)/shard_map/all_to_all | solution.py:290
  108.1 1.3 copy-start.2
  116.6 51.9 %all-to-all-start.3 = ((bf16[16,32,1792]{2,1,0:T(8,128)(2,1)}), bf16[16,32,1792]{2,1,0:T(8,128)(2,1)S(1)}, u32[]{:S(2)}, u32[]{:S(2)}) async-start(bf16[16,32,1792]{2,1,0:T(8,128)(2,1)} %bitcast.15), calls=%async_computation.3 | async-start | bytes 3670016 | tf_op jit(solution)/shard_map/all_to_all | solution.py:292
  124.8 11.0 %copy-start.9 = (s32[128,2]{0,1:T(2,128)S(1)}, s32[128,2]{0,1:T(2,128)}, u32[]{:S(2)}) copy-start(s32[128,2]{0,1:T(2,128)} %param.8) | copy-start | bytes 3076
  124.9 1.5 copy-start.4
  126.4 27.2 %copy-start.12 = (f32[128,2]{0,1:T(2,128)S(1)}, f32[128,2]{0,1:T(2,128)}, u32[]{:S(2)}) copy-start(f32[128,2]{0,1:T(2,128)} %param.9) | copy-start | bytes 3076
  126.8 5.8 %collective-permute-start = (f32[32,512]{1,0:T(8,128)S(1)}, f32[32,512]{1,0:T(8,128)S(1)}, u32[]{:S(2)}, u32[]{:S(2)}) collective-permute-start(f32[32,512]{1,0:T(8,128)S(1)} %shard_map.98), channel_id=1, source_target_pairs={{0,16},{16,0},{32,48},{48,32},{64,80},{80,64},{96,112},{112,96},{1... | collective-permute-start | bytes 196616 | tf_op jit(solution)/shard_map/ppermute | solution.py:233
  132.6 6.2 %collective-permute-start.1 = (f32[32,512]{1,0:T(8,128)S(1)}, f32[32,512]{1,0:T(8,128)S(1)}, u32[]{:S(2)}, u32[]{:S(2)}) collective-permute-start(f32[32,512]{1,0:T(8,128)S(1)} %add.21), channel_id=1, source_target_pairs={{0,32},{16,48},{32,0},{48,16},{64,96},{80,112},{96,64},{112,80},{1... | collective-permute-start | bytes 196616 | tf_op jit(solution)/shard_map/ppermute | solution.py:233
  138.8 6.5 %collective-permute-start.2 = (f32[32,512]{1,0:T(8,128)S(1)}, f32[32,512]{1,0:T(8,128)S(1)}, u32[]{:S(2)}, u32[]{:S(2)}) collective-permute-start(f32[32,512]{1,0:T(8,128)S(1)} %add.22), channel_id=1, source_target_pairs={{0,112},{16,96},{32,80},{48,64},{64,48},{80,32},{96,16},{112,0},{1... | collective-permute-start | bytes 196616 | tf_op jit(solution)/shard_map/ppermute | solution.py:233
  145.1 12.7 %copy-start.5 = (bf16[1792,96]{1,0:T(8,128)(2,1)}, bf16[1792,96]{1,0:T(8,128)(2,1)S(1)}, u32[]{:S(2)}) copy-start(bf16[1792,96]{1,0:T(8,128)(2,1)S(1)} %shard_map.101.refs_1_) | copy-start | bytes 1032196
  145.3 5.3 %collective-permute-start.3 = (f32[32,512]{1,0:T(8,128)S(1)}, f32[32,512]{1,0:T(8,128)S(1)}, u32[]{:S(2)}, u32[]{:S(2)}) collective-permute-start(f32[32,512]{1,0:T(8,128)S(1)} %add.23), channel_id=1, source_target_pairs={{0,128},{128,0},{256,384},{384,256},{1,129},{129,1},{257,385},{385... | collective-permute-start | bytes 196616 | tf_op jit(solution)/shard_map/ppermute | solution.py:233
  150.7 6.5 %collective-permute-start.4 = (f32[32,512]{1,0:T(8,128)S(1)}, f32[32,512]{1,0:T(8,128)S(1)}, u32[]{:S(2)}, u32[]{:S(2)}) collective-permute-start(f32[32,512]{1,0:T(8,128)S(1)} %add.26), channel_id=1, source_target_pairs={{0,384},{128,256},{256,128},{384,0},{1,385},{129,257},{257,129},{3... | collective-permute-start | bytes 196616 | tf_op jit(solution)/shard_map/ppermute | solution.py:233

commit v5 on v4

--- a/solution.py
+++ b/solution.py
@@ -69,7 +69,7 @@
     experts, capacity, routes_hbm, gates_hbm, tokens_hbm, grad_hbm, sent_hbm, routes, gates, tokens, grad, sent, sem
 ):
     width = tokens.shape[1]
-    hidden = grad.shape[1] // 2
+    hidden = grad.shape[2]
     copies = [
         pltpu.make_async_copy(routes_hbm, routes, sem.at[0]),
         pltpu.make_async_copy(gates_hbm, gates, sem.at[1]),
@@ -83,15 +83,17 @@
     copies[1].wait()
     gate = jnp.sum(first * gates[0:1, :] + second * gates[1:2, :], axis=1, keepdims=True)
     either, first, second = (first + second).astype(bf16), first.astype(bf16), second.astype(bf16)
+    copies[3].wait()
+    pairs = grad[...]
+    grad_0, grad_1 = pairs[:, 0, :], pairs[:, 1, :]
     copies[2].wait()
-    copies[3].wait()
     parts = 4
     step = first.shape[0] // parts
     done = []
     for i in range(parts):
         rows = slice(i * step, (i + 1) * step)
         sent[rows, :width] = (nn(either[rows], tokens[...]) * gate[rows]).astype(bf16)
-        grads = nn(first[rows], grad[:, :hidden]) + nn(second[rows], grad[:, hidden:])
+        grads = nn(first[rows], grad_0) + nn(second[rows], grad_1)
         sent[rows, width:] = grads.astype(bf16)
         copy = pltpu.make_async_copy(sent.at[rows], sent_hbm.at[rows], sem.at[4 + i])
         copy.start()
@@ -106,34 +108,37 @@
         select_ref[k * rows : (k + 1) * rows, :] = places.T.astype(bf16)
 
 
-def merge_kernel(
-    width, arrived_ref, weight_0, weight_1, error_ref, seed_ref, grad_pre_ref, merged_ref, factor_ref
-):
+def seeded_kernel(error_ref, seed_ref, seeded_ref):
     rank = seed_ref.shape[1]
-    step = width // TILES
-    tiles = [slice(i * step, (i + 1) * step) for i in range(TILES)]
+    part = nn(error_ref[...], jnp.concatenate(halves(seed_ref[...]), axis=1))
+    seeded_ref[...] = (part[:, :rank] + part[:, rank:]).T
+
+
+def factor_kernel(width, arrived_ref, weight_0, weight_1, seed_ref, seeded_ref, grad_pre_ref, factor_ref):
+    rank = seed_ref.shape[1]
     x = arrived_ref[:, :width]
-    half = weight_1.shape[1]
-
-    def columns(weight, lanes):
+    start = 0
+    for weight in (weight_0, weight_1):
+        lanes = slice(start, start + weight.shape[1])
         pre = nn(x, weight[...])
         s = 1.0 / (1.0 + jnp.exp(-pre))
         grad = arrived_ref[:, width + lanes.start : width + lanes.stop].astype(f32)
         grad_pre_ref[:, lanes] = (grad * (s * (1.0 + pre * (1.0 - s)))).astype(bf16)
-
-    columns(weight_0, slice(0, half))
-    columns(weight_1, slice(half, 2 * half))
+        start = lanes.stop
+    row = nn(grad_pre_ref[...], jnp.concatenate(halves(seed_ref[...]), axis=1))
+    part = tn(jnp.concatenate(halves(row[:, :rank] + row[:, rank:]), axis=1), x)
+    factor = part[:rank] + part[rank:] + seeded_ref[...]
+    for j in range(width // LANES):
+        factor_ref[:, j, :] = factor[:, j * LANES : (j + 1) * LANES]
+
+
+def merge_kernel(width, arrived_ref, grad_pre_ref, error_ref, merged_ref):
+    step = width // TILES
     grad_pre = grad_pre_ref[...]
-    high, low = halves(seed_ref[...])
-    both = jnp.concatenate([high, low], axis=1)
-    for i, rows in enumerate(tiles):
-        upper, lower = halves(tn(arrived_ref[:, rows], grad_pre) + error_ref[rows, :].astype(f32))
-        merged_ref[rows, :] = upper
-        part = nn(upper, both)
-        part = part[:, :rank] + part[:, rank:] + nn(lower, high)
-        part = part.T
-        for j in range(step // LANES):
-            factor_ref[:, i * (step // LANES) + j, :] = part[:, j * LANES : (j + 1) * LANES]
+    for i in range(TILES):
+        rows = slice(i * step, (i + 1) * step)
+        merged = tn(arrived_ref[:, rows], grad_pre) + error_ref[rows, :].astype(f32)
+        merged_ref[rows, :] = merged.astype(bf16)
 
 
 def rows_kernel(grad_pre_ref, weight_0, weight_1, grad_rows_ref):
@@ -247,7 +252,7 @@
     sent = call(
         lambda *refs: prepare_kernel(experts, capacity, *refs),
         shape((slots, width + hidden), bf16),
-        (routes_t, gates.T, tokens, grad_hidden.reshape(row_count, 2 * hidden)),
+        (routes_t, gates.T, tokens, grad_hidden),
         room=FULL,
         in_specs=[HBM, HBM, HBM, HBM],
         out_specs=HBM,
@@ -255,7 +260,7 @@
             pltpu.VMEM((2, row_count), jnp.int32),
             pltpu.VMEM((2, row_count), f32),
             pltpu.VMEM((row_count, width), bf16),
-            pltpu.VMEM((row_count, 2 * hidden), bf16),
+            pltpu.VMEM((row_count, 2, hidden), bf16),
             pltpu.VMEM((slots, width + hidden), bf16),
             dma((8,)),
         ],
@@ -265,22 +270,23 @@
         sent.reshape(experts, capacity, width + hidden), "expert", 0, 0, tiled=True
     ).reshape(slots, width + hidden)
     weight = lax.all_gather(w_mine, DP[1], tiled=True)
-    half = hidden // 2
-    weight_0 = lax.all_gather(weight[:, :half], DP[0], tiled=True)
-    weight_1 = lax.all_gather(weight[:, half:], DP[0], tiled=True)
+    seeded = call(seeded_kernel, shape((rank, width), f32), (error[0, 0], q_seed[0]))
+    most = 3 * hidden // 4
+    rest, seeded = lax.optimization_barrier((weight[:, most:], seeded))
+    weight_0 = lax.all_gather(weight[:, :most], DP[0], tiled=True)
+    weight_1 = lax.all_gather(rest, DP[0], tiled=True)
 
     blocks = width // LANES
-    grad_pre, merged, factor = call(
-        lambda *refs: merge_kernel(width, *refs),
-        (
-            shape((slots, hidden), bf16),
-            shape((width, hidden), bf16),
-            shape((rank, blocks, LANES), f32),
-        ),
-        (arrived, weight_0, weight_1, error[0, 0], q_seed[0]),
+    grad_pre, factor = call(
+        lambda *refs: factor_kernel(width, *refs),
+        (shape((slots, hidden), bf16), shape((rank, blocks, LANES), f32)),
+        (arrived, weight_0, weight_1, q_seed[0], seeded),
     )
     each = rank // replicas
     parts = lax.all_to_all(factor, DP, 0, 0, tiled=True)
+    merged = call(
+        lambda *refs: merge_kernel(width, *refs), shape((width, hidden), bf16), (arrived, grad_pre, error[0, 0])
+    )
     grad_rows = call(rows_kernel, shape((slots, width), bf16), (grad_pre, weight_0, weight_1))
     copies = call(
         sum_and_copy_kernel,
@@ -288,7 +294,7 @@
         (parts.reshape(replicas, each * blocks, LANES),),
     )
     factor = lax.all_to_all(copies, DP, 0, 0, tiled=True).reshape(rank, blocks, LANES)
-    factor, grad_rows = lax.optimization_barrier((factor, grad_rows))
+    factor, grad_rows, merged = lax.optimization_barrier((factor, grad_rows, merged))
     returned = lax.all_to_all(
         grad_rows.reshape(experts, capacity, width), "expert", 0, 0, tiled=True
     ).reshape(slots, width)

time: 171 us -> 185 us (1.082)
  blocking collectives: 67.8 us -> 51.7 us
  between operations: 0.87 us -> 14.3 us
  waiting for transfers between devices: 29.7 us -> 39.2 us
  Pallas kernels: 20 us -> 23.6 us
  starting transfers between devices: 40.8 us -> 44.2 us
    all_gather x0 -> x1, waiting for transfers between devices: none -> 19.5 us  [body(): weight_0 = lax.all_gather(weight[:, :most], DP[0], tiled=True)]
    all_gather x2 -> x1, blocking collectives: 25.9 us -> 11 us  [body(): weight_1 = lax.all_gather(rest, DP[0], tiled=True)]
    all_to_all x1, waiting for transfers between devices: 5.64 us -> 0.01 us  [body(): lax.all_to_all(sent.reshape(experts, capacity, width + hidden), 'expert',...]
    all_to_all x1, waiting for transfers between devices: 7.23 us -> 1.86 us  [body(): lax.all_to_all(copies, DP, 0, 0, tiled=True).reshape(rank, blocks, LANES)]
    pallas_call x9 -> x11, Pallas kernels: 20 us -> 23.6 us  [call(): pl.pallas_call(kernel, out_shape=outs, compiler_params=pltpu.CompilerPara...]
    all_to_all x1, starting transfers between devices: 8.28 us -> 11.2 us  [body(): lax.all_to_all(grad_rows.reshape(experts, capacity, width), 'expert', 0,...]
    unnamed x29 -> x30, local copies, waits for them, and re-layouts: 9.39 us -> 8.89 us
  transfers between devices with their start and end apart: 8 -> 9, of which waited for: 8 -> 7; matrix products, arithmetic and copies ran while one was open for 1% -> 1% of each run, Pallas kernels for 6% -> 7%
where the time goes in v5:
time: 185 us; the launch traced here: 184 us
  blocking collectives  51.7 us (28%)
  starting transfers between devices  44.2 us (24%)
  waiting for transfers between devices  39.2 us (21%)
  Pallas kernels  23.6 us (13%)
  between operations  14.3 us (8%)
  local copies, waits for them, and re-layouts  10.3 us (6%)
    pallas_call x11, Pallas kernels, call(): pl.pallas_call(kernel, out_shape=outs, compiler_params=pltpu.CompilerPara...  23.6 us
    all_gather x1, blocking collectives, body(): weight = lax.all_gather(w_mine, DP[1], tiled=True)  22.6 us
    all_gather x1, waiting for transfers between devices, body(): weight_0 = lax.all_gather(weight[:, :most], DP[0], tiled=True)  19.5 us
    all_to_all x1, blocking collectives, body(): parts = lax.all_to_all(factor, DP, 0, 0, tiled=True)  18 us
    ppermute x5, starting transfers between devices, from_partner(): lax.ppermute(x, axis, [(i, i ^ step) for i in range(lax.axis_size(axis))])  14.9 us
    all_to_all x1, starting transfers between devices, body(): lax.all_to_all(sent.reshape(experts, capacity, width + hidden), 'expert',...  12 us
    all_to_all x1, starting transfers between devices, body(): lax.all_to_all(grad_rows.reshape(experts, capacity, width), 'expert', 0,...  11.2 us
    all_gather x1, blocking collectives, body(): weight_1 = lax.all_gather(rest, DP[0], tiled=True)  11 us
  transfers between devices with their start and end apart: 9, of which 7 were waited for; matrix products, arithmetic and copies ran while one was open for 1% of the time, Pallas kernels for 7%

profile of v5, /device:TPU:1, one launch (start us, length us, event | category | flops | bytes accessed | tf_op | source)
XLA Modules:
  0.0 184.0 jit_solution(13078686283180307982)
XLA Ops:
  7.2 3.5 %shard_map.94 = bf16[512,2304]{1,0:T(8,128)(2,1)} custom-call(s32[2,128]{1,0:T(2,128)} %bitcast.18, f32[2,128]{1,0:T(2,128)} %bitcast.22, bf16[128,1792]{1,0:T(8,128)(2,1)} %refs_2_.1, bf16[128,2,512]{2,1,0:T(2,128)(2,1)} %refs_3_.1), custom_call_target="tpu_custom_call" | custom-call | tf_op jit(solution)/shard_map/pallas_call | solution.py:39
  10.7 12.0 %all-to-all-start = ((bf16[16,32,2304]{2,1,0:T(8,128)(2,1)}), bf16[16,32,2304]{2,1,0:T(8,128)(2,1)S(1)}, u32[]{:S(2)}, u32[]{:S(2)}) async-start(bf16[16,32,2304]{2,1,0:T(8,128)(2,1)} %bitcast.20), calls=%async_computation | async-start | bytes 4718592 | tf_op jit(solution)/shard_map/all_to_all | solution.py:269
  22.7 22.6 %all_gather.9 = bf16[448,512]{1,0:T(8,128)(2,1)S(1)} all-gather(bf16[56,512]{1,0:T(8,128)(2,1)S(1)} %bitcast.21), channel_id=1, replica_groups=mesh['dp_0'=4,'dp_1'=8,'expert'=16] {'dp_1'}, dimensions={0}, use_global_device_ids=true | all-gather | bytes 516096 | tf_op jit(solution)/shard_map/all_gather | solution.py:272
  46.4 1.5 copy-done.3
  47.9 1.1 shard_map.95.refs_4_
  49.0 11.0 %all_gather.11.refs_2_.weight_1 = bf16[1792,128]{1,0:T(8,128)(2,1)S(1)} all-gather(bf16[448,128]{1,0:T(8,128)(2,1)S(1)} %slice.9), channel_id=1, replica_groups=mesh['dp_0'=4,'dp_1'=8,'expert'=16] {'dp_0'}, dimensions={0}, use_global_device_ids=true | all-gather | bytes 573440 | tf_op jit(solution)/shard_map/all_gather | solution.py:277
  60.0 19.5 %all-gather.2.cloned.1.call-done.refs_1_.weight_0 = bf16[1792,384]{1,0:T(8,128)(2,1)} async-done(((bf16[448,384]{1,0:T(8,128)(2,1)}), bf16[1792,384]{1,0:T(8,128)(2,1)}) %all-gather.2.cloned.1.call-update) | async-done | bytes 1376272 | tf_op jit(solution)/shard_map/all_gather | solution.py:276
  79.5 1.3 copy-done.5
  80.8 3.1 %shard_map.96 = (bf16[512,512]{1,0:T(8,128)(2,1)S(1)}, f32[32,14,128]{2,1,0:T(8,128)S(1)}) custom-call(bf16[512,2304]{1,0:T(8,128)(2,1)S(1)} %bitcast.11, bf16[1792,384]{1,0:T(8,128)(2,1)S(1)} %copy-done.5, bf16[1792,128]{1,0:T(8,128)(2,1)S(1)} %all_gather.11.refs_2_.weight_1, f32[512,32]{1,0:T(8,128)S(1)} %bitcast.17, f32[32,1792]{1,0:T(8,128)S(1)} %shard_map.95.refs_4_), custom_call_target="tpu_custom_call" | custom-call | tf_op jit(solution)/shard_map/pallas_call | solution.py:39
  84.8 18.0 %all_to_all.20.parts_ref = f32[32,14,128]{2,1,0:T(8,128)S(1)} all-to-all(f32[32,14,128]{2,1,0:T(8,128)S(1)} %get-tuple-element.24), channel_id=1, replica_groups=mesh['dp_0'=4,'dp_1'=8,'expert'=16] {'dp_0','dp_1'}, dimensions={0} | all-to-all | bytes 458752 | tf_op jit(solution)/shard_map/all_to_all | solution.py:286
  103.5 6.2 %all-to-all-start.2 = ((f32[32,14,128]{2,1,0:T(8,128)}), f32[32,14,128]{2,1,0:T(8,128)S(1)}, u32[]{:S(2)}, u32[]{:S(2)}) async-start(f32[32,14,128]{2,1,0:T(8,128)} %shard_map.97), calls=%async_computation.2 | async-start | bytes 524288 | tf_op jit(solution)/shard_map/all_to_all | solution.py:296
  109.7 1.5 copy-done.4
  111.2 1.0 copy-done.8
  112.2 1.1 shard_map.99.merged_ref.refs_3_
  113.4 1.2 copy-done
  114.7 1.6 shard_map.98
  116.3 1.2 copy-done.2
  117.5 1.9 %all-to-all-done.2.factor_ref = f32[32,14,128]{2,1,0:T(8,128)S(1)} async-done(((f32[32,14,128]{2,1,0:T(8,128)}), f32[32,14,128]{2,1,0:T(8,128)S(1)}, u32[]{:S(2)}, u32[]{:S(2)}) %all-to-all-start.2) | async-done | bytes 229408 | tf_op jit(solution)/shard_map/all_to_all | solution.py:296
  119.4 11.2 %all-to-all-start.3 = ((bf16[16,32,1792]{2,1,0:T(8,128)(2,1)}), bf16[16,32,1792]{2,1,0:T(8,128)(2,1)}, u32[]{:S(2)}, u32[]{:S(2)}) async-start(bf16[16,32,1792]{2,1,0:T(8,128)(2,1)} %bitcast.13), calls=%async_computation.3 | async-start | bytes 3670016 | tf_op jit(solution)/shard_map/all_to_all | solution.py:298
  131.0 3.3 %collective-permute-start = (f32[32,512]{1,0:T(8,128)S(1)}, f32[32,512]{1,0:T(8,128)S(1)}, u32[]{:S(2)}, u32[]{:S(2)}) collective-permute-start(f32[32,512]{1,0:T(8,128)S(1)} %shard_map.100), channel_id=1, source_target_pairs={{0,16},{16,0},{32,48},{48,32},{64,80},{80,64},{96,112},{112,96},{1... | collective-permute-start | bytes 196616 | tf_op jit(solution)/shard_map/ppermute | solution.py:238
  134.3 2.2 %collective-permute-done = f32[32,512]{1,0:T(8,128)S(1)} collective-permute-done((f32[32,512]{1,0:T(8,128)S(1)}, f32[32,512]{1,0:T(8,128)S(1)}, u32[]{:S(2)}, u32[]{:S(2)}) %collective-permute-start) | collective-permute-done | bytes 65568 | tf_op jit(solution)/shard_map/ppermute | solution.py:238
  136.6 3.7 %collective-permute-start.1 = (f32[32,512]{1,0:T(8,128)S(1)}, f32[32,512]{1,0:T(8,128)S(1)}, u32[]{:S(2)}, u32[]{:S(2)}) collective-permute-start(f32[32,512]{1,0:T(8,128)S(1)} %add.21), channel_id=1, source_target_pairs={{0,32},{16,48},{32,0},{48,16},{64,96},{80,112},{96,64},{112,80},{1... | collective-permute-start | bytes 196616 | tf_op jit(solution)/shard_map/ppermute | solution.py:238
  140.6 2.3 %collective-permute-done.1 = f32[32,512]{1,0:T(8,128)S(1)} collective-permute-done((f32[32,512]{1,0:T(8,128)S(1)}, f32[32,512]{1,0:T(8,128)S(1)}, u32[]{:S(2)}, u32[]{:S(2)}) %collective-permute-start.1) | collective-permute-done | bytes 65568 | tf_op jit(solution)/shard_map/ppermute | solution.py:238
  142.9 2.6 %collective-permute-start.2 = (f32[32,512]{1,0:T(8,128)S(1)}, f32[32,512]{1,0:T(8,128)S(1)}, u32[]{:S(2)}, u32[]{:S(2)}) collective-permute-start(f32[32,512]{1,0:T(8,128)S(1)} %add.22), channel_id=1, source_target_pairs={{0,112},{16,96},{32,80},{48,64},{64,48},{80,32},{96,16},{112,0},{1... | collective-permute-start | bytes 196616 | tf_op jit(solution)/shard_map/ppermute | solution.py:238
  145.4 4.0 %shard_map.103.refs_1_ = bf16[1792,96]{1,0:T(8,128)(2,1)S(1)} custom-call(f32[32,14,128]{2,1,0:T(8,128)S(1)} %all-to-all-done.2.factor_ref), custom_call_target="tpu_custom_call" | custom-call | tf_op jit(solution)/shard_map/pallas_call | solution.py:39
  149.5 2.2 %collective-permute-start.3 = (f32[32,512]{1,0:T(8,128)S(1)}, f32[32,512]{1,0:T(8,128)S(1)}, u32[]{:S(2)}, u32[]{:S(2)}) collective-permute-start(f32[32,512]{1,0:T(8,128)S(1)} %add.23), channel_id=1, source_target_pairs={{0,128},{128,0},{256,384},{384,256},{1,129},{129,1},{257,385},{385... | collective-permute-start | bytes 196616 | tf_op jit(solution)/shard_map/ppermute | solution.py:238
  152.4 2.5 %collective-permute-done.3 = f32[32,512]{1,0:T(8,128)S(1)} collective-permute-done((f32[32,512]{1,0:T(8,128)S(1)}, f32[32,512]{1,0:T(8,128)S(1)}, u32[]{:S(2)}, u32[]{:S(2)}) %collective-permute-start.3) | collective-permute-done | bytes 65568 | tf_op jit(solution)/shard_map/ppermute | solution.py:238
  154.9 3.1 %collective-permute-start.4 = (f32[32,512]{1,0:T(8,128)S(1)}, f32[32,512]{1,0:T(8,128)S(1)}, u32[]{:S(2)}, u32[]{:S(2)}) collective-permute-start(f32[32,512]{1,0:T(8,128)S(1)} %add.26), channel_id=1, source_target_pairs={{0,384},{128,256},{256,128},{384,0},{1,385},{129,257},{257,129},{3... | collective-permute-start | bytes 196616 | tf_op jit(solution)/shard_map/ppermute | solution.py:238
  158.1 3.4 %collective-permute-done.4 = f32[32,512]{1,0:T(8,128)S(1)} collective-permute-done((f32[32,512]{1,0:T(8,128)S(1)}, f32[32,512]{1,0:T(8,128)S(1)}, u32[]{:S(2)}, u32[]{:S(2)}) %collective-permute-start.4) | collective-permute-done | bytes 65568 | tf_op jit(solution)/shard_map/ppermute | solution.py:238
  162.2 4.8 %shard_map.104 = (bf16[1792,512]{1,0:T(8,128)(2,1)}, f32[56,512]{1,0:T(8,128)}) custom-call(f32[32,512]{1,0:T(8,128)} %add.27.refs_0_, bf16[1792,96]{1,0:T(8,128)(2,1)} %copy-done.9, bf16[56,96]{1,0:T(8,128)(2,1)} %constant_dynamic-slice_fusion.refs_2_, bf16[1792,512]{1,0:T(8,128)(2,1)} %copy-done), custom_call_target="tpu_custom_call" | custom-call | tf_op jit(solution)/shard_map/pallas_call | solution.py:39
  167.0 7.3 %all-to-all-done.3 = bf16[16,32,1792]{2,1,0:T(8,128)(2,1)} async-done(((bf16[16,32,1792]{2,1,0:T(8,128)(2,1)}), bf16[16,32,1792]{2,1,0:T(8,128)(2,1)}, u32[]{:S(2)}, u32[]{:S(2)}) %all-to-all-start.3) | async-done | bytes 1835040 | tf_op jit(solution)/shard_map/all_to_all | solution.py:298
  174.3 2.9 %shard_map.102 = bf16[128,1792]{1,0:T(8,128)(2,1)} custom-call(bf16[256,512]{1,0:T(8,128)(2,1)S(1)} %shard_map.101.select_ref, f32[128,2]{1,0:T(8,128)S(1)} %copy.11.gates_ref, bf16[512,1792]{1,0:T(8,128)(2,1)} %bitcast.8.returned_ref), custom_call_target="tpu_custom_call" | custom-call | tf_op jit(solution)/shard_map/pallas_call | solution.py:39
  (39 shorter events, 4.7 us)
Async XLA Ops:
  10.7 12.0 %copy-start.12 = (bf16[1,56,512]{2,1,0:T(8,128)(2,1)S(1)}, bf16[1,56,512]{2,1,0:T(8,128)(2,1)}, u32[]{:S(2)}) copy-start(bf16[1,56,512]{2,1,0:T(8,128)(2,1)} %param.11) | copy-start | bytes 172036
  10.7 35.5 %copy-start.11 = (f32[1,512,32]{1,2,0:T(8,128)S(1)}, f32[1,512,32]{1,2,0:T(8,128)}, u32[]{:S(2)}) copy-start(f32[1,512,32]{1,2,0:T(8,128)} %param.13) | copy-start | bytes 196612
  10.7 68.8 %all-to-all-start = ((bf16[16,32,2304]{2,1,0:T(8,128)(2,1)}), bf16[16,32,2304]{2,1,0:T(8,128)(2,1)S(1)}, u32[]{:S(2)}, u32[]{:S(2)}) async-start(bf16[16,32,2304]{2,1,0:T(8,128)(2,1)} %bitcast.20), calls=%async_computation | async-start | bytes 4718592 | tf_op jit(solution)/shard_map/all_to_all | solution.py:269
  22.7 56.8 %all-gather.2.cloned.1.call-start = ((), (), s32[]{:S(2)}) async-start(), calls=%async_computation.4 | async-start | bytes 1720320 | tf_op jit(solution)/shard_map/all_gather | solution.py:276
  46.3 1.5 copy-start.3
  79.5 1.3 copy-start.5
  84.0 0.8 copy-start.7
  103.5 15.8 %all-to-all-start.2 = ((f32[32,14,128]{2,1,0:T(8,128)}), f32[32,14,128]{2,1,0:T(8,128)S(1)}, u32[]{:S(2)}, u32[]{:S(2)}) async-start(f32[32,14,128]{2,1,0:T(8,128)} %shard_map.97), calls=%async_computation.2 | async-start | bytes 524288 | tf_op jit(solution)/shard_map/all_to_all | solution.py:296
  109.7 1.5 copy-start.4
  111.2 1.0 copy-start.8
  112.2 2.4 %copy-start.6 = (bf16[1792,384]{1,0:T(8,128)(2,1)S(1)}, bf16[1792,384]{1,0:T(8,128)(2,1)}, u32[]{:S(2)}) copy-start(bf16[1792,384]{1,0:T(8,128)(2,1)} %all-gather.2.cloned.1.call-done.refs_1_.weight_0) | copy-start | bytes 4128772
  113.4 1.3 copy-start
  116.3 1.2 copy-start.2
  119.4 11.2 %copy-start.1 = (bf16[1792,512]{1,0:T(8,128)(2,1)S(1)}, bf16[1792,512]{1,0:T(8,128)(2,1)}, u32[]{:S(2)}) copy-start(bf16[1792,512]{1,0:T(8,128)(2,1)} %copy-done) | copy-start | bytes 5505028
  119.4 54.9 %all-to-all-start.3 = ((bf16[16,32,1792]{2,1,0:T(8,128)(2,1)}), bf16[16,32,1792]{2,1,0:T(8,128)(2,1)}, u32[]{:S(2)}, u32[]{:S(2)}) async-start(bf16[16,32,1792]{2,1,0:T(8,128)(2,1)} %bitcast.13), calls=%async_computation.3 | async-start | bytes 3670016 | tf_op jit(solution)/shard_map/all_to_all | solution.py:298
  130.5 9.7 %copy-start.10 = (s32[128,2]{0,1:T(2,128)S(1)}, s32[128,2]{0,1:T(2,128)}, u32[]{:S(2)}) copy-start(s32[128,2]{0,1:T(2,128)} %param.8) | copy-start | bytes 3076
  130.6 27.4 %copy-start.13 = (f32[128,2]{0,1:T(2,128)S(1)}, f32[128,2]{0,1:T(2,128)}, u32[]{:S(2)}) copy-start(f32[128,2]{0,1:T(2,128)} %param.9) | copy-start | bytes 3076
  131.0 5.6 %collective-permute-start = (f32[32,512]{1,0:T(8,128)S(1)}, f32[32,512]{1,0:T(8,128)S(1)}, u32[]{:S(2)}, u32[]{:S(2)}) collective-permute-start(f32[32,512]{1,0:T(8,128)S(1)} %shard_map.100), channel_id=1, source_target_pairs={{0,16},{16,0},{32,48},{48,32},{64,80},{80,64},{96,112},{112,96},{1... | collective-permute-start | bytes 196616 | tf_op jit(solution)/shard_map/ppermute | solution.py:238
  136.6 6.3 %collective-permute-start.1 = (f32[32,512]{1,0:T(8,128)S(1)}, f32[32,512]{1,0:T(8,128)S(1)}, u32[]{:S(2)}, u32[]{:S(2)}) collective-permute-start(f32[32,512]{1,0:T(8,128)S(1)} %add.21), channel_id=1, source_target_pairs={{0,32},{16,48},{32,0},{48,16},{64,96},{80,112},{96,64},{112,80},{1... | collective-permute-start | bytes 196616 | tf_op jit(solution)/shard_map/ppermute | solution.py:238
  142.9 6.6 %collective-permute-start.2 = (f32[32,512]{1,0:T(8,128)S(1)}, f32[32,512]{1,0:T(8,128)S(1)}, u32[]{:S(2)}, u32[]{:S(2)}) collective-permute-start(f32[32,512]{1,0:T(8,128)S(1)} %add.22), channel_id=1, source_target_pairs={{0,112},{16,96},{32,80},{48,64},{64,48},{80,32},{96,16},{112,0},{1... | collective-permute-start | bytes 196616 | tf_op jit(solution)/shard_map/ppermute | solution.py:238
  149.5 12.7 %copy-start.9 = (bf16[1792,96]{1,0:T(8,128)(2,1)}, bf16[1792,96]{1,0:T(8,128)(2,1)S(1)}, u32[]{:S(2)}) copy-start(bf16[1792,96]{1,0:T(8,128)(2,1)S(1)} %shard_map.103.refs_1_) | copy-start | bytes 1032196
  149.5 5.4 %collective-permute-start.3 = (f32[32,512]{1,0:T(8,128)S(1)}, f32[32,512]{1,0:T(8,128)S(1)}, u32[]{:S(2)}, u32[]{:S(2)}) collective-permute-start(f32[32,512]{1,0:T(8,128)S(1)} %add.23), channel_id=1, source_target_pairs={{0,128},{128,0},{256,384},{384,256},{1,129},{129,1},{257,385},{385... | collective-permute-start | bytes 196616 | tf_op jit(solution)/shard_map/ppermute | solution.py:238
  154.9 6.6 %collective-permute-start.4 = (f32[32,512]{1,0:T(8,128)S(1)}, f32[32,512]{1,0:T(8,128)S(1)}, u32[]{:S(2)}, u32[]{:S(2)}) collective-permute-start(f32[32,512]{1,0:T(8,128)S(1)} %add.26), channel_id=1, source_target_pairs={{0,384},{128,256},{256,128},{384,0},{1,385},{129,257},{257,129},{3... | collective-permute-start | bytes 196616 | tf_op jit(solution)/shard_map/ppermute | solution.py:238
Sparse Core Ops, SparseCore 0:
  46.3 33.1 all-gather.1

commit v6 on v5

--- a/solution.py
+++ b/solution.py
@@ -108,43 +108,79 @@
         select_ref[k * rows : (k + 1) * rows, :] = places.T.astype(bf16)
 
 
-def seeded_kernel(error_ref, seed_ref, seeded_ref):
+def factor_kernel(
+    width, arrived_ref, weight_0, weight_hbm, error_hbm, seed_ref, grad_pre_hbm, factor_ref, weight_1, error, grad_pre, sem
+):
     rank = seed_ref.shape[1]
-    part = nn(error_ref[...], jnp.concatenate(halves(seed_ref[...]), axis=1))
-    seeded_ref[...] = (part[:, :rank] + part[:, rank:]).T
-
-
-def factor_kernel(width, arrived_ref, weight_0, weight_1, seed_ref, seeded_ref, grad_pre_ref, factor_ref):
-    rank = seed_ref.shape[1]
+    step = width // TILES
+    tiles = [slice(i * step, (i + 1) * step) for i in range(TILES)]
+    fetch = pltpu.make_async_copy(weight_hbm, weight_1, sem.at[TILES])
+    fetch.start()
+    loads = [
+        pltpu.make_async_copy(error_hbm.at[rows], error.at[rows], sem.at[i]) for i, rows in enumerate(tiles)
+    ]
+    for load in loads:
+        load.start()
     x = arrived_ref[:, :width]
     start = 0
     for weight in (weight_0, weight_1):
+        if start:
+            fetch.wait()
         lanes = slice(start, start + weight.shape[1])
         pre = nn(x, weight[...])
         s = 1.0 / (1.0 + jnp.exp(-pre))
         grad = arrived_ref[:, width + lanes.start : width + lanes.stop].astype(f32)
-        grad_pre_ref[:, lanes] = (grad * (s * (1.0 + pre * (1.0 - s)))).astype(bf16)
+        grad_pre[:, lanes] = (grad * (s * (1.0 + pre * (1.0 - s)))).astype(bf16)
         start = lanes.stop
-    row = nn(grad_pre_ref[...], jnp.concatenate(halves(seed_ref[...]), axis=1))
+    store = pltpu.make_async_copy(grad_pre, grad_pre_hbm, sem.at[TILES + 1])
+    store.start()
+    seed = jnp.concatenate(halves(seed_ref[...]), axis=1)
+    row = nn(grad_pre[...], seed)
     part = tn(jnp.concatenate(halves(row[:, :rank] + row[:, rank:]), axis=1), x)
-    factor = part[:rank] + part[rank:] + seeded_ref[...]
-    for j in range(width // LANES):
-        factor_ref[:, j, :] = factor[:, j * LANES : (j + 1) * LANES]
-
-
-def merge_kernel(width, arrived_ref, grad_pre_ref, error_ref, merged_ref):
+    factor = part[:rank] + part[rank:]
+    for i, rows in enumerate(tiles):
+        loads[i].wait()
+        seeded = nn(error[rows, :], seed)
+        total = factor[:, rows] + (seeded[:, :rank] + seeded[:, rank:]).T
+        for j in range(step // LANES):
+            factor_ref[:, i * (step // LANES) + j, :] = total[:, j * LANES : (j + 1) * LANES]
+    store.wait()
+
+
+def merge_kernel(width, arrived_ref, grad_pre_ref, error_hbm, merged_hbm, error, merged, load_sem, store_sem):
     step = width // TILES
+    tiles = [slice(i * step, (i + 1) * step) for i in range(TILES)]
+    loads = [
+        pltpu.make_async_copy(error_hbm.at[rows], error.at[rows], load_sem.at[i])
+        for i, rows in enumerate(tiles)
+    ]
+    for load in loads:
+        load.start()
     grad_pre = grad_pre_ref[...]
-    for i in range(TILES):
+    stores = []
+    for i, rows in enumerate(tiles):
+        product = tn(arrived_ref[:, rows], grad_pre)
+        loads[i].wait()
+        merged[rows, :] = (product + error[rows, :].astype(f32)).astype(bf16)
+        stores.append(pltpu.make_async_copy(merged.at[rows], merged_hbm.at[rows], store_sem.at[i]))
+        stores[i].start()
+    for store in stores:
+        store.wait()
+
+
+def rows_kernel(grad_pre_ref, weight_0, weight_1, grad_rows_hbm, grad_rows, sem):
+    half = weight_0.shape[1]
+    parts = sem.shape[0]
+    step = grad_rows.shape[0] // parts
+    stores = []
+    for i in range(parts):
         rows = slice(i * step, (i + 1) * step)
-        merged = tn(arrived_ref[:, rows], grad_pre) + error_ref[rows, :].astype(f32)
-        merged_ref[rows, :] = merged.astype(bf16)
-
-
-def rows_kernel(grad_pre_ref, weight_0, weight_1, grad_rows_ref):
-    half = weight_0.shape[1]
-    rows = nt(grad_pre_ref[:, :half], weight_0[...]) + nt(grad_pre_ref[:, half:], weight_1[...])
-    grad_rows_ref[...] = rows.astype(bf16)
+        part = nt(grad_pre_ref[rows, :half], weight_0[...]) + nt(grad_pre_ref[rows, half:], weight_1[...])
+        grad_rows[rows, :] = part.astype(bf16)
+        stores.append(pltpu.make_async_copy(grad_rows.at[rows], grad_rows_hbm.at[rows], sem.at[i]))
+        stores[i].start()
+    for store in stores:
+        store.wait()
 
 
 def sum_and_copy_kernel(parts_ref, copies_ref):
@@ -152,14 +188,20 @@
     copies_ref[...] = jnp.broadcast_to(total[None], copies_ref.shape)
 
 
-def right_kernel(factor_ref, merged_ref, right_ref):
-    rank, blocks, _ = factor_ref.shape
+def right_kernel(factor_ref, merged_hbm, right_ref, merged, sem):
+    rank = factor_ref.shape[0]
     step = 2 * LANES
+    loads = []
+    for i in range(sem.shape[0]):
+        rows = slice(i * step, (i + 1) * step)
+        loads.append(pltpu.make_async_copy(merged_hbm.at[rows], merged.at[rows], sem.at[i]))
+        loads[i].start()
     total = jnp.zeros(right_ref.shape, f32)
-    for i in range(blocks // 2):
+    for i, load in enumerate(loads):
         pair = jnp.concatenate([factor_ref[:, 2 * i, :], factor_ref[:, 2 * i + 1, :]], axis=1)
         both = jnp.concatenate(halves(pair), axis=0)
-        part = nn(both, merged_ref[i * step : (i + 1) * step, :])
+        load.wait()
+        part = nn(both, merged[i * step : (i + 1) * step, :])
         total = total + part[:rank] + part[rank:]
     right_ref[...] = total
 
@@ -223,6 +265,10 @@
         store.wait()
 
 
+def in_hbm(x):
+    return pltpu.with_memory_space_constraint(x, pltpu.HBM)
+
+
 def shape(dims, dtype):
     return jax.ShapeDtypeStruct(dims, dtype)
 
@@ -270,24 +316,48 @@
         sent.reshape(experts, capacity, width + hidden), "expert", 0, 0, tiled=True
     ).reshape(slots, width + hidden)
     weight = lax.all_gather(w_mine, DP[1], tiled=True)
-    seeded = call(seeded_kernel, shape((rank, width), f32), (error[0, 0], q_seed[0]))
-    most = 3 * hidden // 4
-    rest, seeded = lax.optimization_barrier((weight[:, most:], seeded))
-    weight_0 = lax.all_gather(weight[:, :most], DP[0], tiled=True)
-    weight_1 = lax.all_gather(rest, DP[0], tiled=True)
+    half = hidden // 2
+    weight_0 = lax.all_gather(weight[:, :half], DP[0], tiled=True)
+    weight_1 = lax.all_gather(weight[:, half:], DP[0], tiled=True)
 
     blocks = width // LANES
+    stored = in_hbm(error[0, 0])
     grad_pre, factor = call(
         lambda *refs: factor_kernel(width, *refs),
-        (shape((slots, hidden), bf16), shape((rank, blocks, LANES), f32)),
-        (arrived, weight_0, weight_1, q_seed[0], seeded),
+        (pltpu.HBM((slots, hidden), bf16), shape((rank, blocks, LANES), f32)),
+        (arrived, weight_0, in_hbm(weight_1), stored, q_seed[0]),
+        in_specs=[VMEM, VMEM, HBM, HBM, VMEM],
+        out_specs=[HBM, VMEM],
+        scratch_shapes=[
+            pltpu.VMEM((width, half), bf16),
+            pltpu.VMEM((width, hidden), bf16),
+            pltpu.VMEM((slots, hidden), bf16),
+            dma((TILES + 2,)),
+        ],
     )
     each = rank // replicas
     parts = lax.all_to_all(factor, DP, 0, 0, tiled=True)
     merged = call(
-        lambda *refs: merge_kernel(width, *refs), shape((width, hidden), bf16), (arrived, grad_pre, error[0, 0])
-    )
-    grad_rows = call(rows_kernel, shape((slots, width), bf16), (grad_pre, weight_0, weight_1))
+        lambda *refs: merge_kernel(width, *refs),
+        pltpu.HBM((width, hidden), bf16),
+        (arrived, grad_pre, stored),
+        in_specs=[VMEM, VMEM, HBM],
+        out_specs=HBM,
+        scratch_shapes=[
+            pltpu.VMEM((width, hidden), bf16),
+            pltpu.VMEM((width, hidden), bf16),
+            dma((TILES,)),
+            dma((TILES,)),
+        ],
+    )
+    grad_rows = call(
+        rows_kernel,
+        pltpu.HBM((slots, width), bf16),
+        (grad_pre, weight_0, weight_1),
+        in_specs=[VMEM, VMEM, VMEM],
+        out_specs=HBM,
+        scratch_shapes=[pltpu.VMEM((slots, width), bf16), dma((2,))],
+    )
     copies = call(
         sum_and_copy_kernel,
         shape((replicas, each * blocks, LANES), f32),
@@ -299,7 +369,14 @@
         grad_rows.reshape(experts, capacity, width), "expert", 0, 0, tiled=True
     ).reshape(slots, width)
 
-    right = call(right_kernel, shape((rank, hidden), f32), (factor, merged))
+    merged = in_hbm(merged)
+    right = call(
+        right_kernel,
+        shape((rank, hidden), f32),
+        (factor, merged),
+        in_specs=[VMEM, HBM],
+        scratch_shapes=[pltpu.VMEM((width, hidden), bf16), dma((blocks // 2,))],
+    )
     left = call(
         left_kernel,
         shape((width, 3 * rank), bf16),

time: 185 us -> 166 us (0.90)
  waiting for transfers between devices: 39.2 us -> 23 us
  blocking collectives: 51.7 us -> 67.7 us
  between operations: 14.3 us -> 0.86 us
  local copies, waits for them, and re-layouts: 10.3 us -> 3.81 us
  Pallas kernels: 23.6 us -> 27.5 us
  starting transfers between devices: 44.2 us -> 41.8 us
    all_gather x1 -> x0, waiting for transfers between devices: 19.5 us -> none  [body(): weight_0 = lax.all_gather(weight[:, :most], DP[0], tiled=True)]
    all_gather x1 -> x2, blocking collectives: 11 us -> 25.9 us  [the longest x1 13.6 us: body(): weight_1 = lax.all_gather(weight[:, half:], DP[0], tiled=True)]
    unnamed x30 -> x18, local copies, waits for them, and re-layouts: 8.89 us -> 3.17 us
    all_to_all x1, waiting for transfers between devices: 0.01 us -> 5.64 us  [body(): lax.all_to_all(sent.reshape(experts, capacity, width + hidden), 'expert',...]
    pallas_call x11 -> x10, Pallas kernels: 23.6 us -> 27.5 us  [call(): pl.pallas_call(kernel, out_shape=outs, compiler_params=pltpu.CompilerPara...]
    all_to_all x1, starting transfers between devices: 11.2 us -> 8.29 us  [body(): lax.all_to_all(grad_rows.reshape(experts, capacity, width), 'expert', 0,...]
  transfers between devices with their start and end apart: 9 -> 8, of which waited for: 7 -> 8; matrix products, arithmetic and copies ran while one was open for 1% -> 1% of each run, Pallas kernels for 7% -> 10%
where the time goes in v6:
time: 166 us; the launch traced here: 165 us
  blocking collectives  67.7 us (41%)
  starting transfers between devices  41.8 us (25%)
  Pallas kernels  27.5 us (17%)
  waiting for transfers between devices  23 us (14%)
  local copies, waits for them, and re-layouts  3.81 us (2%)
    pallas_call x10, Pallas kernels, call(): pl.pallas_call(kernel, out_shape=outs, compiler_params=pltpu.CompilerPara...  27.5 us
    all_gather x1, blocking collectives, body(): weight = lax.all_gather(w_mine, DP[1], tiled=True)  22.6 us
    all_to_all x1, blocking collectives, body(): parts = lax.all_to_all(factor, DP, 0, 0, tiled=True)  19.2 us
    ppermute x5, starting transfers between devices, from_partner(): lax.ppermute(x, axis, [(i, i ^ step) for i in range(lax.axis_size(axis))])  15.2 us
    all_gather x1, blocking collectives, body(): weight_1 = lax.all_gather(weight[:, half:], DP[0], tiled=True)  13.6 us
    all_gather x1, blocking collectives, body(): weight_0 = lax.all_gather(weight[:, :half], DP[0], tiled=True)  12.3 us
    all_to_all x1, starting transfers between devices, body(): lax.all_to_all(sent.reshape(experts, capacity, width + hidden), 'expert',...  12 us
    ppermute x5, waiting for transfers between devices, from_partner(): lax.ppermute(x, axis, [(i, i ^ step) for i in range(lax.axis_size(axis))])  10.1 us
  transfers between devices with their start and end apart: 8, of which 8 were waited for; matrix products, arithmetic and copies ran while one was open for 1% of the time, Pallas kernels for 10%

profile of v6, /device:TPU:1, one launch (start us, length us, event | category | flops | bytes accessed | tf_op | source)
XLA Modules:
  0.0 165.3 jit_solution(1573069202098311914)
XLA Ops:
  0.6 3.6 %shard_map.94 = bf16[512,2304]{1,0:T(8,128)(2,1)} custom-call(s32[2,128]{1,0:T(2,128)} %bitcast.15, f32[2,128]{1,0:T(2,128)} %bitcast.22, bf16[128,1792]{1,0:T(8,128)(2,1)} %refs_2_.1, bf16[128,2,512]{2,1,0:T(2,128)(2,1)} %refs_3_.1), custom_call_target="tpu_custom_call" | custom-call | tf_op jit(solution)/shard_map/pallas_call | solution.py:39
  4.2 12.0 %all-to-all-start = ((bf16[16,32,2304]{2,1,0:T(8,128)(2,1)}), bf16[16,32,2304]{2,1,0:T(8,128)(2,1)S(1)}, u32[]{:S(2)}, u32[]{:S(2)}) async-start(bf16[16,32,2304]{2,1,0:T(8,128)(2,1)} %bitcast.17), calls=%async_computation | async-start | bytes 4718592 | tf_op jit(solution)/shard_map/all_to_all | solution.py:315
  16.3 22.6 %all_gather.9 = bf16[448,512]{1,0:T(8,128)(2,1)S(1)} all-gather(bf16[56,512]{1,0:T(8,128)(2,1)S(1)} %bitcast.21), channel_id=1, replica_groups=mesh['dp_0'=4,'dp_1'=8,'expert'=16] {'dp_1'}, dimensions={0}, use_global_device_ids=true | all-gather | bytes 516096 | tf_op jit(solution)/shard_map/all_gather | solution.py:318
  39.0 12.3 %all_gather.10.refs_1_.weight_0 = bf16[1792,256]{1,0:T(8,128)(2,1)S(1)} all-gather(bf16[448,256]{1,0:T(8,128)(2,1)S(1)} %get-tuple-element.34), channel_id=1, replica_groups=mesh['dp_0'=4,'dp_1'=8,'expert'=16] {'dp_0'}, dimensions={0}, use_global_device_ids=true | all-gather | bytes 1146880 | tf_op jit(solution)/shard_map/all_gather | solution.py:320
  51.3 13.6 %all_gather.11.refs_2_.weight_1 = bf16[1792,256]{1,0:T(8,128)(2,1)} all-gather(bf16[448,256]{1,0:T(8,128)(2,1)S(1)} %get-tuple-element.33), channel_id=1, replica_groups=mesh['dp_0'=4,'dp_1'=8,'expert'=16] {'dp_0'}, dimensions={0}, use_global_device_ids=true | all-gather | bytes 1146880 | tf_op jit(solution)/shard_map/all_gather | solution.py:321
  64.9 5.6 %all-to-all-done = bf16[16,32,2304]{2,1,0:T(8,128)(2,1)S(1)} async-done(((bf16[16,32,2304]{2,1,0:T(8,128)(2,1)}), bf16[16,32,2304]{2,1,0:T(8,128)(2,1)S(1)}, u32[]{:S(2)}, u32[]{:S(2)}) %all-to-all-start) | async-done | bytes 2359328 | tf_op jit(solution)/shard_map/all_to_all | solution.py:315
  70.6 5.6 %shard_map.95 = (bf16[512,512]{1,0:T(8,128)(2,1)}, f32[32,14,128]{2,1,0:T(8,128)S(1)}) custom-call(bf16[512,2304]{1,0:T(8,128)(2,1)S(1)} %bitcast.11, bf16[1792,256]{1,0:T(8,128)(2,1)S(1)} %all_gather.10.refs_1_.weight_0, bf16[1792,256]{1,0:T(8,128)(2,1)} %all_gather.11.refs_2_.weight_1, bf16[1792,512]{1,0:T(8,128)(2,1)} %bitcast.19, f32[512,32]{1,0:T(8,128)S(1)} %bitcast.14), custom_call_target="tpu_custom_call" | custom-call | tf_op jit(solution)/shard_map/pallas_call | solution.py:39
  76.1 19.2 %all_to_all.20.parts_ref = f32[32,14,128]{2,1,0:T(8,128)S(1)} all-to-all(f32[32,14,128]{2,1,0:T(8,128)S(1)} %get-tuple-element.20), channel_id=1, replica_groups=mesh['dp_0'=4,'dp_1'=8,'expert'=16] {'dp_0','dp_1'}, dimensions={0} | all-to-all | bytes 458752 | tf_op jit(solution)/shard_map/all_to_all | solution.py:339
  95.3 0.7 copy-done.3
  96.0 6.3 %all-to-all-start.2 = ((f32[32,14,128]{2,1,0:T(8,128)}), f32[32,14,128]{2,1,0:T(8,128)S(1)}, u32[]{:S(2)}, u32[]{:S(2)}) async-start(f32[32,14,128]{2,1,0:T(8,128)} %copy-done.3), calls=%async_computation.2 | async-start | bytes 524288 | tf_op jit(solution)/shard_map/all_to_all | solution.py:366
  102.3 1.2 copy-done
  103.5 1.0 copy-done.1
  104.5 2.1 %shard_map.97 = bf16[512,1792]{1,0:T(8,128)(2,1)} custom-call(bf16[512,512]{1,0:T(8,128)(2,1)S(1)} %copy-done.1, bf16[1792,256]{1,0:T(8,128)(2,1)S(1)} %all_gather.10.refs_1_.weight_0, bf16[1792,256]{1,0:T(8,128)(2,1)S(1)} %copy-done), custom_call_target="tpu_custom_call" | custom-call | tf_op jit(solution)/shard_map/pallas_call | solution.py:39
  106.7 4.0 %shard_map.98.merged_hbm.refs_3_ = bf16[1792,512]{1,0:T(8,128)(2,1)} custom-call(bf16[512,2304]{1,0:T(8,128)(2,1)S(1)} %bitcast.12, bf16[512,512]{1,0:T(8,128)(2,1)S(1)} %copy-done.1, bf16[1792,512]{1,0:T(8,128)(2,1)} %bitcast.20), custom_call_target="tpu_custom_call" | custom-call | tf_op jit(solution)/shard_map/pallas_call | solution.py:39
  110.8 1.2 all-to-all-done.2.factor_ref
  112.0 8.3 %all-to-all-start.3 = ((bf16[16,32,1792]{2,1,0:T(8,128)(2,1)}), bf16[16,32,1792]{2,1,0:T(8,128)(2,1)S(1)}, u32[]{:S(2)}, u32[]{:S(2)}) async-start(bf16[16,32,1792]{2,1,0:T(8,128)(2,1)} %bitcast.18), calls=%async_computation.3 | async-start | bytes 3670016 | tf_op jit(solution)/shard_map/all_to_all | solution.py:368
  120.3 1.7 %shard_map.99 = f32[32,512]{1,0:T(8,128)S(1)} custom-call(f32[32,14,128]{2,1,0:T(8,128)S(1)} %all-to-all-done.2.factor_ref, bf16[1792,512]{1,0:T(8,128)(2,1)} %shard_map.98.merged_hbm.refs_3_), custom_call_target="tpu_custom_call" | custom-call | tf_op jit(solution)/shard_map/pallas_call | solution.py:39
  122.0 3.5 %collective-permute-start = (f32[32,512]{1,0:T(8,128)S(1)}, f32[32,512]{1,0:T(8,128)S(1)}, u32[]{:S(2)}, u32[]{:S(2)}) collective-permute-start(f32[32,512]{1,0:T(8,128)S(1)} %shard_map.99), channel_id=1, source_target_pairs={{0,16},{16,0},{32,48},{48,32},{64,80},{80,64},{96,112},{112,96},{1... | collective-permute-start | bytes 196616 | tf_op jit(solution)/shard_map/ppermute | solution.py:284
  125.5 2.3 %collective-permute-done = f32[32,512]{1,0:T(8,128)S(1)} collective-permute-done((f32[32,512]{1,0:T(8,128)S(1)}, f32[32,512]{1,0:T(8,128)S(1)}, u32[]{:S(2)}, u32[]{:S(2)}) %collective-permute-start) | collective-permute-done | bytes 65568 | tf_op jit(solution)/shard_map/ppermute | solution.py:284
  127.8 3.2 %collective-permute-start.1 = (f32[32,512]{1,0:T(8,128)S(1)}, f32[32,512]{1,0:T(8,128)S(1)}, u32[]{:S(2)}, u32[]{:S(2)}) collective-permute-start(f32[32,512]{1,0:T(8,128)S(1)} %add.21), channel_id=1, source_target_pairs={{0,32},{16,48},{32,0},{48,16},{64,96},{80,112},{96,64},{112,80},{1... | collective-permute-start | bytes 196616 | tf_op jit(solution)/shard_map/ppermute | solution.py:284
  131.3 2.7 %collective-permute-done.1 = f32[32,512]{1,0:T(8,128)S(1)} collective-permute-done((f32[32,512]{1,0:T(8,128)S(1)}, f32[32,512]{1,0:T(8,128)S(1)}, u32[]{:S(2)}, u32[]{:S(2)}) %collective-permute-start.1) | collective-permute-done | bytes 65568 | tf_op jit(solution)/shard_map/ppermute | solution.py:284
  134.1 2.2 %collective-permute-start.2 = (f32[32,512]{1,0:T(8,128)S(1)}, f32[32,512]{1,0:T(8,128)S(1)}, u32[]{:S(2)}, u32[]{:S(2)}) collective-permute-start(f32[32,512]{1,0:T(8,128)S(1)} %add.22), channel_id=1, source_target_pairs={{0,112},{16,96},{32,80},{48,64},{64,48},{80,32},{96,16},{112,0},{1... | collective-permute-start | bytes 196616 | tf_op jit(solution)/shard_map/ppermute | solution.py:284
  136.3 4.0 %shard_map.102.refs_1_ = bf16[1792,96]{1,0:T(8,128)(2,1)S(1)} custom-call(f32[32,14,128]{2,1,0:T(8,128)S(1)} %all-to-all-done.2.factor_ref), custom_call_target="tpu_custom_call" | custom-call | tf_op jit(solution)/shard_map/pallas_call | solution.py:39
  140.6 2.5 %collective-permute-start.3 = (f32[32,512]{1,0:T(8,128)S(1)}, f32[32,512]{1,0:T(8,128)S(1)}, u32[]{:S(2)}, u32[]{:S(2)}) collective-permute-start(f32[32,512]{1,0:T(8,128)S(1)} %add.23), channel_id=1, source_target_pairs={{0,128},{128,0},{256,384},{384,256},{1,129},{129,1},{257,385},{385... | collective-permute-start | bytes 196616 | tf_op jit(solution)/shard_map/ppermute | solution.py:284
  143.1 0.6 constant_dynamic-slice_fusion.refs_2_
  143.7 2.2 %collective-permute-done.3 = f32[32,512]{1,0:T(8,128)S(1)} collective-permute-done((f32[32,512]{1,0:T(8,128)S(1)}, f32[32,512]{1,0:T(8,128)S(1)}, u32[]{:S(2)}, u32[]{:S(2)}) %collective-permute-start.3) | collective-permute-done | bytes 65568 | tf_op jit(solution)/shard_map/ppermute | solution.py:284
  145.9 3.8 %collective-permute-start.4 = (f32[32,512]{1,0:T(8,128)S(1)}, f32[32,512]{1,0:T(8,128)S(1)}, u32[]{:S(2)}, u32[]{:S(2)}) collective-permute-start(f32[32,512]{1,0:T(8,128)S(1)} %add.26), channel_id=1, source_target_pairs={{0,384},{128,256},{256,128},{384,0},{1,385},{129,257},{257,129},{3... | collective-permute-start | bytes 196616 | tf_op jit(solution)/shard_map/ppermute | solution.py:284
  149.8 2.6 %collective-permute-done.4 = f32[32,512]{1,0:T(8,128)S(1)} collective-permute-done((f32[32,512]{1,0:T(8,128)S(1)}, f32[32,512]{1,0:T(8,128)S(1)}, u32[]{:S(2)}, u32[]{:S(2)}) %collective-permute-start.4) | collective-permute-done | bytes 65568 | tf_op jit(solution)/shard_map/ppermute | solution.py:284
  152.4 0.6 add.27.refs_0_
  153.1 4.8 %shard_map.103 = (bf16[1792,512]{1,0:T(8,128)(2,1)}, f32[56,512]{1,0:T(8,128)}) custom-call(f32[32,512]{1,0:T(8,128)} %add.27.refs_0_, bf16[1792,96]{1,0:T(8,128)(2,1)} %copy-done.2, bf16[56,96]{1,0:T(8,128)(2,1)} %constant_dynamic-slice_fusion.refs_2_, bf16[1792,512]{1,0:T(8,128)(2,1)} %shard_map.98.merged_hbm.refs_3_), custom_call_target="tpu_custom_call" | custom-call | tf_op jit(solution)/shard_map/pallas_call | solution.py:39
  157.9 6.0 %all-to-all-done.3 = bf16[16,32,1792]{2,1,0:T(8,128)(2,1)S(1)} async-done(((bf16[16,32,1792]{2,1,0:T(8,128)(2,1)}), bf16[16,32,1792]{2,1,0:T(8,128)(2,1)S(1)}, u32[]{:S(2)}, u32[]{:S(2)}) %all-to-all-start.3) | async-done | bytes 1835040 | tf_op jit(solution)/shard_map/all_to_all | solution.py:368
  163.9 1.4 shard_map.101
  (23 shorter events, 0.9 us)
Async XLA Ops:
  4.2 12.0 %copy-start.5 = (f32[1,512,32]{1,2,0:T(8,128)S(1)}, f32[1,512,32]{1,2,0:T(8,128)}, u32[]{:S(2)}) copy-start(f32[1,512,32]{1,2,0:T(8,128)} %param.13) | copy-start | bytes 196612
  4.2 12.1 %copy-start.6 = (bf16[1,56,512]{2,1,0:T(8,128)(2,1)S(1)}, bf16[1,56,512]{2,1,0:T(8,128)(2,1)}, u32[]{:S(2)}) copy-start(bf16[1,56,512]{2,1,0:T(8,128)(2,1)} %param.11) | copy-start | bytes 172036
  4.2 66.3 %all-to-all-start = ((bf16[16,32,2304]{2,1,0:T(8,128)(2,1)}), bf16[16,32,2304]{2,1,0:T(8,128)(2,1)S(1)}, u32[]{:S(2)}, u32[]{:S(2)}) async-start(bf16[16,32,2304]{2,1,0:T(8,128)(2,1)} %bitcast.17), calls=%async_computation | async-start | bytes 4718592 | tf_op jit(solution)/shard_map/all_to_all | solution.py:315
  95.3 0.7 copy-start.3
  96.0 16.0 %all-to-all-start.2 = ((f32[32,14,128]{2,1,0:T(8,128)}), f32[32,14,128]{2,1,0:T(8,128)S(1)}, u32[]{:S(2)}, u32[]{:S(2)}) async-start(f32[32,14,128]{2,1,0:T(8,128)} %copy-done.3), calls=%async_computation.2 | async-start | bytes 524288 | tf_op jit(solution)/shard_map/all_to_all | solution.py:366
  102.3 1.2 copy-start
  103.5 1.0 copy-start.1
  112.0 51.9 %all-to-all-start.3 = ((bf16[16,32,1792]{2,1,0:T(8,128)(2,1)}), bf16[16,32,1792]{2,1,0:T(8,128)(2,1)S(1)}, u32[]{:S(2)}, u32[]{:S(2)}) async-start(bf16[16,32,1792]{2,1,0:T(8,128)(2,1)} %bitcast.18), calls=%async_computation.3 | async-start | bytes 3670016 | tf_op jit(solution)/shard_map/all_to_all | solution.py:368
  120.3 10.8 %copy-start.4 = (s32[128,2]{0,1:T(2,128)S(1)}, s32[128,2]{0,1:T(2,128)}, u32[]{:S(2)}) copy-start(s32[128,2]{0,1:T(2,128)} %param.8) | copy-start | bytes 3076
  120.3 29.4 %copy-start.7 = (f32[128,2]{0,1:T(2,128)S(1)}, f32[128,2]{0,1:T(2,128)}, u32[]{:S(2)}) copy-start(f32[128,2]{0,1:T(2,128)} %param.9) | copy-start | bytes 3076
  122.0 5.9 %collective-permute-start = (f32[32,512]{1,0:T(8,128)S(1)}, f32[32,512]{1,0:T(8,128)S(1)}, u32[]{:S(2)}, u32[]{:S(2)}) collective-permute-start(f32[32,512]{1,0:T(8,128)S(1)} %shard_map.99), channel_id=1, source_target_pairs={{0,16},{16,0},{32,48},{48,32},{64,80},{80,64},{96,112},{112,96},{1... | collective-permute-start | bytes 196616 | tf_op jit(solution)/shard_map/ppermute | solution.py:284
  127.8 6.2 %collective-permute-start.1 = (f32[32,512]{1,0:T(8,128)S(1)}, f32[32,512]{1,0:T(8,128)S(1)}, u32[]{:S(2)}, u32[]{:S(2)}) collective-permute-start(f32[32,512]{1,0:T(8,128)S(1)} %add.21), channel_id=1, source_target_pairs={{0,32},{16,48},{32,0},{48,16},{64,96},{80,112},{96,64},{112,80},{1... | collective-permute-start | bytes 196616 | tf_op jit(solution)/shard_map/ppermute | solution.py:284
  134.1 6.5 %collective-permute-start.2 = (f32[32,512]{1,0:T(8,128)S(1)}, f32[32,512]{1,0:T(8,128)S(1)}, u32[]{:S(2)}, u32[]{:S(2)}) collective-permute-start(f32[32,512]{1,0:T(8,128)S(1)} %add.22), channel_id=1, source_target_pairs={{0,112},{16,96},{32,80},{48,64},{64,48},{80,32},{96,16},{112,0},{1... | collective-permute-start | bytes 196616 | tf_op jit(solution)/shard_map/ppermute | solution.py:284
  140.3 12.7 %copy-start.2 = (bf16[1792,96]{1,0:T(8,128)(2,1)}, bf16[1792,96]{1,0:T(8,128)(2,1)S(1)}, u32[]{:S(2)}) copy-start(bf16[1792,96]{1,0:T(8,128)(2,1)S(1)} %shard_map.102.refs_1_) | copy-start | bytes 1032196
  140.6 5.3 %collective-permute-start.3 = (f32[32,512]{1,0:T(8,128)S(1)}, f32[32,512]{1,0:T(8,128)S(1)}, u32[]{:S(2)}, u32[]{:S(2)}) collective-permute-start(f32[32,512]{1,0:T(8,128)S(1)} %add.23), channel_id=1, source_target_pairs={{0,128},{128,0},{256,384},{384,256},{1,129},{129,1},{257,385},{385... | collective-permute-start | bytes 196616 | tf_op jit(solution)/shard_map/ppermute | solution.py:284
  145.9 6.5 %collective-permute-start.4 = (f32[32,512]{1,0:T(8,128)S(1)}, f32[32,512]{1,0:T(8,128)S(1)}, u32[]{:S(2)}, u32[]{:S(2)}) collective-permute-start(f32[32,512]{1,0:T(8,128)S(1)} %add.26), channel_id=1, source_target_pairs={{0,384},{128,256},{256,128},{384,0},{1,385},{129,257},{257,129},{3... | collective-permute-start | bytes 196616 | tf_op jit(solution)/shard_map/ppermute | solution.py:284

commit v7 on v6

--- a/solution.py
+++ b/solution.py
@@ -6,8 +6,8 @@
 from jax.sharding import Mesh
 from jax.sharding import PartitionSpec as P
 
-DP = ("dp_0", "dp_1")
-DP_EXPERT = ("dp_0", "dp_1", "expert")
+DP = ("dp_0", "dp_1", "dp_2")
+DP_EXPERT = ("dp_0", "dp_1", "dp_2", "expert")
 
 f32, bf16 = jnp.float32, jnp.bfloat16
 HBM = pl.BlockSpec(memory_space=pltpu.HBM)
@@ -69,7 +69,6 @@
     experts, capacity, routes_hbm, gates_hbm, tokens_hbm, grad_hbm, sent_hbm, routes, gates, tokens, grad, sent, sem
 ):
     width = tokens.shape[1]
-    hidden = grad.shape[2]
     copies = [
         pltpu.make_async_copy(routes_hbm, routes, sem.at[0]),
         pltpu.make_async_copy(gates_hbm, gates, sem.at[1]),
@@ -83,9 +82,6 @@
     copies[1].wait()
     gate = jnp.sum(first * gates[0:1, :] + second * gates[1:2, :], axis=1, keepdims=True)
     either, first, second = (first + second).astype(bf16), first.astype(bf16), second.astype(bf16)
-    copies[3].wait()
-    pairs = grad[...]
-    grad_0, grad_1 = pairs[:, 0, :], pairs[:, 1, :]
     copies[2].wait()
     parts = 4
     step = first.shape[0] // parts
@@ -93,11 +89,13 @@
     for i in range(parts):
         rows = slice(i * step, (i + 1) * step)
         sent[rows, :width] = (nn(either[rows], tokens[...]) * gate[rows]).astype(bf16)
-        grads = nn(first[rows], grad_0) + nn(second[rows], grad_1)
-        sent[rows, width:] = grads.astype(bf16)
-        copy = pltpu.make_async_copy(sent.at[rows], sent_hbm.at[rows], sem.at[4 + i])
-        copy.start()
-        done.append(copy)
+        done.append(pltpu.make_async_copy(sent.at[rows, :width], sent_hbm.at[rows, :width], sem.at[4 + i]))
+        done[i].start()
+    copies[3].wait()
+    pairs = grad[...]
+    sent[:, width:] = (nn(first, pairs[:, 0, :]) + nn(second, pairs[:, 1, :])).astype(bf16)
+    done.append(pltpu.make_async_copy(sent.at[:, width:], sent_hbm.at[:, width:], sem.at[4 + parts]))
+    done[parts].start()
     for copy in done:
         copy.wait()
 
@@ -183,9 +181,15 @@
         store.wait()
 
 
-def sum_and_copy_kernel(parts_ref, copies_ref):
-    total = jnp.sum(parts_ref[...], axis=0)
-    copies_ref[...] = jnp.broadcast_to(total[None], copies_ref.shape)
+def sum_and_copy_kernel(parts_ref, copies_hbm, total, sem):
+    total[...] = jnp.sum(parts_ref[...], axis=0)
+    copies = [
+        pltpu.make_async_copy(total, copies_hbm.at[i], sem.at[i]) for i in range(copies_hbm.shape[0])
+    ]
+    for copy in copies:
+        copy.start()
+    for copy in copies:
+        copy.wait()
 
 
 def right_kernel(factor_ref, merged_hbm, right_ref, merged, sem):
@@ -308,14 +312,14 @@
             pltpu.VMEM((row_count, width), bf16),
             pltpu.VMEM((row_count, 2, hidden), bf16),
             pltpu.VMEM((slots, width + hidden), bf16),
-            dma((8,)),
+            dma((9,)),
         ],
     )
     w_mine, sent = lax.optimization_barrier((w_in[0], sent))
     arrived = lax.all_to_all(
         sent.reshape(experts, capacity, width + hidden), "expert", 0, 0, tiled=True
     ).reshape(slots, width + hidden)
-    weight = lax.all_gather(w_mine, DP[1], tiled=True)
+    weight = lax.all_gather(lax.all_gather(w_mine, DP[2], tiled=True), DP[1], tiled=True)
     half = hidden // 2
     weight_0 = lax.all_gather(weight[:, :half], DP[0], tiled=True)
     weight_1 = lax.all_gather(weight[:, half:], DP[0], tiled=True)
@@ -360,8 +364,11 @@
     )
     copies = call(
         sum_and_copy_kernel,
-        shape((replicas, each * blocks, LANES), f32),
+        pltpu.HBM((replicas, each * blocks, LANES), f32),
         (parts.reshape(replicas, each * blocks, LANES),),
+        in_specs=[VMEM],
+        out_specs=HBM,
+        scratch_shapes=[pltpu.VMEM((each * blocks, LANES), f32), dma((replicas,))],
     )
     factor = lax.all_to_all(copies, DP, 0, 0, tiled=True).reshape(rank, blocks, LANES)
     factor, grad_rows, merged = lax.optimization_barrier((factor, grad_rows, merged))
@@ -390,7 +397,7 @@
         shape((2 * row_count, slots), bf16),
         (routes_t,),
     )
-    steps = [(axis, step) for axis in DP[::-1] for step in partners(lax.axis_size(axis))]
+    steps = [(axis, step) for axis in (DP[1:], DP[0]) for step in partners(lax.axis_size(axis))]
     for i, (axis, step) in enumerate(steps):
         other = from_partner(right, axis, step)
         if i == len(steps) - 4:
@@ -426,7 +433,7 @@
 
 
 def solution(mesh):
-    torus = Mesh(mesh.devices.reshape(4, 8, mesh.shape["expert"]), DP_EXPERT)
+    torus = Mesh(mesh.devices.reshape(4, 4, 2, mesh.shape["expert"]), DP_EXPERT)
     in_specs = (
         P(DP_EXPERT, None),
         P(DP_EXPERT, None),

time: 166 us -> 167 us (level)
  waiting for transfers between devices: 23 us -> 26.3 us
  blocking collectives: 67.7 us -> 64.7 us
    all_to_all x1, waiting for transfers between devices: 5.64 us -> 8.58 us  [body(): lax.all_to_all(sent.reshape(experts, capacity, width + hidden), 'expert',...]
    all_gather x1 -> x2, blocking collectives: 22.6 us -> 19.8 us  [the longest x1 15.6 us: body(): lax.all_gather(lax.all_gather(w_mine, DP[2], tiled=True), DP[1], tiled=True)]
  transfers between devices with their start and end apart: 8 -> 8, of which waited for: 8 -> 7; matrix products, arithmetic and copies ran while one was open for 1% -> 1% of each run, Pallas kernels for 10% -> 10%
where the time goes in v7:
time: 167 us; the launch traced here: 166 us
  blocking collectives  64.7 us (39%)
  starting transfers between devices  41.8 us (25%)
  Pallas kernels  28.4 us (17%)
  waiting for transfers between devices  26.3 us (16%)
  local copies, waits for them, and re-layouts  3.12 us (2%)
    pallas_call x10, Pallas kernels, call(): pl.pallas_call(kernel, out_shape=outs, compiler_params=pltpu.CompilerPara...  28.4 us
    all_to_all x1, blocking collectives, body(): parts = lax.all_to_all(factor, DP, 0, 0, tiled=True)  19.1 us
    all_gather x1, blocking collectives, body(): lax.all_gather(lax.all_gather(w_mine, DP[2], tiled=True), DP[1], tiled=True)  15.6 us
    ppermute x5, starting transfers between devices, from_partner(): lax.ppermute(x, axis, [(i, i ^ step) for i in range(lax.axis_size(axis))])  14.8 us
    all_gather x1, blocking collectives, body(): weight_1 = lax.all_gather(weight[:, half:], DP[0], tiled=True)  13.5 us
    all_gather x1, blocking collectives, body(): weight_0 = lax.all_gather(weight[:, :half], DP[0], tiled=True)  12.3 us
    all_to_all x1, starting transfers between devices, body(): lax.all_to_all(sent.reshape(experts, capacity, width + hidden), 'expert',...  12 us
    ppermute x5, waiting for transfers between devices, from_partner(): lax.ppermute(x, axis, [(i, i ^ step) for i in range(lax.axis_size(axis))])  10.2 us
  transfers between devices with their start and end apart: 8, of which 7 were waited for; matrix products, arithmetic and copies ran while one was open for 1% of the time, Pallas kernels for 10%

profile of v7, /device:TPU:1, one launch (start us, length us, event | category | flops | bytes accessed | tf_op | source)
XLA Modules:
  0.0 165.9 jit_solution(15039517664024294347)
XLA Ops:
  0.6 3.5 %shard_map.94 = bf16[512,2304]{1,0:T(8,128)(2,1)} custom-call(s32[2,128]{1,0:T(2,128)} %bitcast.15, f32[2,128]{1,0:T(2,128)} %bitcast.22, bf16[128,1792]{1,0:T(8,128)(2,1)} %refs_2_.1, bf16[128,2,512]{2,1,0:T(2,128)(2,1)} %refs_3_.1), custom_call_target="tpu_custom_call" | custom-call | tf_op jit(solution)/shard_map/pallas_call | solution.py:39
  4.2 12.0 %all-to-all-start = ((bf16[16,32,2304]{2,1,0:T(8,128)(2,1)}), bf16[16,32,2304]{2,1,0:T(8,128)(2,1)S(1)}, u32[]{:S(2)}, u32[]{:S(2)}) async-start(bf16[16,32,2304]{2,1,0:T(8,128)(2,1)} %bitcast.17), calls=%async_computation | async-start | bytes 4718592 | tf_op jit(solution)/shard_map/all_to_all | solution.py:319
  16.3 4.2 %all_gather.12 = bf16[112,512]{1,0:T(8,128)(2,1)S(1)} all-gather(bf16[56,512]{1,0:T(8,128)(2,1)S(1)} %bitcast.21), channel_id=1, replica_groups=mesh['dp_0'=4,'dp_1'=4,'dp_2'=2,'expert'=16] {'dp_2'}, dimensions={0}, use_global_device_ids=true | all-gather | bytes 172032 | tf_op jit(solution)/shard_map/all_gather | solution.py:322
  20.5 15.6 %all_gather.13 = bf16[448,512]{1,0:T(8,128)(2,1)S(1)} all-gather(bf16[112,512]{1,0:T(8,128)(2,1)S(1)} %all_gather.12), channel_id=1, replica_groups=mesh['dp_0'=4,'dp_1'=4,'dp_2'=2,'expert'=16] {'dp_1'}, dimensions={0}, use_global_device_ids=true | all-gather | bytes 573440 | tf_op jit(solution)/shard_map/all_gather | solution.py:322
  36.2 12.3 %all_gather.14.refs_1_.weight_0 = bf16[1792,256]{1,0:T(8,128)(2,1)S(1)} all-gather(bf16[448,256]{1,0:T(8,128)(2,1)S(1)} %get-tuple-element.34), channel_id=1, replica_groups=mesh['dp_0'=4,'dp_1'=4,'dp_2'=2,'expert'=16] {'dp_0'}, dimensions={0}, use_global_device_ids=true | all-gather | bytes 1146880 | tf_op jit(solution)/shard_map/all_gather | solution.py:324
  48.4 13.5 %all_gather.15.refs_2_.weight_1 = bf16[1792,256]{1,0:T(8,128)(2,1)} all-gather(bf16[448,256]{1,0:T(8,128)(2,1)S(1)} %get-tuple-element.33), channel_id=1, replica_groups=mesh['dp_0'=4,'dp_1'=4,'dp_2'=2,'expert'=16] {'dp_0'}, dimensions={0}, use_global_device_ids=true | all-gather | bytes 1146880 | tf_op jit(solution)/shard_map/all_gather | solution.py:325
  61.9 8.6 %all-to-all-done = bf16[16,32,2304]{2,1,0:T(8,128)(2,1)S(1)} async-done(((bf16[16,32,2304]{2,1,0:T(8,128)(2,1)}), bf16[16,32,2304]{2,1,0:T(8,128)(2,1)S(1)}, u32[]{:S(2)}, u32[]{:S(2)}) %all-to-all-start) | async-done | bytes 2359328 | tf_op jit(solution)/shard_map/all_to_all | solution.py:319
  70.5 5.5 %shard_map.95 = (bf16[512,512]{1,0:T(8,128)(2,1)}, f32[32,14,128]{2,1,0:T(8,128)S(1)}) custom-call(bf16[512,2304]{1,0:T(8,128)(2,1)S(1)} %bitcast.11, bf16[1792,256]{1,0:T(8,128)(2,1)S(1)} %all_gather.14.refs_1_.weight_0, bf16[1792,256]{1,0:T(8,128)(2,1)} %all_gather.15.refs_2_.weight_1, bf16[1792,512]{1,0:T(8,128)(2,1)} %bitcast.19, f32[512,32]{1,0:T(8,128)S(1)} %bitcast.14), custom_call_target="tpu_custom_call" | custom-call | tf_op jit(solution)/shard_map/pallas_call | solution.py:39
  76.1 19.1 %all_to_all.20.parts_ref = f32[32,14,128]{2,1,0:T(8,128)S(1)} all-to-all(f32[32,14,128]{2,1,0:T(8,128)S(1)} %get-tuple-element.20), channel_id=1, replica_groups=mesh['dp_0'=4,'dp_1'=4,'dp_2'=2,'expert'=16] {'dp_0','dp_1','dp_2'}, dimensions={0} | all-to-all | bytes 458752 | tf_op jit(solution)/shard_map/all_to_all | solution.py:343
  95.2 1.0 shard_map.96
  96.3 6.2 %all-to-all-start.2 = ((f32[32,14,128]{2,1,0:T(8,128)}), f32[32,14,128]{2,1,0:T(8,128)S(1)}, u32[]{:S(2)}, u32[]{:S(2)}) async-start(f32[32,14,128]{2,1,0:T(8,128)} %shard_map.96), calls=%async_computation.2 | async-start | bytes 524288 | tf_op jit(solution)/shard_map/all_to_all | solution.py:373
  102.5 1.2 copy-done
  103.6 1.0 copy-done.1
  104.7 2.1 %shard_map.97 = bf16[512,1792]{1,0:T(8,128)(2,1)} custom-call(bf16[512,512]{1,0:T(8,128)(2,1)S(1)} %copy-done.1, bf16[1792,256]{1,0:T(8,128)(2,1)S(1)} %all_gather.14.refs_1_.weight_0, bf16[1792,256]{1,0:T(8,128)(2,1)S(1)} %copy-done), custom_call_target="tpu_custom_call" | custom-call | tf_op jit(solution)/shard_map/pallas_call | solution.py:39
  106.8 4.1 %shard_map.98.merged_hbm.refs_3_ = bf16[1792,512]{1,0:T(8,128)(2,1)} custom-call(bf16[512,2304]{1,0:T(8,128)(2,1)S(1)} %bitcast.12, bf16[512,512]{1,0:T(8,128)(2,1)S(1)} %copy-done.1, bf16[1792,512]{1,0:T(8,128)(2,1)} %bitcast.20), custom_call_target="tpu_custom_call" | custom-call | tf_op jit(solution)/shard_map/pallas_call | solution.py:39
  110.9 1.2 all-to-all-done.2.factor_ref
  112.1 8.8 %all-to-all-start.3 = ((bf16[16,32,1792]{2,1,0:T(8,128)(2,1)}), bf16[16,32,1792]{2,1,0:T(8,128)(2,1)S(1)}, u32[]{:S(2)}, u32[]{:S(2)}) async-start(bf16[16,32,1792]{2,1,0:T(8,128)(2,1)} %bitcast.18), calls=%async_computation.3 | async-start | bytes 3670016 | tf_op jit(solution)/shard_map/all_to_all | solution.py:375
  120.9 1.7 %shard_map.99 = f32[32,512]{1,0:T(8,128)S(1)} custom-call(f32[32,14,128]{2,1,0:T(8,128)S(1)} %all-to-all-done.2.factor_ref, bf16[1792,512]{1,0:T(8,128)(2,1)} %shard_map.98.merged_hbm.refs_3_), custom_call_target="tpu_custom_call" | custom-call | tf_op jit(solution)/shard_map/pallas_call | solution.py:39
  122.6 3.4 %collective-permute-start = (f32[32,512]{1,0:T(8,128)S(1)}, f32[32,512]{1,0:T(8,128)S(1)}, u32[]{:S(2)}, u32[]{:S(2)}) collective-permute-start(f32[32,512]{1,0:T(8,128)S(1)} %shard_map.99), channel_id=1, source_target_pairs={{0,16},{16,0},{32,48},{48,32},{64,80},{80,64},{96,112},{112,96},{1... | collective-permute-start | bytes 196616 | tf_op jit(solution)/shard_map/ppermute | solution.py:288
  126.0 2.2 %collective-permute-done = f32[32,512]{1,0:T(8,128)S(1)} collective-permute-done((f32[32,512]{1,0:T(8,128)S(1)}, f32[32,512]{1,0:T(8,128)S(1)}, u32[]{:S(2)}, u32[]{:S(2)}) %collective-permute-start) | collective-permute-done | bytes 65568 | tf_op jit(solution)/shard_map/ppermute | solution.py:288
  128.2 3.5 %collective-permute-start.1 = (f32[32,512]{1,0:T(8,128)S(1)}, f32[32,512]{1,0:T(8,128)S(1)}, u32[]{:S(2)}, u32[]{:S(2)}) collective-permute-start(f32[32,512]{1,0:T(8,128)S(1)} %add.24), channel_id=1, source_target_pairs={{0,32},{16,48},{32,0},{48,16},{64,96},{80,112},{96,64},{112,80},{1... | collective-permute-start | bytes 196616 | tf_op jit(solution)/shard_map/ppermute | solution.py:288
  132.0 2.4 %collective-permute-done.1 = f32[32,512]{1,0:T(8,128)S(1)} collective-permute-done((f32[32,512]{1,0:T(8,128)S(1)}, f32[32,512]{1,0:T(8,128)S(1)}, u32[]{:S(2)}, u32[]{:S(2)}) %collective-permute-start.1) | collective-permute-done | bytes 65568 | tf_op jit(solution)/shard_map/ppermute | solution.py:288
  134.4 2.5 %collective-permute-start.2 = (f32[32,512]{1,0:T(8,128)S(1)}, f32[32,512]{1,0:T(8,128)S(1)}, u32[]{:S(2)}, u32[]{:S(2)}) collective-permute-start(f32[32,512]{1,0:T(8,128)S(1)} %add.25), channel_id=1, source_target_pairs={{0,112},{16,96},{32,80},{48,64},{64,48},{80,32},{96,16},{112,0},{1... | collective-permute-start | bytes 196616 | tf_op jit(solution)/shard_map/ppermute | solution.py:288
  136.9 4.0 %shard_map.102.refs_1_ = bf16[1792,96]{1,0:T(8,128)(2,1)S(1)} custom-call(f32[32,14,128]{2,1,0:T(8,128)S(1)} %all-to-all-done.2.factor_ref), custom_call_target="tpu_custom_call" | custom-call | tf_op jit(solution)/shard_map/pallas_call | solution.py:39
  141.0 2.2 %collective-permute-start.3 = (f32[32,512]{1,0:T(8,128)S(1)}, f32[32,512]{1,0:T(8,128)S(1)}, u32[]{:S(2)}, u32[]{:S(2)}) collective-permute-start(f32[32,512]{1,0:T(8,128)S(1)} %add.26), channel_id=1, source_target_pairs={{0,128},{128,0},{256,384},{384,256},{1,129},{129,1},{257,385},{385... | collective-permute-start | bytes 196616 | tf_op jit(solution)/shard_map/ppermute | solution.py:288
  143.8 2.5 %collective-permute-done.3 = f32[32,512]{1,0:T(8,128)S(1)} collective-permute-done((f32[32,512]{1,0:T(8,128)S(1)}, f32[32,512]{1,0:T(8,128)S(1)}, u32[]{:S(2)}, u32[]{:S(2)}) %collective-permute-start.3) | collective-permute-done | bytes 65568 | tf_op jit(solution)/shard_map/ppermute | solution.py:288
  146.3 3.3 %collective-permute-start.4 = (f32[32,512]{1,0:T(8,128)S(1)}, f32[32,512]{1,0:T(8,128)S(1)}, u32[]{:S(2)}, u32[]{:S(2)}) collective-permute-start(f32[32,512]{1,0:T(8,128)S(1)} %add.30), channel_id=1, source_target_pairs={{0,384},{128,256},{256,128},{384,0},{1,385},{129,257},{257,129},{3... | collective-permute-start | bytes 196616 | tf_op jit(solution)/shard_map/ppermute | solution.py:288
  149.7 3.1 %collective-permute-done.4 = f32[32,512]{1,0:T(8,128)S(1)} collective-permute-done((f32[32,512]{1,0:T(8,128)S(1)}, f32[32,512]{1,0:T(8,128)S(1)}, u32[]{:S(2)}, u32[]{:S(2)}) %collective-permute-start.4) | collective-permute-done | bytes 65568 | tf_op jit(solution)/shard_map/ppermute | solution.py:288
  152.8 0.6 add.31.refs_0_
  153.4 4.8 %shard_map.103 = (bf16[1792,512]{1,0:T(8,128)(2,1)}, f32[56,512]{1,0:T(8,128)}) custom-call(f32[32,512]{1,0:T(8,128)} %add.31.refs_0_, bf16[1792,96]{1,0:T(8,128)(2,1)} %copy-done.2, bf16[56,96]{1,0:T(8,128)(2,1)} %constant_dynamic-slice_fusion.refs_2_, bf16[1792,512]{1,0:T(8,128)(2,1)} %shard_map.98.merged_hbm.refs_3_), custom_call_target="tpu_custom_call" | custom-call | tf_op jit(solution)/shard_map/pallas_call | solution.py:39
  158.3 6.3 %all-to-all-done.3 = bf16[16,32,1792]{2,1,0:T(8,128)(2,1)S(1)} async-done(((bf16[16,32,1792]{2,1,0:T(8,128)(2,1)}), bf16[16,32,1792]{2,1,0:T(8,128)(2,1)S(1)}, u32[]{:S(2)}, u32[]{:S(2)}) %all-to-all-start.3) | async-done | bytes 1835040 | tf_op jit(solution)/shard_map/all_to_all | solution.py:375
  164.6 1.4 shard_map.101
  (22 shorter events, 1.2 us)
Async XLA Ops:
  4.2 12.0 %copy-start.4 = (f32[1,512,32]{1,2,0:T(8,128)S(1)}, f32[1,512,32]{1,2,0:T(8,128)}, u32[]{:S(2)}) copy-start(f32[1,512,32]{1,2,0:T(8,128)} %param.13) | copy-start | bytes 196612
  4.2 12.1 %copy-start.5 = (bf16[1,56,512]{2,1,0:T(8,128)(2,1)S(1)}, bf16[1,56,512]{2,1,0:T(8,128)(2,1)}, u32[]{:S(2)}) copy-start(bf16[1,56,512]{2,1,0:T(8,128)(2,1)} %param.11) | copy-start | bytes 172036
  4.2 66.3 %all-to-all-start = ((bf16[16,32,2304]{2,1,0:T(8,128)(2,1)}), bf16[16,32,2304]{2,1,0:T(8,128)(2,1)S(1)}, u32[]{:S(2)}, u32[]{:S(2)}) async-start(bf16[16,32,2304]{2,1,0:T(8,128)(2,1)} %bitcast.17), calls=%async_computation | async-start | bytes 4718592 | tf_op jit(solution)/shard_map/all_to_all | solution.py:319
  96.3 15.9 %all-to-all-start.2 = ((f32[32,14,128]{2,1,0:T(8,128)}), f32[32,14,128]{2,1,0:T(8,128)S(1)}, u32[]{:S(2)}, u32[]{:S(2)}) async-start(f32[32,14,128]{2,1,0:T(8,128)} %shard_map.96), calls=%async_computation.2 | async-start | bytes 524288 | tf_op jit(solution)/shard_map/all_to_all | solution.py:373
  102.5 1.2 copy-start
  103.6 1.0 copy-start.1
  112.1 52.5 %all-to-all-start.3 = ((bf16[16,32,1792]{2,1,0:T(8,128)(2,1)}), bf16[16,32,1792]{2,1,0:T(8,128)(2,1)S(1)}, u32[]{:S(2)}, u32[]{:S(2)}) async-start(bf16[16,32,1792]{2,1,0:T(8,128)(2,1)} %bitcast.18), calls=%async_computation.3 | async-start | bytes 3670016 | tf_op jit(solution)/shard_map/all_to_all | solution.py:375
  120.9 10.8 %copy-start.3 = (s32[128,2]{0,1:T(2,128)S(1)}, s32[128,2]{0,1:T(2,128)}, u32[]{:S(2)}) copy-start(s32[128,2]{0,1:T(2,128)} %param.8) | copy-start | bytes 3076
  120.9 28.6 %copy-start.6 = (f32[128,2]{0,1:T(2,128)S(1)}, f32[128,2]{0,1:T(2,128)}, u32[]{:S(2)}) copy-start(f32[128,2]{0,1:T(2,128)} %param.9) | copy-start | bytes 3076
  122.6 5.6 %collective-permute-start = (f32[32,512]{1,0:T(8,128)S(1)}, f32[32,512]{1,0:T(8,128)S(1)}, u32[]{:S(2)}, u32[]{:S(2)}) collective-permute-start(f32[32,512]{1,0:T(8,128)S(1)} %shard_map.99), channel_id=1, source_target_pairs={{0,16},{16,0},{32,48},{48,32},{64,80},{80,64},{96,112},{112,96},{1... | collective-permute-start | bytes 196616 | tf_op jit(solution)/shard_map/ppermute | solution.py:288
  128.2 6.2 %collective-permute-start.1 = (f32[32,512]{1,0:T(8,128)S(1)}, f32[32,512]{1,0:T(8,128)S(1)}, u32[]{:S(2)}, u32[]{:S(2)}) collective-permute-start(f32[32,512]{1,0:T(8,128)S(1)} %add.24), channel_id=1, source_target_pairs={{0,32},{16,48},{32,0},{48,16},{64,96},{80,112},{96,64},{112,80},{1... | collective-permute-start | bytes 196616 | tf_op jit(solution)/shard_map/ppermute | solution.py:288
  134.4 6.5 %collective-permute-start.2 = (f32[32,512]{1,0:T(8,128)S(1)}, f32[32,512]{1,0:T(8,128)S(1)}, u32[]{:S(2)}, u32[]{:S(2)}) collective-permute-start(f32[32,512]{1,0:T(8,128)S(1)} %add.25), channel_id=1, source_target_pairs={{0,112},{16,96},{32,80},{48,64},{64,48},{80,32},{96,16},{112,0},{1... | collective-permute-start | bytes 196616 | tf_op jit(solution)/shard_map/ppermute | solution.py:288
  140.9 12.5 %copy-start.2 = (bf16[1792,96]{1,0:T(8,128)(2,1)}, bf16[1792,96]{1,0:T(8,128)(2,1)S(1)}, u32[]{:S(2)}) copy-start(bf16[1792,96]{1,0:T(8,128)(2,1)S(1)} %shard_map.102.refs_1_) | copy-start | bytes 1032196
  141.0 5.3 %collective-permute-start.3 = (f32[32,512]{1,0:T(8,128)S(1)}, f32[32,512]{1,0:T(8,128)S(1)}, u32[]{:S(2)}, u32[]{:S(2)}) collective-permute-start(f32[32,512]{1,0:T(8,128)S(1)} %add.26), channel_id=1, source_target_pairs={{0,128},{128,0},{256,384},{384,256},{1,129},{129,1},{257,385},{385... | collective-permute-start | bytes 196616 | tf_op jit(solution)/shard_map/ppermute | solution.py:288
  146.3 6.5 %collective-permute-start.4 = (f32[32,512]{1,0:T(8,128)S(1)}, f32[32,512]{1,0:T(8,128)S(1)}, u32[]{:S(2)}, u32[]{:S(2)}) collective-permute-start(f32[32,512]{1,0:T(8,128)S(1)} %add.30), channel_id=1, source_target_pairs={{0,384},{128,256},{256,128},{384,0},{1,385},{129,257},{257,129},{3... | collective-permute-start | bytes 196616 | tf_op jit(solution)/shard_map/ppermute | solution.py:288

commit v8 on v6

--- a/solution.py
+++ b/solution.py
@@ -6,8 +6,8 @@
 from jax.sharding import Mesh
 from jax.sharding import PartitionSpec as P
 
-DP = ("dp_0", "dp_1")
-DP_EXPERT = ("dp_0", "dp_1", "expert")
+DP = ("dp_0", "dp_1", "dp_2")
+DP_EXPERT = ("dp_0", "dp_1", "dp_2", "expert")
 
 f32, bf16 = jnp.float32, jnp.bfloat16
 HBM = pl.BlockSpec(memory_space=pltpu.HBM)
@@ -109,7 +109,7 @@
 
 
 def factor_kernel(
-    width, arrived_ref, weight_0, weight_hbm, error_hbm, seed_ref, grad_pre_hbm, factor_ref, weight_1, error, grad_pre, sem
+    width, arrived_ref, weight_0, weight_hbm, error_hbm, seed_ref, grad_pre_hbm, factor_hbm, weight_1, error, grad_pre, out, sem
 ):
     rank = seed_ref.shape[1]
     step = width // TILES
@@ -143,8 +143,11 @@
         seeded = nn(error[rows, :], seed)
         total = factor[:, rows] + (seeded[:, :rank] + seeded[:, rank:]).T
         for j in range(step // LANES):
-            factor_ref[:, i * (step // LANES) + j, :] = total[:, j * LANES : (j + 1) * LANES]
+            out[:, i * (step // LANES) + j, :] = total[:, j * LANES : (j + 1) * LANES]
+    send = pltpu.make_async_copy(out, factor_hbm, sem.at[TILES + 2])
+    send.start()
     store.wait()
+    send.wait()
 
 
 def merge_kernel(width, arrived_ref, grad_pre_ref, error_hbm, merged_hbm, error, merged, load_sem, store_sem):
@@ -315,7 +318,7 @@
     arrived = lax.all_to_all(
         sent.reshape(experts, capacity, width + hidden), "expert", 0, 0, tiled=True
     ).reshape(slots, width + hidden)
-    weight = lax.all_gather(w_mine, DP[1], tiled=True)
+    weight = lax.all_gather(lax.all_gather(w_mine, DP[2], tiled=True), DP[1], tiled=True)
     half = hidden // 2
     weight_0 = lax.all_gather(weight[:, :half], DP[0], tiled=True)
     weight_1 = lax.all_gather(weight[:, half:], DP[0], tiled=True)
@@ -324,15 +327,16 @@
     stored = in_hbm(error[0, 0])
     grad_pre, factor = call(
         lambda *refs: factor_kernel(width, *refs),
-        (pltpu.HBM((slots, hidden), bf16), shape((rank, blocks, LANES), f32)),
+        (pltpu.HBM((slots, hidden), bf16), pltpu.HBM((rank, blocks, LANES), f32)),
         (arrived, weight_0, in_hbm(weight_1), stored, q_seed[0]),
         in_specs=[VMEM, VMEM, HBM, HBM, VMEM],
-        out_specs=[HBM, VMEM],
+        out_specs=[HBM, HBM],
         scratch_shapes=[
             pltpu.VMEM((width, half), bf16),
             pltpu.VMEM((width, hidden), bf16),
             pltpu.VMEM((slots, hidden), bf16),
-            dma((TILES + 2,)),
+            pltpu.VMEM((rank, blocks, LANES), f32),
+            dma((TILES + 3,)),
         ],
     )
     each = rank // replicas
@@ -358,13 +362,14 @@
         out_specs=HBM,
         scratch_shapes=[pltpu.VMEM((slots, width), bf16), dma((2,))],
     )
+    parts, merged = lax.optimization_barrier((parts, merged))
     copies = call(
         sum_and_copy_kernel,
         shape((replicas, each * blocks, LANES), f32),
         (parts.reshape(replicas, each * blocks, LANES),),
     )
     factor = lax.all_to_all(copies, DP, 0, 0, tiled=True).reshape(rank, blocks, LANES)
-    factor, grad_rows, merged = lax.optimization_barrier((factor, grad_rows, merged))
+    factor, grad_rows = lax.optimization_barrier((factor, grad_rows))
     returned = lax.all_to_all(
         grad_rows.reshape(experts, capacity, width), "expert", 0, 0, tiled=True
     ).reshape(slots, width)
@@ -390,7 +395,7 @@
         shape((2 * row_count, slots), bf16),
         (routes_t,),
     )
-    steps = [(axis, step) for axis in DP[::-1] for step in partners(lax.axis_size(axis))]
+    steps = [(axis, step) for axis in (DP[1:], DP[0]) for step in partners(lax.axis_size(axis))]
     for i, (axis, step) in enumerate(steps):
         other = from_partner(right, axis, step)
         if i == len(steps) - 4:
@@ -426,7 +431,7 @@
 
 
 def solution(mesh):
-    torus = Mesh(mesh.devices.reshape(4, 8, mesh.shape["expert"]), DP_EXPERT)
+    torus = Mesh(mesh.devices.reshape(4, 4, 2, mesh.shape["expert"]), DP_EXPERT)
     in_specs = (
         P(DP_EXPERT, None),
         P(DP_EXPERT, None),

time: 166 us -> 167 us (level)
  blocking collectives: 67.7 us -> 45.6 us
  waiting for transfers between devices: 23 us -> 35 us
  starting transfers between devices: 41.8 us -> 51.4 us
    all_to_all x1 -> x0, blocking collectives: 19.2 us -> none  [body(): parts = lax.all_to_all(factor, DP, 0, 0, tiled=True)]
    all_to_all x0 -> x1, starting transfers between devices: none -> 9.68 us  [body(): parts = lax.all_to_all(factor, DP, 0, 0, tiled=True)]
    all_to_all x0 -> x1, waiting for transfers between devices: none -> 4.59 us  [body(): parts = lax.all_to_all(factor, DP, 0, 0, tiled=True)]
    all_to_all x1, waiting for transfers between devices: 1.23 us -> 5.29 us  [body(): lax.all_to_all(copies, DP, 0, 0, tiled=True).reshape(rank, blocks, LANES)]
    all_to_all x1, waiting for transfers between devices: 5.64 us -> 8.55 us  [body(): lax.all_to_all(sent.reshape(experts, capacity, width + hidden), 'expert',...]
    all_gather x1 -> x2, blocking collectives: 22.6 us -> 19.8 us  [the longest x1 15.7 us: body(): lax.all_gather(lax.all_gather(w_mine, DP[2], tiled=True), DP[1], tiled=True)]
  transfers between devices with their start and end apart: 8 -> 9, of which waited for: 8 -> 8; matrix products, arithmetic and copies ran while one was open for 1% -> 1% of each run, Pallas kernels for 10% -> 10%
where the time goes in v8:
time: 167 us
  starting transfers between devices  51.4 us (31%)
  blocking collectives  45.6 us (27%)
  waiting for transfers between devices  35 us (21%)
  Pallas kernels  28.9 us (17%)
  local copies, waits for them, and re-layouts  4.15 us (2%)
    pallas_call x10, Pallas kernels, call(): pl.pallas_call(kernel, out_shape=outs, compiler_params=pltpu.CompilerPara...  28.9 us
    all_gather x1, blocking collectives, body(): lax.all_gather(lax.all_gather(w_mine, DP[2], tiled=True), DP[1], tiled=True)  15.7 us
    ppermute x5, starting transfers between devices, from_partner(): lax.ppermute(x, axis, [(i, i ^ step) for i in range(lax.axis_size(axis))])  14.8 us
    all_gather x1, blocking collectives, body(): weight_1 = lax.all_gather(weight[:, half:], DP[0], tiled=True)  13.5 us
    all_gather x1, blocking collectives, body(): weight_0 = lax.all_gather(weight[:, :half], DP[0], tiled=True)  12.3 us
    all_to_all x1, starting transfers between devices, body(): lax.all_to_all(sent.reshape(experts, capacity, width + hidden), 'expert',...  12 us
    ppermute x5, waiting for transfers between devices, from_partner(): lax.ppermute(x, axis, [(i, i ^ step) for i in range(lax.axis_size(axis))])  10.3 us
    all_to_all x1, starting transfers between devices, body(): parts = lax.all_to_all(factor, DP, 0, 0, tiled=True)  9.68 us
  transfers between devices with their start and end apart: 9, of which 8 were waited for; matrix products, arithmetic and copies ran while one was open for 1% of the time, Pallas kernels for 10%

profile of v8, /device:TPU:1, one launch (start us, length us, event | category | flops | bytes accessed | tf_op | source)
XLA Modules:
  0.0 166.6 jit_solution(13700937077014364483)
XLA Ops:
  0.6 3.5 %shard_map.94 = bf16[512,2304]{1,0:T(8,128)(2,1)} custom-call(s32[2,128]{1,0:T(2,128)} %bitcast.15, f32[2,128]{1,0:T(2,128)} %bitcast.22, bf16[128,1792]{1,0:T(8,128)(2,1)} %refs_2_.1, bf16[128,2,512]{2,1,0:T(2,128)(2,1)} %refs_3_.1), custom_call_target="tpu_custom_call" | custom-call | tf_op jit(solution)/shard_map/pallas_call | solution.py:39
  4.2 12.0 %all-to-all-start = ((bf16[16,32,2304]{2,1,0:T(8,128)(2,1)}), bf16[16,32,2304]{2,1,0:T(8,128)(2,1)S(1)}, u32[]{:S(2)}, u32[]{:S(2)}) async-start(bf16[16,32,2304]{2,1,0:T(8,128)(2,1)} %bitcast.17), calls=%async_computation | async-start | bytes 4718592 | tf_op jit(solution)/shard_map/all_to_all | solution.py:318
  16.3 4.2 %all_gather.12 = bf16[112,512]{1,0:T(8,128)(2,1)S(1)} all-gather(bf16[56,512]{1,0:T(8,128)(2,1)S(1)} %bitcast.21), channel_id=1, replica_groups=mesh['dp_0'=4,'dp_1'=4,'dp_2'=2,'expert'=16] {'dp_2'}, dimensions={0}, use_global_device_ids=true | all-gather | bytes 172032 | tf_op jit(solution)/shard_map/all_gather | solution.py:321
  20.5 15.7 %all_gather.13 = bf16[448,512]{1,0:T(8,128)(2,1)S(1)} all-gather(bf16[112,512]{1,0:T(8,128)(2,1)S(1)} %all_gather.12), channel_id=1, replica_groups=mesh['dp_0'=4,'dp_1'=4,'dp_2'=2,'expert'=16] {'dp_1'}, dimensions={0}, use_global_device_ids=true | all-gather | bytes 573440 | tf_op jit(solution)/shard_map/all_gather | solution.py:321
  36.2 12.3 %all_gather.14.refs_1_.weight_0 = bf16[1792,256]{1,0:T(8,128)(2,1)S(1)} all-gather(bf16[448,256]{1,0:T(8,128)(2,1)S(1)} %get-tuple-element.36), channel_id=1, replica_groups=mesh['dp_0'=4,'dp_1'=4,'dp_2'=2,'expert'=16] {'dp_0'}, dimensions={0}, use_global_device_ids=true | all-gather | bytes 1146880 | tf_op jit(solution)/shard_map/all_gather | solution.py:323
  48.5 13.5 %all_gather.15.refs_2_.weight_1 = bf16[1792,256]{1,0:T(8,128)(2,1)} all-gather(bf16[448,256]{1,0:T(8,128)(2,1)S(1)} %get-tuple-element.35), channel_id=1, replica_groups=mesh['dp_0'=4,'dp_1'=4,'dp_2'=2,'expert'=16] {'dp_0'}, dimensions={0}, use_global_device_ids=true | all-gather | bytes 1146880 | tf_op jit(solution)/shard_map/all_gather | solution.py:324
  62.0 8.6 %all-to-all-done = bf16[16,32,2304]{2,1,0:T(8,128)(2,1)S(1)} async-done(((bf16[16,32,2304]{2,1,0:T(8,128)(2,1)}), bf16[16,32,2304]{2,1,0:T(8,128)(2,1)S(1)}, u32[]{:S(2)}, u32[]{:S(2)}) %all-to-all-start) | async-done | bytes 2359328 | tf_op jit(solution)/shard_map/all_to_all | solution.py:318
  70.5 6.2 %shard_map.95 = (bf16[512,512]{1,0:T(8,128)(2,1)}, f32[32,14,128]{2,1,0:T(8,128)}) custom-call(bf16[512,2304]{1,0:T(8,128)(2,1)S(1)} %bitcast.11, bf16[1792,256]{1,0:T(8,128)(2,1)S(1)} %all_gather.14.refs_1_.weight_0, bf16[1792,256]{1,0:T(8,128)(2,1)} %all_gather.15.refs_2_.weight_1, bf16[1792,512]{1,0:T(8,128)(2,1)} %bitcast.19, f32[512,32]{1,0:T(8,128)S(1)} %bitcast.14), custom_call_target="tpu_custom_call" | custom-call | tf_op jit(solution)/shard_map/pallas_call | solution.py:39
  76.8 9.7 %all-to-all-start.1 = ((f32[32,14,128]{2,1,0:T(8,128)}), f32[32,14,128]{2,1,0:T(8,128)S(1)}, u32[]{:S(2)}, u32[]{:S(2)}) async-start(f32[32,14,128]{2,1,0:T(8,128)} %get-tuple-element.21), calls=%async_computation.1 | async-start | bytes 524288 | tf_op jit(solution)/shard_map/all_to_all | solution.py:343
  86.5 1.0 copy-done.1
  87.5 4.0 %shard_map.96.merged_hbm.refs_3_ = bf16[1792,512]{1,0:T(8,128)(2,1)} custom-call(bf16[512,2304]{1,0:T(8,128)(2,1)S(1)} %bitcast.12, bf16[512,512]{1,0:T(8,128)(2,1)S(1)} %copy-done.1, bf16[1792,512]{1,0:T(8,128)(2,1)} %bitcast.20), custom_call_target="tpu_custom_call" | custom-call | tf_op jit(solution)/shard_map/pallas_call | solution.py:39
  91.6 4.6 %all-to-all-done.1.parts_ref = f32[32,14,128]{2,1,0:T(8,128)S(1)} async-done(((f32[32,14,128]{2,1,0:T(8,128)}), f32[32,14,128]{2,1,0:T(8,128)S(1)}, u32[]{:S(2)}, u32[]{:S(2)}) %all-to-all-start.1) | async-done | bytes 229408 | tf_op jit(solution)/shard_map/all_to_all | solution.py:343
  96.9 6.3 %all-to-all-start.2 = ((f32[32,14,128]{2,1,0:T(8,128)}), f32[32,14,128]{2,1,0:T(8,128)S(1)}, u32[]{:S(2)}, u32[]{:S(2)}) async-start(f32[32,14,128]{2,1,0:T(8,128)} %shard_map.97), calls=%async_computation.2 | async-start | bytes 524288 | tf_op jit(solution)/shard_map/all_to_all | solution.py:371
  103.2 1.2 copy-done
  104.4 1.0 copy-done.2
  105.4 2.1 %shard_map.98 = bf16[512,1792]{1,0:T(8,128)(2,1)} custom-call(bf16[512,512]{1,0:T(8,128)(2,1)S(1)} %copy-done.2, bf16[1792,256]{1,0:T(8,128)(2,1)S(1)} %all_gather.14.refs_1_.weight_0, bf16[1792,256]{1,0:T(8,128)(2,1)S(1)} %copy-done), custom_call_target="tpu_custom_call" | custom-call | tf_op jit(solution)/shard_map/pallas_call | solution.py:39
  107.6 5.3 %all-to-all-done.2.factor_ref = f32[32,14,128]{2,1,0:T(8,128)S(1)} async-done(((f32[32,14,128]{2,1,0:T(8,128)}), f32[32,14,128]{2,1,0:T(8,128)S(1)}, u32[]{:S(2)}, u32[]{:S(2)}) %all-to-all-start.2) | async-done | bytes 229408 | tf_op jit(solution)/shard_map/all_to_all | solution.py:371
  112.9 8.7 %all-to-all-start.3 = ((bf16[16,32,1792]{2,1,0:T(8,128)(2,1)}), bf16[16,32,1792]{2,1,0:T(8,128)(2,1)S(1)}, u32[]{:S(2)}, u32[]{:S(2)}) async-start(bf16[16,32,1792]{2,1,0:T(8,128)(2,1)} %bitcast.18), calls=%async_computation.3 | async-start | bytes 3670016 | tf_op jit(solution)/shard_map/all_to_all | solution.py:373
  121.6 1.7 %shard_map.99 = f32[32,512]{1,0:T(8,128)S(1)} custom-call(f32[32,14,128]{2,1,0:T(8,128)S(1)} %all-to-all-done.2.factor_ref, bf16[1792,512]{1,0:T(8,128)(2,1)} %shard_map.96.merged_hbm.refs_3_), custom_call_target="tpu_custom_call" | custom-call | tf_op jit(solution)/shard_map/pallas_call | solution.py:39
  123.2 3.4 %collective-permute-start = (f32[32,512]{1,0:T(8,128)S(1)}, f32[32,512]{1,0:T(8,128)S(1)}, u32[]{:S(2)}, u32[]{:S(2)}) collective-permute-start(f32[32,512]{1,0:T(8,128)S(1)} %shard_map.99), channel_id=1, source_target_pairs={{0,16},{16,0},{32,48},{48,32},{64,80},{80,64},{96,112},{112,96},{1... | collective-permute-start | bytes 196616 | tf_op jit(solution)/shard_map/ppermute | solution.py:287
  126.6 2.2 %collective-permute-done = f32[32,512]{1,0:T(8,128)S(1)} collective-permute-done((f32[32,512]{1,0:T(8,128)S(1)}, f32[32,512]{1,0:T(8,128)S(1)}, u32[]{:S(2)}, u32[]{:S(2)}) %collective-permute-start) | collective-permute-done | bytes 65568 | tf_op jit(solution)/shard_map/ppermute | solution.py:287
  128.8 3.5 %collective-permute-start.1 = (f32[32,512]{1,0:T(8,128)S(1)}, f32[32,512]{1,0:T(8,128)S(1)}, u32[]{:S(2)}, u32[]{:S(2)}) collective-permute-start(f32[32,512]{1,0:T(8,128)S(1)} %add.24), channel_id=1, source_target_pairs={{0,32},{16,48},{32,0},{48,16},{64,96},{80,112},{96,64},{112,80},{1... | collective-permute-start | bytes 196616 | tf_op jit(solution)/shard_map/ppermute | solution.py:287
  132.6 2.4 %collective-permute-done.1 = f32[32,512]{1,0:T(8,128)S(1)} collective-permute-done((f32[32,512]{1,0:T(8,128)S(1)}, f32[32,512]{1,0:T(8,128)S(1)}, u32[]{:S(2)}, u32[]{:S(2)}) %collective-permute-start.1) | collective-permute-done | bytes 65568 | tf_op jit(solution)/shard_map/ppermute | solution.py:287
  135.0 2.5 %collective-permute-start.2 = (f32[32,512]{1,0:T(8,128)S(1)}, f32[32,512]{1,0:T(8,128)S(1)}, u32[]{:S(2)}, u32[]{:S(2)}) collective-permute-start(f32[32,512]{1,0:T(8,128)S(1)} %add.25), channel_id=1, source_target_pairs={{0,112},{16,96},{32,80},{48,64},{64,48},{80,32},{96,16},{112,0},{1... | collective-permute-start | bytes 196616 | tf_op jit(solution)/shard_map/ppermute | solution.py:287
  137.6 4.0 %shard_map.102.refs_1_ = bf16[1792,96]{1,0:T(8,128)(2,1)S(1)} custom-call(f32[32,14,128]{2,1,0:T(8,128)S(1)} %all-to-all-done.2.factor_ref), custom_call_target="tpu_custom_call" | custom-call | tf_op jit(solution)/shard_map/pallas_call | solution.py:39
  141.6 2.2 %collective-permute-start.3 = (f32[32,512]{1,0:T(8,128)S(1)}, f32[32,512]{1,0:T(8,128)S(1)}, u32[]{:S(2)}, u32[]{:S(2)}) collective-permute-start(f32[32,512]{1,0:T(8,128)S(1)} %add.26), channel_id=1, source_target_pairs={{0,128},{128,0},{256,384},{384,256},{1,129},{129,1},{257,385},{385... | collective-permute-start | bytes 196616 | tf_op jit(solution)/shard_map/ppermute | solution.py:287
  144.5 2.4 %collective-permute-done.3 = f32[32,512]{1,0:T(8,128)S(1)} collective-permute-done((f32[32,512]{1,0:T(8,128)S(1)}, f32[32,512]{1,0:T(8,128)S(1)}, u32[]{:S(2)}, u32[]{:S(2)}) %collective-permute-start.3) | collective-permute-done | bytes 65568 | tf_op jit(solution)/shard_map/ppermute | solution.py:287
  146.9 3.1 %collective-permute-start.4 = (f32[32,512]{1,0:T(8,128)S(1)}, f32[32,512]{1,0:T(8,128)S(1)}, u32[]{:S(2)}, u32[]{:S(2)}) collective-permute-start(f32[32,512]{1,0:T(8,128)S(1)} %add.30), channel_id=1, source_target_pairs={{0,384},{128,256},{256,128},{384,0},{1,385},{129,257},{257,129},{3... | collective-permute-start | bytes 196616 | tf_op jit(solution)/shard_map/ppermute | solution.py:287
  150.2 3.3 %collective-permute-done.4 = f32[32,512]{1,0:T(8,128)S(1)} collective-permute-done((f32[32,512]{1,0:T(8,128)S(1)}, f32[32,512]{1,0:T(8,128)S(1)}, u32[]{:S(2)}, u32[]{:S(2)}) %collective-permute-start.4) | collective-permute-done | bytes 65568 | tf_op jit(solution)/shard_map/ppermute | solution.py:287
  154.1 4.8 %shard_map.103 = (bf16[1792,512]{1,0:T(8,128)(2,1)}, f32[56,512]{1,0:T(8,128)}) custom-call(f32[32,512]{1,0:T(8,128)} %add.31.refs_0_, bf16[1792,96]{1,0:T(8,128)(2,1)} %copy-done.3, bf16[56,96]{1,0:T(8,128)(2,1)} %constant_dynamic-slice_fusion.refs_2_, bf16[1792,512]{1,0:T(8,128)(2,1)} %shard_map.96.merged_hbm.refs_3_), custom_call_target="tpu_custom_call" | custom-call | tf_op jit(solution)/shard_map/pallas_call | solution.py:39
  158.9 6.3 %all-to-all-done.3 = bf16[16,32,1792]{2,1,0:T(8,128)(2,1)S(1)} async-done(((bf16[16,32,1792]{2,1,0:T(8,128)(2,1)}), bf16[16,32,1792]{2,1,0:T(8,128)(2,1)S(1)}, u32[]{:S(2)}, u32[]{:S(2)}) %all-to-all-start.3) | async-done | bytes 1835040 | tf_op jit(solution)/shard_map/all_to_all | solution.py:373
  165.2 1.4 shard_map.101
  (25 shorter events, 2.6 us)
Async XLA Ops:
  4.2 12.0 %copy-start.5 = (f32[1,512,32]{1,2,0:T(8,128)S(1)}, f32[1,512,32]{1,2,0:T(8,128)}, u32[]{:S(2)}) copy-start(f32[1,512,32]{1,2,0:T(8,128)} %param.13) | copy-start | bytes 196612
  4.2 12.1 %copy-start.6 = (bf16[1,56,512]{2,1,0:T(8,128)(2,1)S(1)}, bf16[1,56,512]{2,1,0:T(8,128)(2,1)}, u32[]{:S(2)}) copy-start(bf16[1,56,512]{2,1,0:T(8,128)(2,1)} %param.11) | copy-start | bytes 172036
  4.2 66.3 %all-to-all-start = ((bf16[16,32,2304]{2,1,0:T(8,128)(2,1)}), bf16[16,32,2304]{2,1,0:T(8,128)(2,1)S(1)}, u32[]{:S(2)}, u32[]{:S(2)}) async-start(bf16[16,32,2304]{2,1,0:T(8,128)(2,1)} %bitcast.17), calls=%async_computation | async-start | bytes 4718592 | tf_op jit(solution)/shard_map/all_to_all | solution.py:318
  76.8 19.4 %all-to-all-start.1 = ((f32[32,14,128]{2,1,0:T(8,128)}), f32[32,14,128]{2,1,0:T(8,128)S(1)}, u32[]{:S(2)}, u32[]{:S(2)}) async-start(f32[32,14,128]{2,1,0:T(8,128)} %get-tuple-element.21), calls=%async_computation.1 | async-start | bytes 524288 | tf_op jit(solution)/shard_map/all_to_all | solution.py:343
  86.5 1.0 copy-start.1
  96.9 16.0 %all-to-all-start.2 = ((f32[32,14,128]{2,1,0:T(8,128)}), f32[32,14,128]{2,1,0:T(8,128)S(1)}, u32[]{:S(2)}, u32[]{:S(2)}) async-start(f32[32,14,128]{2,1,0:T(8,128)} %shard_map.97), calls=%async_computation.2 | async-start | bytes 524288 | tf_op jit(solution)/shard_map/all_to_all | solution.py:371
  103.2 1.2 copy-start
  104.4 1.0 copy-start.2
  112.9 52.3 %all-to-all-start.3 = ((bf16[16,32,1792]{2,1,0:T(8,128)(2,1)}), bf16[16,32,1792]{2,1,0:T(8,128)(2,1)S(1)}, u32[]{:S(2)}, u32[]{:S(2)}) async-start(bf16[16,32,1792]{2,1,0:T(8,128)(2,1)} %bitcast.18), calls=%async_computation.3 | async-start | bytes 3670016 | tf_op jit(solution)/shard_map/all_to_all | solution.py:373
  121.6 10.8 %copy-start.4 = (s32[128,2]{0,1:T(2,128)S(1)}, s32[128,2]{0,1:T(2,128)}, u32[]{:S(2)}) copy-start(s32[128,2]{0,1:T(2,128)} %param.8) | copy-start | bytes 3076
  121.6 28.5 %copy-start.7 = (f32[128,2]{0,1:T(2,128)S(1)}, f32[128,2]{0,1:T(2,128)}, u32[]{:S(2)}) copy-start(f32[128,2]{0,1:T(2,128)} %param.9) | copy-start | bytes 3076
  123.2 5.6 %collective-permute-start = (f32[32,512]{1,0:T(8,128)S(1)}, f32[32,512]{1,0:T(8,128)S(1)}, u32[]{:S(2)}, u32[]{:S(2)}) collective-permute-start(f32[32,512]{1,0:T(8,128)S(1)} %shard_map.99), channel_id=1, source_target_pairs={{0,16},{16,0},{32,48},{48,32},{64,80},{80,64},{96,112},{112,96},{1... | collective-permute-start | bytes 196616 | tf_op jit(solution)/shard_map/ppermute | solution.py:287
  128.8 6.2 %collective-permute-start.1 = (f32[32,512]{1,0:T(8,128)S(1)}, f32[32,512]{1,0:T(8,128)S(1)}, u32[]{:S(2)}, u32[]{:S(2)}) collective-permute-start(f32[32,512]{1,0:T(8,128)S(1)} %add.24), channel_id=1, source_target_pairs={{0,32},{16,48},{32,0},{48,16},{64,96},{80,112},{96,64},{112,80},{1... | collective-permute-start | bytes 196616 | tf_op jit(solution)/shard_map/ppermute | solution.py:287
  135.0 6.6 %collective-permute-start.2 = (f32[32,512]{1,0:T(8,128)S(1)}, f32[32,512]{1,0:T(8,128)S(1)}, u32[]{:S(2)}, u32[]{:S(2)}) collective-permute-start(f32[32,512]{1,0:T(8,128)S(1)} %add.25), channel_id=1, source_target_pairs={{0,112},{16,96},{32,80},{48,64},{64,48},{80,32},{96,16},{112,0},{1... | collective-permute-start | bytes 196616 | tf_op jit(solution)/shard_map/ppermute | solution.py:287
  141.6 12.5 %copy-start.3 = (bf16[1792,96]{1,0:T(8,128)(2,1)}, bf16[1792,96]{1,0:T(8,128)(2,1)S(1)}, u32[]{:S(2)}) copy-start(bf16[1792,96]{1,0:T(8,128)(2,1)S(1)} %shard_map.102.refs_1_) | copy-start | bytes 1032196
  141.6 5.3 %collective-permute-start.3 = (f32[32,512]{1,0:T(8,128)S(1)}, f32[32,512]{1,0:T(8,128)S(1)}, u32[]{:S(2)}, u32[]{:S(2)}) collective-permute-start(f32[32,512]{1,0:T(8,128)S(1)} %add.26), channel_id=1, source_target_pairs={{0,128},{128,0},{256,384},{384,256},{1,129},{129,1},{257,385},{385... | collective-permute-start | bytes 196616 | tf_op jit(solution)/shard_map/ppermute | solution.py:287
  146.9 6.5 %collective-permute-start.4 = (f32[32,512]{1,0:T(8,128)S(1)}, f32[32,512]{1,0:T(8,128)S(1)}, u32[]{:S(2)}, u32[]{:S(2)}) collective-permute-start(f32[32,512]{1,0:T(8,128)S(1)} %add.30), channel_id=1, source_target_pairs={{0,384},{128,256},{256,128},{384,0},{1,385},{129,257},{257,129},{3... | collective-permute-start | bytes 196616 | tf_op jit(solution)/shard_map/ppermute | solution.py:287

commit v9 on v6

--- a/solution.py
+++ b/solution.py
@@ -6,8 +6,8 @@
 from jax.sharding import Mesh
 from jax.sharding import PartitionSpec as P
 
-DP = ("dp_0", "dp_1")
-DP_EXPERT = ("dp_0", "dp_1", "expert")
+DP = ("dp_0", "dp_1", "dp_2")
+DP_EXPERT = ("dp_0", "dp_1", "dp_2", "expert")
 
 f32, bf16 = jnp.float32, jnp.bfloat16
 HBM = pl.BlockSpec(memory_space=pltpu.HBM)
@@ -315,7 +315,7 @@
     arrived = lax.all_to_all(
         sent.reshape(experts, capacity, width + hidden), "expert", 0, 0, tiled=True
     ).reshape(slots, width + hidden)
-    weight = lax.all_gather(w_mine, DP[1], tiled=True)
+    weight = lax.all_gather(lax.all_gather(w_mine, DP[2], tiled=True), DP[1], tiled=True)
     half = hidden // 2
     weight_0 = lax.all_gather(weight[:, :half], DP[0], tiled=True)
     weight_1 = lax.all_gather(weight[:, half:], DP[0], tiled=True)
@@ -390,7 +390,7 @@
         shape((2 * row_count, slots), bf16),
         (routes_t,),
     )
-    steps = [(axis, step) for axis in DP[::-1] for step in partners(lax.axis_size(axis))]
+    steps = [(axis, step) for axis in (DP[1:], DP[0]) for step in partners(lax.axis_size(axis))]
     for i, (axis, step) in enumerate(steps):
         other = from_partner(right, axis, step)
         if i == len(steps) - 4:
@@ -426,7 +426,7 @@
 
 
 def solution(mesh):
-    torus = Mesh(mesh.devices.reshape(4, 8, mesh.shape["expert"]), DP_EXPERT)
+    torus = Mesh(mesh.devices.reshape(4, 4, 2, mesh.shape["expert"]), DP_EXPERT)
     in_specs = (
         P(DP_EXPERT, None),
         P(DP_EXPERT, None),

time: 166 us -> 166 us (level)
  waiting for transfers between devices: 23 us -> 26.3 us
  blocking collectives: 67.7 us -> 64.8 us
    all_to_all x1, waiting for transfers between devices: 5.64 us -> 8.55 us  [body(): lax.all_to_all(sent.reshape(experts, capacity, width + hidden), 'expert',...]
    all_gather x1 -> x2, blocking collectives: 22.6 us -> 19.8 us  [the longest x1 15.7 us: body(): lax.all_gather(lax.all_gather(w_mine, DP[2], tiled=True), DP[1], tiled=True)]
  transfers between devices with their start and end apart: 8 -> 8, of which waited for: 8 -> 7; matrix products, arithmetic and copies ran while one was open for 1% -> 1% of each run, Pallas kernels for 10% -> 10%
where the time goes in v9:
time: 166 us
  blocking collectives  64.8 us (39%)
  starting transfers between devices  41.8 us (25%)
  Pallas kernels  27.5 us (17%)
  waiting for transfers between devices  26.3 us (16%)
  local copies, waits for them, and re-layouts  3.81 us (2%)
    pallas_call x10, Pallas kernels, call(): pl.pallas_call(kernel, out_shape=outs, compiler_params=pltpu.CompilerPara...  27.5 us
    all_to_all x1, blocking collectives, body(): parts = lax.all_to_all(factor, DP, 0, 0, tiled=True)  19.2 us
    all_gather x1, blocking collectives, body(): lax.all_gather(lax.all_gather(w_mine, DP[2], tiled=True), DP[1], tiled=True)  15.7 us
    ppermute x5, starting transfers between devices, from_partner(): lax.ppermute(x, axis, [(i, i ^ step) for i in range(lax.axis_size(axis))])  14.8 us
    all_gather x1, blocking collectives, body(): weight_1 = lax.all_gather(weight[:, half:], DP[0], tiled=True)  13.5 us
    all_gather x1, blocking collectives, body(): weight_0 = lax.all_gather(weight[:, :half], DP[0], tiled=True)  12.3 us
    all_to_all x1, starting transfers between devices, body(): lax.all_to_all(sent.reshape(experts, capacity, width + hidden), 'expert',...  12 us
    ppermute x5, waiting for transfers between devices, from_partner(): lax.ppermute(x, axis, [(i, i ^ step) for i in range(lax.axis_size(axis))])  10.2 us
  transfers between devices with their start and end apart: 8, of which 7 were waited for; matrix products, arithmetic and copies ran while one was open for 1% of the time, Pallas kernels for 10%

profile of v9, /device:TPU:1, one launch (start us, length us, event | category | flops | bytes accessed | tf_op | source)
XLA Modules:
  0.0 165.7 jit_solution(359551633143797291)
XLA Ops:
  0.6 3.6 %shard_map.94 = bf16[512,2304]{1,0:T(8,128)(2,1)} custom-call(s32[2,128]{1,0:T(2,128)} %bitcast.15, f32[2,128]{1,0:T(2,128)} %bitcast.22, bf16[128,1792]{1,0:T(8,128)(2,1)} %refs_2_.1, bf16[128,2,512]{2,1,0:T(2,128)(2,1)} %refs_3_.1), custom_call_target="tpu_custom_call" | custom-call | tf_op jit(solution)/shard_map/pallas_call | solution.py:39
  4.2 12.0 %all-to-all-start = ((bf16[16,32,2304]{2,1,0:T(8,128)(2,1)}), bf16[16,32,2304]{2,1,0:T(8,128)(2,1)S(1)}, u32[]{:S(2)}, u32[]{:S(2)}) async-start(bf16[16,32,2304]{2,1,0:T(8,128)(2,1)} %bitcast.17), calls=%async_computation | async-start | bytes 4718592 | tf_op jit(solution)/shard_map/all_to_all | solution.py:315
  16.3 4.2 %all_gather.12 = bf16[112,512]{1,0:T(8,128)(2,1)S(1)} all-gather(bf16[56,512]{1,0:T(8,128)(2,1)S(1)} %bitcast.21), channel_id=1, replica_groups=mesh['dp_0'=4,'dp_1'=4,'dp_2'=2,'expert'=16] {'dp_2'}, dimensions={0}, use_global_device_ids=true | all-gather | bytes 172032 | tf_op jit(solution)/shard_map/all_gather | solution.py:318
  20.5 15.7 %all_gather.13 = bf16[448,512]{1,0:T(8,128)(2,1)S(1)} all-gather(bf16[112,512]{1,0:T(8,128)(2,1)S(1)} %all_gather.12), channel_id=1, replica_groups=mesh['dp_0'=4,'dp_1'=4,'dp_2'=2,'expert'=16] {'dp_1'}, dimensions={0}, use_global_device_ids=true | all-gather | bytes 573440 | tf_op jit(solution)/shard_map/all_gather | solution.py:318
  36.2 12.3 %all_gather.14.refs_1_.weight_0 = bf16[1792,256]{1,0:T(8,128)(2,1)S(1)} all-gather(bf16[448,256]{1,0:T(8,128)(2,1)S(1)} %get-tuple-element.34), channel_id=1, replica_groups=mesh['dp_0'=4,'dp_1'=4,'dp_2'=2,'expert'=16] {'dp_0'}, dimensions={0}, use_global_device_ids=true | all-gather | bytes 1146880 | tf_op jit(solution)/shard_map/all_gather | solution.py:320
  48.5 13.5 %all_gather.15.refs_2_.weight_1 = bf16[1792,256]{1,0:T(8,128)(2,1)} all-gather(bf16[448,256]{1,0:T(8,128)(2,1)S(1)} %get-tuple-element.33), channel_id=1, replica_groups=mesh['dp_0'=4,'dp_1'=4,'dp_2'=2,'expert'=16] {'dp_0'}, dimensions={0}, use_global_device_ids=true | all-gather | bytes 1146880 | tf_op jit(solution)/shard_map/all_gather | solution.py:321
  62.0 8.6 %all-to-all-done = bf16[16,32,2304]{2,1,0:T(8,128)(2,1)S(1)} async-done(((bf16[16,32,2304]{2,1,0:T(8,128)(2,1)}), bf16[16,32,2304]{2,1,0:T(8,128)(2,1)S(1)}, u32[]{:S(2)}, u32[]{:S(2)}) %all-to-all-start) | async-done | bytes 2359328 | tf_op jit(solution)/shard_map/all_to_all | solution.py:315
  70.6 5.6 %shard_map.95 = (bf16[512,512]{1,0:T(8,128)(2,1)}, f32[32,14,128]{2,1,0:T(8,128)S(1)}) custom-call(bf16[512,2304]{1,0:T(8,128)(2,1)S(1)} %bitcast.11, bf16[1792,256]{1,0:T(8,128)(2,1)S(1)} %all_gather.14.refs_1_.weight_0, bf16[1792,256]{1,0:T(8,128)(2,1)} %all_gather.15.refs_2_.weight_1, bf16[1792,512]{1,0:T(8,128)(2,1)} %bitcast.19, f32[512,32]{1,0:T(8,128)S(1)} %bitcast.14), custom_call_target="tpu_custom_call" | custom-call | tf_op jit(solution)/shard_map/pallas_call | solution.py:39
  76.1 19.2 %all_to_all.20.parts_ref = f32[32,14,128]{2,1,0:T(8,128)S(1)} all-to-all(f32[32,14,128]{2,1,0:T(8,128)S(1)} %get-tuple-element.20), channel_id=1, replica_groups=mesh['dp_0'=4,'dp_1'=4,'dp_2'=2,'expert'=16] {'dp_0','dp_1','dp_2'}, dimensions={0} | all-to-all | bytes 458752 | tf_op jit(solution)/shard_map/all_to_all | solution.py:339
  95.3 0.7 copy-done.3
  96.0 6.3 %all-to-all-start.2 = ((f32[32,14,128]{2,1,0:T(8,128)}), f32[32,14,128]{2,1,0:T(8,128)S(1)}, u32[]{:S(2)}, u32[]{:S(2)}) async-start(f32[32,14,128]{2,1,0:T(8,128)} %copy-done.3), calls=%async_computation.2 | async-start | bytes 524288 | tf_op jit(solution)/shard_map/all_to_all | solution.py:366
  102.3 1.2 copy-done
  103.5 1.0 copy-done.1
  104.5 2.1 %shard_map.97 = bf16[512,1792]{1,0:T(8,128)(2,1)} custom-call(bf16[512,512]{1,0:T(8,128)(2,1)S(1)} %copy-done.1, bf16[1792,256]{1,0:T(8,128)(2,1)S(1)} %all_gather.14.refs_1_.weight_0, bf16[1792,256]{1,0:T(8,128)(2,1)S(1)} %copy-done), custom_call_target="tpu_custom_call" | custom-call | tf_op jit(solution)/shard_map/pallas_call | solution.py:39
  106.7 4.0 %shard_map.98.merged_hbm.refs_3_ = bf16[1792,512]{1,0:T(8,128)(2,1)} custom-call(bf16[512,2304]{1,0:T(8,128)(2,1)S(1)} %bitcast.12, bf16[512,512]{1,0:T(8,128)(2,1)S(1)} %copy-done.1, bf16[1792,512]{1,0:T(8,128)(2,1)} %bitcast.20), custom_call_target="tpu_custom_call" | custom-call | tf_op jit(solution)/shard_map/pallas_call | solution.py:39
  110.8 1.2 all-to-all-done.2.factor_ref
  112.0 8.7 %all-to-all-start.3 = ((bf16[16,32,1792]{2,1,0:T(8,128)(2,1)}), bf16[16,32,1792]{2,1,0:T(8,128)(2,1)S(1)}, u32[]{:S(2)}, u32[]{:S(2)}) async-start(bf16[16,32,1792]{2,1,0:T(8,128)(2,1)} %bitcast.18), calls=%async_computation.3 | async-start | bytes 3670016 | tf_op jit(solution)/shard_map/all_to_all | solution.py:368
  120.7 1.7 %shard_map.99 = f32[32,512]{1,0:T(8,128)S(1)} custom-call(f32[32,14,128]{2,1,0:T(8,128)S(1)} %all-to-all-done.2.factor_ref, bf16[1792,512]{1,0:T(8,128)(2,1)} %shard_map.98.merged_hbm.refs_3_), custom_call_target="tpu_custom_call" | custom-call | tf_op jit(solution)/shard_map/pallas_call | solution.py:39
  122.4 3.4 %collective-permute-start = (f32[32,512]{1,0:T(8,128)S(1)}, f32[32,512]{1,0:T(8,128)S(1)}, u32[]{:S(2)}, u32[]{:S(2)}) collective-permute-start(f32[32,512]{1,0:T(8,128)S(1)} %shard_map.99), channel_id=1, source_target_pairs={{0,16},{16,0},{32,48},{48,32},{64,80},{80,64},{96,112},{112,96},{1... | collective-permute-start | bytes 196616 | tf_op jit(solution)/shard_map/ppermute | solution.py:284
  125.7 2.2 %collective-permute-done = f32[32,512]{1,0:T(8,128)S(1)} collective-permute-done((f32[32,512]{1,0:T(8,128)S(1)}, f32[32,512]{1,0:T(8,128)S(1)}, u32[]{:S(2)}, u32[]{:S(2)}) %collective-permute-start) | collective-permute-done | bytes 65568 | tf_op jit(solution)/shard_map/ppermute | solution.py:284
  127.9 3.5 %collective-permute-start.1 = (f32[32,512]{1,0:T(8,128)S(1)}, f32[32,512]{1,0:T(8,128)S(1)}, u32[]{:S(2)}, u32[]{:S(2)}) collective-permute-start(f32[32,512]{1,0:T(8,128)S(1)} %add.24), channel_id=1, source_target_pairs={{0,32},{16,48},{32,0},{48,16},{64,96},{80,112},{96,64},{112,80},{1... | collective-permute-start | bytes 196616 | tf_op jit(solution)/shard_map/ppermute | solution.py:284
  131.8 2.4 %collective-permute-done.1 = f32[32,512]{1,0:T(8,128)S(1)} collective-permute-done((f32[32,512]{1,0:T(8,128)S(1)}, f32[32,512]{1,0:T(8,128)S(1)}, u32[]{:S(2)}, u32[]{:S(2)}) %collective-permute-start.1) | collective-permute-done | bytes 65568 | tf_op jit(solution)/shard_map/ppermute | solution.py:284
  134.1 2.5 %collective-permute-start.2 = (f32[32,512]{1,0:T(8,128)S(1)}, f32[32,512]{1,0:T(8,128)S(1)}, u32[]{:S(2)}, u32[]{:S(2)}) collective-permute-start(f32[32,512]{1,0:T(8,128)S(1)} %add.25), channel_id=1, source_target_pairs={{0,112},{16,96},{32,80},{48,64},{64,48},{80,32},{96,16},{112,0},{1... | collective-permute-start | bytes 196616 | tf_op jit(solution)/shard_map/ppermute | solution.py:284
  136.7 4.0 %shard_map.102.refs_1_ = bf16[1792,96]{1,0:T(8,128)(2,1)S(1)} custom-call(f32[32,14,128]{2,1,0:T(8,128)S(1)} %all-to-all-done.2.factor_ref), custom_call_target="tpu_custom_call" | custom-call | tf_op jit(solution)/shard_map/pallas_call | solution.py:39
  140.7 2.2 %collective-permute-start.3 = (f32[32,512]{1,0:T(8,128)S(1)}, f32[32,512]{1,0:T(8,128)S(1)}, u32[]{:S(2)}, u32[]{:S(2)}) collective-permute-start(f32[32,512]{1,0:T(8,128)S(1)} %add.26), channel_id=1, source_target_pairs={{0,128},{128,0},{256,384},{384,256},{1,129},{129,1},{257,385},{385... | collective-permute-start | bytes 196616 | tf_op jit(solution)/shard_map/ppermute | solution.py:284
  143.5 2.5 %collective-permute-done.3 = f32[32,512]{1,0:T(8,128)S(1)} collective-permute-done((f32[32,512]{1,0:T(8,128)S(1)}, f32[32,512]{1,0:T(8,128)S(1)}, u32[]{:S(2)}, u32[]{:S(2)}) %collective-permute-start.3) | collective-permute-done | bytes 65568 | tf_op jit(solution)/shard_map/ppermute | solution.py:284
  146.0 3.3 %collective-permute-start.4 = (f32[32,512]{1,0:T(8,128)S(1)}, f32[32,512]{1,0:T(8,128)S(1)}, u32[]{:S(2)}, u32[]{:S(2)}) collective-permute-start(f32[32,512]{1,0:T(8,128)S(1)} %add.30), channel_id=1, source_target_pairs={{0,384},{128,256},{256,128},{384,0},{1,385},{129,257},{257,129},{3... | collective-permute-start | bytes 196616 | tf_op jit(solution)/shard_map/ppermute | solution.py:284
  149.4 3.1 %collective-permute-done.4 = f32[32,512]{1,0:T(8,128)S(1)} collective-permute-done((f32[32,512]{1,0:T(8,128)S(1)}, f32[32,512]{1,0:T(8,128)S(1)}, u32[]{:S(2)}, u32[]{:S(2)}) %collective-permute-start.4) | collective-permute-done | bytes 65568 | tf_op jit(solution)/shard_map/ppermute | solution.py:284
  152.6 0.6 add.31.refs_0_
  153.2 4.8 %shard_map.103 = (bf16[1792,512]{1,0:T(8,128)(2,1)}, f32[56,512]{1,0:T(8,128)}) custom-call(f32[32,512]{1,0:T(8,128)} %add.31.refs_0_, bf16[1792,96]{1,0:T(8,128)(2,1)} %copy-done.2, bf16[56,96]{1,0:T(8,128)(2,1)} %constant_dynamic-slice_fusion.refs_2_, bf16[1792,512]{1,0:T(8,128)(2,1)} %shard_map.98.merged_hbm.refs_3_), custom_call_target="tpu_custom_call" | custom-call | tf_op jit(solution)/shard_map/pallas_call | solution.py:39
  158.0 6.3 %all-to-all-done.3 = bf16[16,32,1792]{2,1,0:T(8,128)(2,1)S(1)} async-done(((bf16[16,32,1792]{2,1,0:T(8,128)(2,1)}), bf16[16,32,1792]{2,1,0:T(8,128)(2,1)S(1)}, u32[]{:S(2)}, u32[]{:S(2)}) %all-to-all-start.3) | async-done | bytes 1835040 | tf_op jit(solution)/shard_map/all_to_all | solution.py:368
  164.3 1.4 shard_map.101
  (24 shorter events, 1.3 us)
Async XLA Ops:
  4.2 12.0 %copy-start.5 = (f32[1,512,32]{1,2,0:T(8,128)S(1)}, f32[1,512,32]{1,2,0:T(8,128)}, u32[]{:S(2)}) copy-start(f32[1,512,32]{1,2,0:T(8,128)} %param.13) | copy-start | bytes 196612
  4.2 12.1 %copy-start.6 = (bf16[1,56,512]{2,1,0:T(8,128)(2,1)S(1)}, bf16[1,56,512]{2,1,0:T(8,128)(2,1)}, u32[]{:S(2)}) copy-start(bf16[1,56,512]{2,1,0:T(8,128)(2,1)} %param.11) | copy-start | bytes 172036
  4.2 66.3 %all-to-all-start = ((bf16[16,32,2304]{2,1,0:T(8,128)(2,1)}), bf16[16,32,2304]{2,1,0:T(8,128)(2,1)S(1)}, u32[]{:S(2)}, u32[]{:S(2)}) async-start(bf16[16,32,2304]{2,1,0:T(8,128)(2,1)} %bitcast.17), calls=%async_computation | async-start | bytes 4718592 | tf_op jit(solution)/shard_map/all_to_all | solution.py:315
  95.3 0.7 copy-start.3
  96.0 16.0 %all-to-all-start.2 = ((f32[32,14,128]{2,1,0:T(8,128)}), f32[32,14,128]{2,1,0:T(8,128)S(1)}, u32[]{:S(2)}, u32[]{:S(2)}) async-start(f32[32,14,128]{2,1,0:T(8,128)} %copy-done.3), calls=%async_computation.2 | async-start | bytes 524288 | tf_op jit(solution)/shard_map/all_to_all | solution.py:366
  102.3 1.2 copy-start
  103.5 1.0 copy-start.1
  112.0 52.3 %all-to-all-start.3 = ((bf16[16,32,1792]{2,1,0:T(8,128)(2,1)}), bf16[16,32,1792]{2,1,0:T(8,128)(2,1)S(1)}, u32[]{:S(2)}, u32[]{:S(2)}) async-start(bf16[16,32,1792]{2,1,0:T(8,128)(2,1)} %bitcast.18), calls=%async_computation.3 | async-start | bytes 3670016 | tf_op jit(solution)/shard_map/all_to_all | solution.py:368
  120.7 10.8 %copy-start.4 = (s32[128,2]{0,1:T(2,128)S(1)}, s32[128,2]{0,1:T(2,128)}, u32[]{:S(2)}) copy-start(s32[128,2]{0,1:T(2,128)} %param.8) | copy-start | bytes 3076
  120.7 28.6 %copy-start.7 = (f32[128,2]{0,1:T(2,128)S(1)}, f32[128,2]{0,1:T(2,128)}, u32[]{:S(2)}) copy-start(f32[128,2]{0,1:T(2,128)} %param.9) | copy-start | bytes 3076
  122.4 5.5 %collective-permute-start = (f32[32,512]{1,0:T(8,128)S(1)}, f32[32,512]{1,0:T(8,128)S(1)}, u32[]{:S(2)}, u32[]{:S(2)}) collective-permute-start(f32[32,512]{1,0:T(8,128)S(1)} %shard_map.99), channel_id=1, source_target_pairs={{0,16},{16,0},{32,48},{48,32},{64,80},{80,64},{96,112},{112,96},{1... | collective-permute-start | bytes 196616 | tf_op jit(solution)/shard_map/ppermute | solution.py:284
  127.9 6.2 %collective-permute-start.1 = (f32[32,512]{1,0:T(8,128)S(1)}, f32[32,512]{1,0:T(8,128)S(1)}, u32[]{:S(2)}, u32[]{:S(2)}) collective-permute-start(f32[32,512]{1,0:T(8,128)S(1)} %add.24), channel_id=1, source_target_pairs={{0,32},{16,48},{32,0},{48,16},{64,96},{80,112},{96,64},{112,80},{1... | collective-permute-start | bytes 196616 | tf_op jit(solution)/shard_map/ppermute | solution.py:284
  134.1 6.6 %collective-permute-start.2 = (f32[32,512]{1,0:T(8,128)S(1)}, f32[32,512]{1,0:T(8,128)S(1)}, u32[]{:S(2)}, u32[]{:S(2)}) collective-permute-start(f32[32,512]{1,0:T(8,128)S(1)} %add.25), channel_id=1, source_target_pairs={{0,112},{16,96},{32,80},{48,64},{64,48},{80,32},{96,16},{112,0},{1... | collective-permute-start | bytes 196616 | tf_op jit(solution)/shard_map/ppermute | solution.py:284
  140.7 12.5 %copy-start.2 = (bf16[1792,96]{1,0:T(8,128)(2,1)}, bf16[1792,96]{1,0:T(8,128)(2,1)S(1)}, u32[]{:S(2)}) copy-start(bf16[1792,96]{1,0:T(8,128)(2,1)S(1)} %shard_map.102.refs_1_) | copy-start | bytes 1032196
  140.7 5.3 %collective-permute-start.3 = (f32[32,512]{1,0:T(8,128)S(1)}, f32[32,512]{1,0:T(8,128)S(1)}, u32[]{:S(2)}, u32[]{:S(2)}) collective-permute-start(f32[32,512]{1,0:T(8,128)S(1)} %add.26), channel_id=1, source_target_pairs={{0,128},{128,0},{256,384},{384,256},{1,129},{129,1},{257,385},{385... | collective-permute-start | bytes 196616 | tf_op jit(solution)/shard_map/ppermute | solution.py:284
  146.0 6.5 %collective-permute-start.4 = (f32[32,512]{1,0:T(8,128)S(1)}, f32[32,512]{1,0:T(8,128)S(1)}, u32[]{:S(2)}, u32[]{:S(2)}) collective-permute-start(f32[32,512]{1,0:T(8,128)S(1)} %add.30), channel_id=1, source_target_pairs={{0,384},{128,256},{256,128},{384,0},{1,385},{129,257},{257,129},{3... | collective-permute-start | bytes 196616 | tf_op jit(solution)/shard_map/ppermute | solution.py:284
